TPU v7x, 32 devices: a whole 2x2x4 slice. The times are simulated.
32 devices in a mesh: parts: 2 (over x), slab: 16 (over z, y, core).
Axes of the slice: x: 2, y: 2, z: 4, core: 2. Of those that a mesh axis runs over, the one named last changes fastest.
Arguments:
- features: bfloat16 [32768, 64], P(('parts', 'slab')), parts along dimension 0, may hold values from -6 to 6
- weight_one: bfloat16 [27, 64, 64], replicated, may hold values from -0.21875 to 0.21875
- weight_two: bfloat16 [27, 64, 64], replicated, may hold values from -0.21875 to 0.21875
- rules: int32 [32768, 27], P(('parts', 'slab')), parts along dimension 0, may hold values from -1 to 1535, as said below
- cotangent: bfloat16 [32768, 64], P(('parts', 'slab')), parts along dimension 0, may hold values from -6 to 6
Outputs:
- features_grad: bfloat16 [32768, 64], P(('parts', 'slab')), parts along dimension 0
- grad_one: float32 [54, 64, 64], P('parts'), parts along dimension 0
- grad_two: float32 [54, 64, 64], P('parts'), parts along dimension 0
There are 2 independent parts, one for each index of `parts`. A program takes and returns all parts, laid end to end along the dimension named above; an argument that names none is the same for every part. Nothing has to cross between parts.
Inputs may be any that keep to these rules, and one draw needn't show every extreme that they name: `rules`: the rows of an owner block are the cells of a box of 4 planes of 16 x 16 cells, plane by plane along the slab, then row by row; owner blocks follow one another along the slab. Offset k = 9 (dz + 1) + 3 (dy + 1) + (dx + 1) of the cell at (z, y, x) holds 256 + (z + dz) * 256 + (y + dy) * 16 + (x + dx) when the cell and its neighbour at (z + dz, y + dy, x + dx) are both occupied and the neighbour lies inside the slab window's cross section, else -1; unoccupied cells hold -1 at every offset. The occupied share differs from owner to owner, and some owner is fully occupied.
All inputs are finite; a program needn't handle non-finite values.
Results may differ from a plain program's by a relative error of at most 0.0049.
Values may be sent and summed in bfloat16 or wider, within the bound.
No kernel may reach another device: no remote copies, remote signals or barrier semaphores. Data moves between devices by JAX's collectives and lax.ppermute only.
A program may use at most 64 MiB of HBM per device.

v0:
```python
import jax
import jax.numpy as jnp
from jax import lax
from jax.sharding import PartitionSpec as P

SIDE = 16


def with_halo(block, sides, width):
    for axis, dim in sides:
        count = lax.axis_size(axis)
        forward = [(i, i + 1) for i in range(count - 1)]
        backward = [(target, source) for source, target in forward]
        low = lax.ppermute(
            lax.slice_in_dim(block, block.shape[dim] - width, None, axis=dim), axis, forward
        )
        high = lax.ppermute(lax.slice_in_dim(block, 0, width, axis=dim), axis, backward)
        block = jnp.concatenate([low, block, high], axis=dim)
    return block


def from_behind(shard, axis, by):
    devices = lax.axis_size(axis)
    pairs = [(i, i + by) for i in range(devices) if 0 <= i + by < devices]
    return lax.ppermute(shard, axis, pairs)


def collect(extended, rule):
    taken = jnp.take(extended, jnp.maximum(rule, 0), axis=0)
    taken = jnp.where((rule >= 0)[:, :, None], taken, jnp.zeros((), extended.dtype))
    return taken.reshape(rule.shape[0], -1)


def widen(values, rim):
    return with_halo(values, (("slab", 0),), rim)


def give_back(extended, rows, rim):
    middle = extended[rim : rim + rows]
    from_right = from_behind(extended[:rim], "slab", -1)
    from_left = from_behind(extended[rim + rows :], "slab", 1)
    middle = middle.at[:rim].add(from_left)
    middle = middle.at[rows - rim :].add(from_right)
    return middle


def on_device(features, weight_one, weight_two, rules, cotangent):
    rows, chans = features.shape
    koff = rules.shape[1]
    rim = SIDE * SIDE
    span = rows + 2 * rim
    block = min(1024, rows)
    count = rows // block
    w_first = weight_one.reshape(koff * chans, chans)
    w_second = weight_two.reshape(koff * chans, chans)
    rule_blocks = rules.reshape(count, block, koff)
    cot_blocks = cotangent.reshape(count, block, chans)
    ext_in = widen(features, rim)

    def forward_block(rule):
        return jnp.dot(collect(ext_in, rule), w_first, preferred_element_type=jnp.float32)

    pre = lax.map(lambda rule: forward_block(rule), rule_blocks).reshape(rows, chans)
    hidden = jax.nn.silu(pre).astype(jnp.bfloat16)
    ext_hidden = widen(hidden, rim)
    blank_weight = jnp.zeros((koff * chans, chans), jnp.float32)
    blank_span = jnp.zeros((span, chans), jnp.float32)

    def both_terms(extended, wflat):

        def step(carry, item):
            total, acc = carry
            rule, grads = item
            gathered = collect(extended, rule)
            total = total + lax.dot_general(
                gathered, grads, (((0,), (0,)), ((), ())), preferred_element_type=jnp.float32
            )
            terms = jnp.dot(grads, wflat.T, preferred_element_type=jnp.float32).reshape(-1, chans)
            target = jnp.where(rule >= 0, rule, span).reshape(-1)
            acc = acc + jax.ops.segment_sum(terms, target, num_segments=span + 1)[:span]
            return ((total, acc), None)

        return step

    (grad_two, spread_two), _ = lax.scan(
        both_terms(ext_hidden, w_second), (blank_weight, blank_span), (rule_blocks, cot_blocks)
    )
    grad_two = lax.psum(grad_two, "slab")
    hidden_grad = give_back(spread_two, rows, rim)
    sig = jax.nn.sigmoid(pre)
    pre_grad = (hidden_grad * sig * (1.0 + pre * (1.0 - sig))).astype(jnp.bfloat16)
    grad_blocks = pre_grad.reshape(count, block, chans)
    (grad_one, spread_one), _ = lax.scan(
        both_terms(ext_in, w_first), (blank_weight, blank_span), (rule_blocks, grad_blocks)
    )
    features_grad = give_back(spread_one, rows, rim).astype(jnp.bfloat16)
    grad_one = lax.psum(grad_one, "slab")
    return (
        features_grad,
        grad_one.reshape(koff, chans, chans),
        grad_two.reshape(koff, chans, chans),
    )


def solution(mesh):
    return jax.shard_map(
        on_device,
        mesh=mesh,
        in_specs=(
            P(("parts", "slab"), None),
            P(),
            P(),
            P(("parts", "slab"), None),
            P(("parts", "slab"), None),
        ),
        out_specs=(P(("parts", "slab"), None), P("parts", None, None), P("parts", None, None)),
        check_vma=False,
    )
```

profile of v0, /device:TPU:0, one launch (start us, length us, event | category | flops | bytes accessed | tf_op | source)
XLA Modules:
  0.0 810.8 jit_solution(7303114241820944090)
XLA Ops:
  7.2 0.0 copy-start
  7.2 0.0 all-reduce.3.cloned.1.call-start
  7.2 1.0 broadcast_maximum_fusion
  8.2 0.2 copy.38
  8.4 0.4 reshape.189
  8.8 5.2 fusion.11
  13.9 11.7 %reshape.183 = f32[27648,64]{1,0:T(8,128)} reshape(f32[1024,1728]{1,0:T(8,128)} %fusion.11) | data formatting | bytes 14155776 | tf_op jit(solution)/shard_map/while/body/eval_jaxpr/reshape | solution.py:78
  25.6 167.4 %scatter_custom_fusion = f32[1537,64]{1,0:T(8,128)S(1)} fusion(s32[27648]{0:T(1024)S(1)} %reshape.189, f32[27648,64]{1,0:T(8,128)} %reshape.183, f32[]{:T(128)} %constant.149.clone.1), kind=kCustom, calls=%fused_computation.9 | custom fusion | flops 1769472 | bytes 393984 | tf_op jit(solution)/shard_map/while/body/eval_jaxpr/scatter-add | solution.py:80
  193.0 0.1 copy.66
  193.1 5.1 collective-permute-start
  198.2 0.1 copy.67
  198.3 1.3 collective-permute-start.1
  199.6 0.0 copy-done.6
  199.6 0.2 copy.46
  199.8 8.3 %collective-permute-start.2 = (bf16[256,64]{1,0:T(8,128)(2,1)S(1)}, bf16[256,64]{1,0:T(8,128)(2,1)S(1)}, u32[]{:S(2)}, u32[]{:S(2)}) collective-permute-start(bf16[256,64]{1,0:T(8,128)(2,1)S(1)} %get-tuple-element.124), channel_id=1, source_target_pairs={{0,1},{1,2},{2,3},{3,4},{4,5},{5,6},{6,7},{7,8},{8,9},{9,10},{10,1... | collective-permute-start | bytes 98312 | tf_op jit(solution)/shard_map/ppermute | solution.py:14
  208.1 1.3 collective-permute-start.3
  209.4 0.2 copy.49
  209.6 0.4 reshape.201
  210.0 0.0 copy-done.5
  210.1 0.1 copy.65
  210.2 0.2 copy.64
  210.4 0.3 copy.44
  210.7 0.3 copy.45
  211.0 0.0 collective-permute-done.2
  211.0 1.5 collective-permute-done.3
  212.5 0.1 pad_maximum_fusion
  212.6 97.0 %gather_fusion = bf16[27648,64]{1,0:T(8,128)(2,1)} fusion(bf16[1536,64]{1,0:T(8,128)(2,1)S(1)} %pad_maximum_fusion, s32[27648]{0:T(1024)S(1)} %broadcast_clamp_fusion), kind=kCustom, calls=%fused_computation.clone | custom fusion | bytes 7188480 | tf_op jit(solution)/shard_map/while/body/eval_jaxpr/jit(_take)/gather | solution.py:29
  309.6 12.2 %reshape.204 = bf16[1024,27,64]{2,1,0:T(8,128)(2,1)} reshape(bf16[27648,64]{1,0:T(8,128)(2,1)} %gather_fusion) | data formatting | bytes 7077888 | tf_op jit(solution)/shard_map/while/body/eval_jaxpr/jit(_take)/gather | solution.py:29
  321.9 13.2 %select_select_fusion.1 = bf16[1024,27,64]{2,1,0:T(8,128)(2,1)} fusion(bf16[1024,27,64]{2,1,0:T(8,128)(2,1)} %reshape.204, pred[1024,27]{1,0:T(8,128)(4,1)S(1)} %copy.45, pred[1024,27]{1,0:T(8,128)(4,1)S(1)} %copy.44), kind=kLoop, calls=%fused_computation.5 | loop fusion | flops 3538944 | bytes 7133184 | tf_op jit(solution)/shard_map/while/body/eval_jaxpr/jit(_where)/select_n | solution.py:30
  335.1 10.8 %copy.50 = bf16[1024,27,64]{0,2,1:T(8,128)(2,1)} copy(bf16[1024,27,64]{2,1,0:T(8,128)(2,1)} %select_select_fusion.1) | data formatting | bytes 7077888 | tf_op jit(solution)/shard_map/while/body/eval_jaxpr/jit(_where)/select_n | solution.py:30
  345.9 0.0 collective-permute-done
  345.9 0.0 collective-permute-done.1
  345.9 0.0 copy-done
  345.9 2.9 multiply_convert_fusion
  348.8 4.8 collective-permute-start.6
  353.6 1.5 collective-permute-start.7
  355.1 3.2 fusion.13
  358.3 4.1 fusion.12
  362.4 11.6 %reshape.191 = f32[27648,64]{1,0:T(8,128)} reshape(f32[1024,1728]{1,0:T(8,128)} %fusion.12) | data formatting | bytes 14155776 | tf_op jit(solution)/shard_map/while/body/eval_jaxpr/reshape | solution.py:78
  374.0 167.4 %scatter_custom_fusion.1 = f32[1537,64]{1,0:T(8,128)S(1)} fusion(s32[27648]{0:T(1024)S(1)} %reshape.189, f32[27648,64]{1,0:T(8,128)} %reshape.191, f32[]{:T(128)} %constant.149.clone.1), kind=kCustom, calls=%fused_computation.7 | custom fusion | flops 1769472 | bytes 393984 | tf_op jit(solution)/shard_map/while/body/eval_jaxpr/scatter-add | solution.py:80
  541.4 0.0 copy-start.2
  541.4 1.4 reshape.160
  542.8 5.8 collective-permute-start.4
  548.6 1.3 collective-permute-start.5
  549.9 0.0 collective-permute-done.6
  549.9 0.0 collective-permute-done.7
  550.0 0.2 copy.56
  550.2 97.0 %gather_fusion.1 = bf16[27648,64]{1,0:T(8,128)(2,1)} fusion(bf16[1536,64]{1,0:T(8,128)(2,1)S(1)} %copy.56, s32[27648]{0:T(1024)S(1)} %broadcast_clamp_fusion), kind=kCustom, calls=%fused_computation.1.clone | custom fusion | bytes 7188480 | tf_op jit(solution)/shard_map/while/body/eval_jaxpr/jit(_take)/gather | solution.py:29
  647.2 0.0 copy-done.2
  647.2 12.2 %reshape.208 = bf16[1024,27,64]{2,1,0:T(8,128)(2,1)} reshape(bf16[27648,64]{1,0:T(8,128)(2,1)} %gather_fusion.1) | data formatting | bytes 7077888 | tf_op jit(solution)/shard_map/while/body/eval_jaxpr/jit(_take)/gather | solution.py:29
  659.5 13.2 %select_select_fusion = bf16[1024,27,64]{2,1,0:T(8,128)(2,1)} fusion(bf16[1024,27,64]{2,1,0:T(8,128)(2,1)} %reshape.208, pred[1024,27]{1,0:T(8,128)(4,1)S(1)} %copy.45, pred[1024,27]{1,0:T(8,128)(4,1)S(1)} %copy.44), kind=kLoop, calls=%fused_computation.4 | loop fusion | flops 3538944 | bytes 7133184 | tf_op jit(solution)/shard_map/while/body/eval_jaxpr/jit(_where)/select_n | solution.py:30
  672.7 0.0 slice-start
  672.7 0.0 copy-start.1
  672.7 10.9 %copy.57 = bf16[1024,27,64]{0,2,1:T(8,128)(2,1)} copy(bf16[1024,27,64]{2,1,0:T(8,128)(2,1)} %select_select_fusion) | data formatting | bytes 7077888 | tf_op jit(solution)/shard_map/while/body/eval_jaxpr/jit(_where)/select_n | solution.py:30
  683.6 0.0 copy-done.4
  683.6 3.2 fusion.14
  686.8 1.4 reshape.162
  688.3 0.0 all-reduce.3.cloned.1.call-update
  688.3 0.0 collective-permute-done.4
  688.3 0.0 collective-permute-done.5
  688.4 0.8 copy.58
  689.2 109.5 %all-reduce.3.cloned.1.call-done = (f32[27,64,64]{1,0,2:T(8,128)}, f32[27,64,64]{1,0,2:T(8,128)}) async-done(((f32[27,64,64]{1,0,2:T(8,128)}, f32[27,64,64]{1,0,2:T(8,128)}), (f32[27,64,64]{1,0,2:T(8,128)}, f32[27,64,64]{1,0,2:T(8,128)})) %all-reduce.3.cloned.1.call-update) | async-done | bytes 884752 | tf_op jit(solution)/shard_map/psum | solution.py:97
  798.7 2.6 copy.59
  801.3 2.6 copy.60
  (20 shorter events, 0.3 us)
Async XLA Ops:
  7.2 338.7 %copy-start = (bf16[27,64,64]{2,1,0:T(8,128)(2,1)S(1)}, bf16[27,64,64]{2,1,0:T(8,128)(2,1)}, u32[]{:S(2)}) copy-start(bf16[27,64,64]{2,1,0:T(8,128)(2,1)} %param.16) | copy-start | bytes 663556
  7.2 791.5 %all-reduce.3.cloned.1.call-start = ((), (), s32[]{:S(2)}) async-start(), calls=%async_computation | async-start | bytes 4194304 | tf_op jit(solution)/shard_map/psum | solution.py:97
  13.9 185.7 %copy-start.6 = (bf16[1024,64]{0,1:T(8,128)(2,1)S(1)}, bf16[1024,64]{0,1:T(8,128)(2,1)}, u32[]{:S(2)}) copy-start(bf16[1024,64]{0,1:T(8,128)(2,1)} %param.15) | copy-start | bytes 393220
  13.9 196.1 %copy-start.5 = (s32[1024,27]{0,1:T(8,128)S(1)}, s32[1024,27]{0,1:T(8,128)}, u32[]{:S(2)}) copy-start(s32[1024,27]{0,1:T(8,128)} %param.18) | copy-start | bytes 331780
  193.1 152.8 %collective-permute-start = (f32[256,64]{0,1:T(8,128)S(1)}, f32[256,64]{0,1:T(8,128)S(1)}, u32[]{:S(2)}, u32[]{:S(2)}) collective-permute-start(f32[256,64]{0,1:T(8,128)S(1)} %copy.66), channel_id=1, source_target_pairs={{0,1},{1,2},{2,3},{3,4},{4,5},{5,6},{6,7},{7,8},{8,9},{9,10},{10,1... | collective-permute-start | bytes 196616 | tf_op jit(solution)/shard_map/ppermute | solution.py:25
  198.3 147.6 %collective-permute-start.1 = (f32[256,64]{0,1:T(8,128)S(1)}, f32[256,64]{0,1:T(8,128)S(1)}, u32[]{:S(2)}, u32[]{:S(2)}) collective-permute-start(f32[256,64]{0,1:T(8,128)S(1)} %copy.67), channel_id=1, source_target_pairs={{1,0},{2,1},{3,2},{4,3},{5,4},{6,5},{7,6},{8,7},{9,8},{10,9},{11,1... | collective-permute-start | bytes 196616 | tf_op jit(solution)/shard_map/ppermute | solution.py:25
  199.8 11.2 %collective-permute-start.2 = (bf16[256,64]{1,0:T(8,128)(2,1)S(1)}, bf16[256,64]{1,0:T(8,128)(2,1)S(1)}, u32[]{:S(2)}, u32[]{:S(2)}) collective-permute-start(bf16[256,64]{1,0:T(8,128)(2,1)S(1)} %get-tuple-element.124), channel_id=1, source_target_pairs={{0,1},{1,2},{2,3},{3,4},{4,5},{5,6},{6,7},{7,8},{8,9},{9,10},{10,1... | collective-permute-start | bytes 98312 | tf_op jit(solution)/shard_map/ppermute | solution.py:14
  208.1 4.4 collective-permute-start.3
  348.8 201.1 %collective-permute-start.6 = (bf16[256,64]{0,1:T(8,128)(2,1)S(1)}, bf16[256,64]{0,1:T(8,128)(2,1)S(1)}, u32[]{:S(2)}, u32[]{:S(2)}) collective-permute-start(bf16[256,64]{0,1:T(8,128)(2,1)S(1)} %get-tuple-element.126), channel_id=1, source_target_pairs={{0,1},{1,2},{2,3},{3,4},{4,5},{5,6},{6,7},{7,8},{8,9},{9,10},{10,1... | collective-permute-start | bytes 98312 | tf_op jit(solution)/shard_map/ppermute | solution.py:14
  353.6 196.3 %collective-permute-start.7 = (bf16[256,64]{0,1:T(8,128)(2,1)S(1)}, bf16[256,64]{0,1:T(8,128)(2,1)S(1)}, u32[]{:S(2)}, u32[]{:S(2)}) collective-permute-start(bf16[256,64]{0,1:T(8,128)(2,1)S(1)} %get-tuple-element.127), channel_id=1, source_target_pairs={{1,0},{2,1},{3,2},{4,3},{5,4},{6,5},{7,6},{8,7},{9,8},{10,9},{11,1... | collective-permute-start | bytes 98312 | tf_op jit(solution)/shard_map/ppermute | solution.py:17
  541.4 105.9 %copy-start.2 = (f32[1537,64]{1,0:T(8,128)}, f32[1537,64]{1,0:T(8,128)S(1)}, u32[]{:S(2)}) copy-start(f32[1537,64]{1,0:T(8,128)S(1)} %scatter_custom_fusion.1) | copy-start | bytes 1180420
  542.8 145.5 %collective-permute-start.4 = (f32[256,64]{1,0:T(8,128)S(1)}, f32[256,64]{1,0:T(8,128)S(1)}, u32[]{:S(2)}, u32[]{:S(2)}) collective-permute-start(f32[256,64]{1,0:T(8,128)S(1)} %get-tuple-element.118), channel_id=1, source_target_pairs={{0,1},{1,2},{2,3},{3,4},{4,5},{5,6},{6,7},{7,8},{8,9},{9,10},{10,1... | collective-permute-start | bytes 196616 | tf_op jit(solution)/shard_map/ppermute | solution.py:25
  548.6 139.7 %collective-permute-start.5 = (f32[256,64]{1,0:T(8,128)S(1)}, f32[256,64]{1,0:T(8,128)S(1)}, u32[]{:S(2)}, u32[]{:S(2)}) collective-permute-start(f32[256,64]{1,0:T(8,128)S(1)} %get-tuple-element.117), channel_id=1, source_target_pairs={{1,0},{2,1},{3,2},{4,3},{5,4},{6,5},{7,6},{8,7},{9,8},{10,9},{11,1... | collective-permute-start | bytes 196616 | tf_op jit(solution)/shard_map/ppermute | solution.py:25
  672.7 11.0 %copy-start.4 = (bf16[1024,64]{0,1:T(8,128)(2,1)S(1)}, bf16[1024,64]{0,1:T(8,128)(2,1)}, u32[]{:S(2)}) copy-start(bf16[1024,64]{0,1:T(8,128)(2,1)} %param.19) | copy-start | bytes 393220
  672.7 15.6 %copy-start.3 = (f32[1537,64]{1,0:T(8,128)S(1)}, f32[1537,64]{1,0:T(8,128)}, u32[]{:S(2)}) copy-start(f32[1537,64]{1,0:T(8,128)} %copy-done.2) | copy-start | bytes 1180420
  672.7 15.6 %slice-start = ((f32[1537,64]{1,0:T(8,128)}), f32[1024,64]{1,0:T(8,128)S(1)}, s32[]{:S(2)}) async-start(f32[1537,64]{1,0:T(8,128)} %copy-done.2), calls=%async_computation.1 | async-start | bytes 1048576 | tf_op jit(solution)/shard_map/slice | solution.py:39
  672.7 131.2 %copy-start.1 = (bf16[27,64,64]{2,1,0:T(8,128)(2,1)S(1)}, bf16[27,64,64]{2,1,0:T(8,128)(2,1)}, u32[]{:S(2)}) copy-start(bf16[27,64,64]{2,1,0:T(8,128)(2,1)} %param.16) | copy-start | bytes 663556
Sparse Core Ops, SparseCore 0:
  688.4 110.2 all-reduce.2
where the time goes:
time: 813 us; the launch traced here: 811 us
  other arithmetic  362 us (45%)
  local copies, waits for them, and re-layouts  275 us (34%)
  waiting for transfers between devices  111 us (14%)
  starting transfers between devices  29.4 us (4%)
  matrix products  18.4 us (2%)
  between operations  14.4 us (2%)
    scatter-add x2, other arithmetic, step(): acc = acc + jax.ops.segment_sum(terms, target, num_segments=span + 1)[:span]  335 us
    gather x4, local copies, waits for them, and re-layouts, collect(): taken = jnp.take(extended, jnp.maximum(rule, 0), axis=0)  219 us
    psum x1, waiting for transfers between devices, on_device(): grad_one = lax.psum(grad_one, 'slab')  109 us
    select_n x2, other arithmetic, collect(): jnp.where((rule >= 0)[:, :, None], taken, jnp.zeros((), extended.dtype))  26.4 us
    reshape x2, local copies, waits for them, and re-layouts, step(): jnp.dot(grads, wflat.T, preferred_element_type=jnp.float32)  23.3 us
    select_n x2, local copies, waits for them, and re-layouts, collect(): jnp.where((rule >= 0)[:, :, None], taken, jnp.zeros((), extended.dtype))  21.7 us
  transfers between devices with their start and end apart: 9, of which 2 were waited for; matrix products, arithmetic and copies ran while one was open for 57% of the time, Pallas kernels for 0%

commit v1 on v0

v1 whole, which is shorter than its diff:
```python
import functools

import jax
import jax.numpy as jnp
from jax import lax
from jax.experimental import pallas as pl
from jax.experimental.pallas import tpu as pltpu
from jax.sharding import PartitionSpec as P

SIDE = 16
RIM = SIDE * SIDE
BF = jnp.bfloat16
F32 = jnp.float32
OFFSETS = [dy * SIDE + dx for dy in (-1, 0, 1) for dx in (-1, 0, 1)]


def edge_masks(length):
    lane = lax.broadcasted_iota(jnp.int32, (1, length), 1)
    x, y = lane % SIDE, (lane // SIDE) % SIDE
    inside = {}
    for dy in (-1, 0, 1):
        for dx in (-1, 0, 1):
            ok = (x + dx >= 0) & (x + dx < SIDE) & (y + dy >= 0) & (y + dy < SIDE)
            inside[dy * SIDE + dx] = jnp.where(ok, 1.0, 0.0).astype(BF)
    return inside


def write_shifts(dst, values):
    length = values.shape[1]
    inside = edge_masks(length)
    chans = values.shape[0]
    for j, off in enumerate(OFFSETS):
        moved = values if off == 0 else pltpu.roll(values, (-off) % length, 1) * inside[off]
        dst[j * chans : (j + 1) * chans, :] = moved


def dot(a, b, ca, cb):
    return lax.dot_general(a, b, (((ca,), (cb,)), ((), ())), preferred_element_type=F32)


def join_planes(terms, chans):
    n = terms.shape[1]
    return (
        terms[:chans, : n - 2 * RIM]
        + terms[chans : 2 * chans, RIM : n - RIM]
        + terms[2 * chans :, 2 * RIM :]
    )


def backward_weights(w_ref, dst, chans):
    for dz in range(3):
        for j in range(9):
            dst[dz * chans : (dz + 1) * chans, j * chans : (j + 1) * chans] = w_ref[26 - (dz * 9 + j)]


def forward_weights(w_ref, dst, chans):
    for dz in range(3):
        for j in range(9):
            dst[j * chans : (j + 1) * chans, dz * chans : (dz + 1) * chans] = w_ref[dz * 9 + j]


def prep_kernel(f_ref, c_ref, r_ref, low_ref, high_ref):
    n = f_ref.shape[1]
    chans = f_ref.shape[0]
    mask = jnp.where(r_ref[5:6, :] >= 0, 1.0, 0.0).astype(BF)
    for ref, start in ((low_ref, 0), (high_ref, n - 2 * RIM)):
        m = mask[:, start : start + 2 * RIM]
        ref[:chans, :] = f_ref[:, start : start + 2 * RIM] * m
        ref[chans : 2 * chans, :] = c_ref[:, start : start + 2 * RIM] * m
        ref[2 * chans :, :] = jnp.broadcast_to(m, (16, 2 * RIM))


def main_kernel(f_ref, c_ref, r_ref, left_ref, right_ref, w1_ref, w2_ref, pg_ref, grads_ref,
                s_f, s_c, wf, wb):
    chans, n = f_ref.shape
    mask = jnp.where(r_ref[5:6, :] >= 0, 1.0, 0.0).astype(BF)
    ext_m = jnp.concatenate(
        [left_ref[2 * chans : 2 * chans + 1, RIM:], mask, right_ref[2 * chans : 2 * chans + 1, :RIM]], 1
    ).astype(F32)
    ext_f = jnp.concatenate([left_ref[:chans, :], f_ref[...] * mask, right_ref[:chans, :]], 1)
    ext_c = jnp.concatenate(
        [left_ref[chans : 2 * chans, :], c_ref[...] * mask, right_ref[chans : 2 * chans, :]], 1
    )
    write_shifts(s_f, ext_f)
    write_shifts(s_c, ext_c)
    forward_weights(w1_ref, wf, chans)
    backward_weights(w2_ref, wb, chans)
    pre = join_planes(dot(wf[...], s_f[...], 0, 0), chans)
    sig = 1.0 / (1.0 + jnp.exp(-pre))
    hidden = (pre * sig * ext_m).astype(BF)[:, RIM : RIM + n]
    blank = jnp.zeros((chans, 2 * RIM), BF)
    hid = jnp.concatenate([blank, hidden, blank], 1)
    hid3 = jnp.concatenate([hid[:, (2 - d) * RIM : (2 - d) * RIM + n + 2 * RIM] for d in range(3)], 0)
    g2 = dot(hid3, s_c[:, RIM : n + 3 * RIM], 1, 1)
    hg = join_planes(dot(wb[...], s_c[...], 1, 0), chans) * ext_m
    pg = (hg * sig * (1.0 + pre * (1.0 - sig))).astype(BF)
    pg_ref[...] = pg
    own = jnp.concatenate([blank, pg[:, RIM : RIM + n], blank], 1)
    own3 = jnp.concatenate([own[:, (2 - d) * RIM : (2 - d) * RIM + n + 2 * RIM] for d in range(3)], 0)
    g1 = dot(s_f[:, RIM : n + 3 * RIM], own3, 1, 1)
    for dz in range(3):
        for j in range(9):
            k = dz * 9 + j
            r = 26 - k
            bz, bj = r // 9, r % 9
            grads_ref[k * chans : (k + 1) * chans, :chans] = g1[
                j * chans : (j + 1) * chans, dz * chans : (dz + 1) * chans
            ]
            grads_ref[k * chans : (k + 1) * chans, chans:] = g2[
                bz * chans : (bz + 1) * chans, bj * chans : (bj + 1) * chans
            ]


def last_kernel(pg_ref, r_ref, w1_ref, out_ref, s_p, wb):
    chans = w1_ref.shape[1]
    mask = jnp.where(r_ref[5:6, :] >= 0, 1.0, 0.0)
    write_shifts(s_p, pg_ref[...])
    backward_weights(w1_ref, wb, chans)
    out = join_planes(dot(wb[...], s_p[...], 1, 0), chans) * mask
    out_ref[...] = out.astype(BF)


def whole(shape):
    return pl.BlockSpec(shape, lambda i: (0,) * len(shape))


def call(kernel, args, specs, outs, scratch=(), cost=None):
    return pl.pallas_call(
        kernel,
        grid=(1,),
        in_specs=specs,
        out_specs=[whole(o.shape) for o in outs],
        out_shape=outs,
        scratch_shapes=list(scratch),
        compiler_params=pltpu.CompilerParams(vmem_limit_bytes=40 * 1024 * 1024),
        cost_estimate=cost,
    )(*args)


def all_sum(part, axis):
    count = lax.axis_size(axis)
    me = lax.axis_index(axis)

    def swap(x, bit):
        return lax.ppermute(x, axis, [(i, i ^ bit) for i in range(count)])

    halved, bit = [], 1
    cur = part
    while bit < count and len(halved) < 2:
        n = cur.shape[0] // 2
        upper = (me & bit) > 0
        low, high = cur[:n], cur[n:]
        cur = jnp.where(upper, high, low) + swap(jnp.where(upper, low, high).astype(BF), bit).astype(F32)
        halved.append(bit)
        bit *= 2
    while bit < count:
        sent = cur.astype(BF)
        cur = sent.astype(F32) + swap(sent, bit).astype(F32)
        bit *= 2
    cur = cur.astype(BF)
    for bit in reversed(halved):
        upper = (me & bit) > 0
        other = swap(cur, bit)
        cur = jnp.concatenate([jnp.where(upper, other, cur), jnp.where(upper, cur, other)], 0)
    return cur


def on_device(features, weight_one, weight_two, rules, cotangent):
    rows, chans = features.shape
    koff = rules.shape[1]
    ft, ct, rt = features.T, cotangent.T, rules.T
    count = lax.axis_size("slab")
    rule_spec = pl.BlockSpec((8, rows), lambda i: (1, 0))
    halo = jax.ShapeDtypeStruct((2 * chans + 16, 2 * RIM), BF)
    low, high = call(
        prep_kernel, (ft, ct, rt), [whole(ft.shape), whole(ct.shape), rule_spec], [halo, halo]
    )
    left = lax.ppermute(high, "slab", [(i, i + 1) for i in range(count - 1)])
    right = lax.ppermute(low, "slab", [(i + 1, i) for i in range(count - 1)])
    wide = rows + 4 * RIM
    pg, grads = call(
        main_kernel,
        (ft, ct, rt, left, right, weight_one, weight_two),
        [whole(ft.shape), whole(ct.shape), rule_spec, whole(left.shape), whole(right.shape),
         whole(weight_one.shape), whole(weight_two.shape)],
        [jax.ShapeDtypeStruct((chans, rows + 2 * RIM), BF),
         jax.ShapeDtypeStruct((koff * chans, 2 * chans), F32)],
        [pltpu.VMEM((9 * chans, wide), BF), pltpu.VMEM((9 * chans, wide), BF),
         pltpu.VMEM((9 * chans, 3 * chans), BF), pltpu.VMEM((3 * chans, 9 * chans), BF)],
    )
    (fg,) = call(
        last_kernel,
        (pg, rt, weight_one),
        [whole(pg.shape), rule_spec, whole(weight_one.shape)],
        [jax.ShapeDtypeStruct((chans, rows), BF)],
        [pltpu.VMEM((9 * chans, rows + 2 * RIM), BF), pltpu.VMEM((3 * chans, 9 * chans), BF)],
        pl.CostEstimate(flops=2 * rows * koff * chans * chans, bytes_accessed=2 * rows * chans * 4, transcendentals=0),
    )
    total = all_sum(grads, "slab").reshape(koff, chans, 2 * chans)
    return fg.T, total[:, :, :chans].astype(F32), total[:, :, chans:].astype(F32)


def solution(mesh):
    return jax.shard_map(
        on_device,
        mesh=mesh,
        in_specs=(
            P(("parts", "slab"), None),
            P(),
            P(),
            P(("parts", "slab"), None),
            P(("parts", "slab"), None),
        ),
        out_specs=(P(("parts", "slab"), None), P("parts", None, None), P("parts", None, None)),
        check_vma=False,
    )
```

time: 813 us -> 49.1 us (0.06)
  other arithmetic: 362 us -> 1.81 us
  local copies, waits for them, and re-layouts: 275 us -> 4.74 us
  waiting for transfers between devices: 111 us -> 19.3 us
  matrix products: 18.4 us -> 0 us
  between operations: 14.4 us -> 0.78 us
  starting transfers between devices: 29.4 us -> 16.2 us
    scatter-add x6 -> x0, other arithmetic: 335 us -> none  [the longest x2 335 us: step(): acc = acc + jax.ops.segment_sum(terms, target, num_segments=span + 1)[:span]]
    gather x4 -> x0, local copies, waits for them, and re-layouts: 219 us -> none  [collect(): taken = jnp.take(extended, jnp.maximum(rule, 0), axis=0)]
    psum x1 -> x0, waiting for transfers between devices: 109 us -> none  [on_device(): grad_one = lax.psum(grad_one, 'slab')]
    reshape x5 -> x0, local copies, waits for them, and re-layouts: 26.5 us -> none  [the longest x2 23.3 us: step(): jnp.dot(grads, wflat.T, preferred_element_type=jnp.float32)]
    select_n x2, other arithmetic: 26.4 us -> 0.11 us  [all_sum(): jnp.where(upper, other, cur)]
    select_n x4 -> x0, local copies, waits for them, and re-layouts: 22.1 us -> none  [the longest x2 21.7 us: collect(): jnp.where((rule >= 0)[:, :, None], taken, jnp.zeros((), extended.dtype))]
    dot_general x5 -> x0, matrix products: 18.4 us -> none  [the longest x2 9.21 us: step(): jnp.dot(grads, wflat.T, preferred_element_type=jnp.float32)]
    ppermute x8, waiting for transfers between devices: 1.53 us -> 19.3 us  [the longest x6 15.2 us: swap(): return lax.ppermute(x, axis, [(i, i ^ bit) for i in range(count)])]
  transfers between devices with their start and end apart: 9 -> 8, of which waited for: 2 -> 6; matrix products, arithmetic and copies ran while one was open for 57% -> 0% of each run, Pallas kernels for 0% -> 3%
where the time goes in v1:
time: 49.1 us; the launch traced here: 48.8 us
  waiting for transfers between devices  19.3 us (39%)
  starting transfers between devices  16.2 us (33%)
  Pallas kernels  6.03 us (12%)
  local copies, waits for them, and re-layouts  4.74 us (10%)
  other arithmetic  1.81 us (4%)
  between operations  0.78 us (2%)
    ppermute x6, waiting for transfers between devices, swap(): return lax.ppermute(x, axis, [(i, i ^ bit) for i in range(count)])  15.2 us
    ppermute x6, starting transfers between devices, swap(): return lax.ppermute(x, axis, [(i, i ^ bit) for i in range(count)])  12.4 us
    pallas_call x3, Pallas kernels, call(): pl.pallas_call(kernel, grid=(1,), in_specs=specs, out_specs=[whole(o.shap...  6.03 us
    unnamed x18, local copies, waits for them, and re-layouts  4.74 us
    ppermute x1, waiting for transfers between devices, on_device(): right = lax.ppermute(low, 'slab', [(i + 1, i) for i in range(count - 1)])  4.07 us
    ppermute x1, starting transfers between devices, on_device(): left = lax.ppermute(high, 'slab', [(i, i + 1) for i in range(count - 1)])  2.5 us
    convert_element_type x1, other arithmetic, on_device(): total[:, :, chans:].astype(F32)  1.43 us
    ppermute x1, starting transfers between devices, on_device(): right = lax.ppermute(low, 'slab', [(i + 1, i) for i in range(count - 1)])  1.29 us
  transfers between devices with their start and end apart: 8, of which 6 were waited for; matrix products, arithmetic and copies ran while one was open for 0% of the time, Pallas kernels for 3%

profile of v1, /device:TPU:0, one launch (start us, length us, event | category | flops | bytes accessed | tf_op | source)
XLA Modules:
  0.0 48.8 jit_solution(7318486574212741144)
XLA Ops:
  0.6 0.0 copy-start.2
  0.6 0.9 %copy-done.2 = s32[1024,27]{0,1:T(8,128)S(1)} copy-done((s32[1024,27]{0,1:T(8,128)S(1)}, s32[1024,27]{0,1:T(8,128)}, u32[]{:S(2)}) %copy-start.2) | copy-done | bytes 110616
  1.5 0.0 copy-start.4
  1.5 0.9 %copy-done.4 = bf16[1024,64]{0,1:T(8,128)(2,1)S(1)} copy-done((bf16[1024,64]{0,1:T(8,128)(2,1)S(1)}, bf16[1024,64]{0,1:T(8,128)(2,1)}, u32[]{:S(2)}) %copy-start.4) | copy-done | bytes 131096
  2.4 0.0 copy-start.6
  2.4 0.9 %copy-done.6 = bf16[1024,64]{0,1:T(8,128)(2,1)S(1)} copy-done((bf16[1024,64]{0,1:T(8,128)(2,1)S(1)}, bf16[1024,64]{0,1:T(8,128)(2,1)}, u32[]{:S(2)}) %copy-start.6) | copy-done | bytes 131096
  3.3 0.0 copy-start.3
  3.3 0.0 copy-start.5
  3.3 0.0 copy-start.7
  3.4 2.5 %collective-permute-start = (bf16[144,512]{1,0:T(8,128)(2,1)S(1)}, bf16[144,512]{1,0:T(8,128)(2,1)S(1)}, u32[]{:S(2)}, u32[]{:S(2)}) collective-permute-start(bf16[144,512]{1,0:T(8,128)(2,1)S(1)} %get-tuple-element.7), channel_id=1, source_target_pairs={{0,1},{1,2},{2,3},{3,4},{4,5},{5,6},{6,7},{7,8},{8,9},{9,10},{10,1... | collective-permute-start | bytes 442376 | tf_op jit(solution)/shard_map/ppermute | solution.py:178
  5.9 1.3 %collective-permute-start.1 = (bf16[144,512]{1,0:T(8,128)(2,1)S(1)}, bf16[144,512]{1,0:T(8,128)(2,1)S(1)}, u32[]{:S(2)}, u32[]{:S(2)}) collective-permute-start(bf16[144,512]{1,0:T(8,128)(2,1)S(1)} %get-tuple-element.8), channel_id=1, source_target_pairs={{1,0},{2,1},{3,2},{4,3},{5,4},{6,5},{7,6},{8,7},{9,8},{10,9},{11,1... | collective-permute-start | bytes 442376 | tf_op jit(solution)/shard_map/ppermute | solution.py:179
  7.2 0.0 collective-permute-done.left_ref
  7.2 4.1 %collective-permute-done.1.right_ref = bf16[144,512]{1,0:T(8,128)(2,1)S(1)} collective-permute-done((bf16[144,512]{1,0:T(8,128)(2,1)S(1)}, bf16[144,512]{1,0:T(8,128)(2,1)S(1)}, u32[]{:S(2)}, u32[]{:S(2)}) %collective-permute-start.1) | collective-permute-done | bytes 147488 | tf_op jit(solution)/shard_map/ppermute | solution.py:179
  11.3 0.0 copy-done.3
  11.3 0.0 copy-done.5
  11.3 0.0 copy-done.7
  11.3 0.0 copy-start
  11.3 1.0 %copy-done = bf16[27,64,64]{2,1,0:T(8,128)(2,1)S(1)} copy-done((bf16[27,64,64]{2,1,0:T(8,128)(2,1)S(1)}, bf16[27,64,64]{2,1,0:T(8,128)(2,1)}, u32[]{:S(2)}) %copy-start) | copy-done | bytes 221208
  12.3 0.0 copy-start.8
  12.3 1.0 %copy-done.8 = bf16[27,64,64]{2,1,0:T(8,128)(2,1)S(1)} copy-done((bf16[27,64,64]{2,1,0:T(8,128)(2,1)S(1)}, bf16[27,64,64]{2,1,0:T(8,128)(2,1)}, u32[]{:S(2)}) %copy-start.8) | copy-done | bytes 221208
  13.3 4.4 %shard_map.77 = (bf16[64,1536]{1,0:T(8,128)(2,1)S(1)}, f32[1728,128]{1,0:T(8,128)S(1)}) custom-call(bf16[64,1024]{1,0:T(8,128)(2,1)S(1)} %bitcast.9, bf16[64,1024]{1,0:T(8,128)(2,1)S(1)} %bitcast.11, s32[27,1024]{1,0:T(8,128)S(1)} %bitcast.6, bf16[144,512]{1,0:T(8,128)(2,1)S(1)} %collective-permute-done.left_ref, ...), custom_call_target="tpu_custom_call" | custom-call | tf_op jit(solution)/shard_map/pallas_call | solution.py:128
  17.8 3.8 %collective-permute-start.2 = (bf16[864,128]{1,0:T(8,128)(2,1)S(1)}, bf16[864,128]{1,0:T(8,128)(2,1)S(1)}, u32[]{:S(2)}, u32[]{:S(2)}) collective-permute-start(bf16[864,128]{1,0:T(8,128)(2,1)S(1)} %select_convert_fusion), channel_id=1, source_target_pairs={{0,1},{1,0},{2,3},{3,2},{4,5},{5,4},{6,7},{7,6},{8,9},{9,8},{10,11... | collective-permute-start | bytes 663560 | tf_op jit(solution)/shard_map/ppermute | solution.py:145
  21.6 1.1 %collective-permute-done.2 = bf16[864,128]{1,0:T(8,128)(2,1)S(1)} collective-permute-done((bf16[864,128]{1,0:T(8,128)(2,1)S(1)}, bf16[864,128]{1,0:T(8,128)(2,1)S(1)}, u32[]{:S(2)}, u32[]{:S(2)}) %collective-permute-start.2) | collective-permute-done | bytes 221216 | tf_op jit(solution)/shard_map/ppermute | solution.py:145
  22.7 0.1 convert_add_fusion
  22.8 2.5 %collective-permute-start.3 = (bf16[432,128]{1,0:T(8,128)(2,1)S(1)}, bf16[432,128]{1,0:T(8,128)(2,1)S(1)}, u32[]{:S(2)}, u32[]{:S(2)}) collective-permute-start(bf16[432,128]{1,0:T(8,128)(2,1)S(1)} %select_convert_fusion.1), channel_id=1, source_target_pairs={{0,2},{1,3},{2,0},{3,1},{4,6},{5,7},{6,4},{7,5},{8,10},{9,11},{10,... | collective-permute-start | bytes 331784 | tf_op jit(solution)/shard_map/ppermute | solution.py:145
  25.3 3.6 %collective-permute-done.3 = bf16[432,128]{1,0:T(8,128)(2,1)S(1)} collective-permute-done((bf16[432,128]{1,0:T(8,128)(2,1)S(1)}, bf16[432,128]{1,0:T(8,128)(2,1)S(1)}, u32[]{:S(2)}, u32[]{:S(2)}) %collective-permute-start.3) | collective-permute-done | bytes 110624 | tf_op jit(solution)/shard_map/ppermute | solution.py:145
  28.9 1.6 %collective-permute-start.4 = (bf16[432,128]{1,0:T(8,128)(2,1)S(1)}, bf16[432,128]{1,0:T(8,128)(2,1)S(1)}, u32[]{:S(2)}, u32[]{:S(2)}) collective-permute-start(bf16[432,128]{1,0:T(8,128)(2,1)S(1)} %add_convert_fusion.2), channel_id=1, source_target_pairs={{0,4},{1,5},{2,6},{3,7},{4,0},{5,1},{6,2},{7,3},{8,12},{9,13},{10,... | collective-permute-start | bytes 331784 | tf_op jit(solution)/shard_map/ppermute | solution.py:145
  30.5 3.2 %collective-permute-done.4 = bf16[432,128]{1,0:T(8,128)(2,1)S(1)} collective-permute-done((bf16[432,128]{1,0:T(8,128)(2,1)S(1)}, bf16[432,128]{1,0:T(8,128)(2,1)S(1)}, u32[]{:S(2)}, u32[]{:S(2)}) %collective-permute-start.4) | collective-permute-done | bytes 110624 | tf_op jit(solution)/shard_map/ppermute | solution.py:145
  33.7 2.7 %collective-permute-start.5 = (bf16[432,128]{1,0:T(8,128)(2,1)S(1)}, bf16[432,128]{1,0:T(8,128)(2,1)S(1)}, u32[]{:S(2)}, u32[]{:S(2)}) collective-permute-start(bf16[432,128]{1,0:T(8,128)(2,1)S(1)} %add_convert_fusion.1), channel_id=1, source_target_pairs={{0,8},{1,9},{2,10},{3,11},{4,12},{5,13},{6,14},{7,15},{8,0},{9,1},... | collective-permute-start | bytes 331784 | tf_op jit(solution)/shard_map/ppermute | solution.py:145
  36.4 4.3 %collective-permute-done.5 = bf16[432,128]{1,0:T(8,128)(2,1)S(1)} collective-permute-done((bf16[432,128]{1,0:T(8,128)(2,1)S(1)}, bf16[432,128]{1,0:T(8,128)(2,1)S(1)}, u32[]{:S(2)}, u32[]{:S(2)}) %collective-permute-start.5) | collective-permute-done | bytes 110624 | tf_op jit(solution)/shard_map/ppermute | solution.py:145
  40.7 0.0 copy-start.1
  40.7 1.8 %collective-permute-start.6 = (bf16[432,128]{1,0:T(8,128)(2,1)S(1)}, bf16[432,128]{1,0:T(8,128)(2,1)S(1)}, u32[]{:S(2)}, u32[]{:S(2)}) collective-permute-start(bf16[432,128]{1,0:T(8,128)(2,1)S(1)} %add_convert_fusion), channel_id=1, source_target_pairs={{0,2},{1,3},{2,0},{3,1},{4,6},{5,7},{6,4},{7,5},{8,10},{9,11},{10,... | collective-permute-start | bytes 331784 | tf_op jit(solution)/shard_map/ppermute | solution.py:145
  42.5 3.1 %collective-permute-done.6 = bf16[432,128]{1,0:T(8,128)(2,1)S(1)} collective-permute-done((bf16[432,128]{1,0:T(8,128)(2,1)S(1)}, bf16[432,128]{1,0:T(8,128)(2,1)S(1)}, u32[]{:S(2)}, u32[]{:S(2)}) %collective-permute-start.6) | collective-permute-done | bytes 110624 | tf_op jit(solution)/shard_map/ppermute | solution.py:145
  45.6 0.1 collective-permute-start.7
  45.7 0.0 copy-done.1
  45.7 1.6 %shard_map.78 = bf16[64,1024]{1,0:T(8,128)(2,1)} custom-call(bf16[64,1536]{1,0:T(8,128)(2,1)S(1)} %get-tuple-element.9.pg_ref, s32[27,1024]{1,0:T(8,128)S(1)} %bitcast.7, bf16[27,64,64]{2,1,0:T(8,128)(2,1)S(1)} %copy-done.1), custom_call_target="tpu_custom_call" | custom-call | flops 226492416 | bytes 524288 | tf_op jit(solution)/shard_map/pallas_call | solution.py:128
  47.2 0.0 collective-permute-done.7
  47.2 0.1 broadcast_select_fusion.1
  47.4 1.4 %slice_convert_fusion = (f32[27,64,64]{2,1,0:T(8,128)}, f32[27,64,64]{2,1,0:T(8,128)}) fusion(bf16[27,64,128]{2,1,0:T(8,128)(2,1)S(1)} %bitcast.12), kind=kLoop, calls=%fused_computation | loop fusion | flops 221184 | bytes 1327104 | tf_op jit(solution)/shard_map/convert_element_type | solution.py:200
  (9 shorter events, 0.3 us)
Async XLA Ops:
  0.6 0.9 %copy-start.2 = (s32[1024,27]{0,1:T(8,128)S(1)}, s32[1024,27]{0,1:T(8,128)}, u32[]{:S(2)}) copy-start(s32[1024,27]{0,1:T(8,128)} %param.8) | copy-start | bytes 331780
  1.5 0.9 %copy-start.4 = (bf16[1024,64]{0,1:T(8,128)(2,1)S(1)}, bf16[1024,64]{0,1:T(8,128)(2,1)}, u32[]{:S(2)}) copy-start(bf16[1024,64]{0,1:T(8,128)(2,1)} %param.5) | copy-start | bytes 393220
  2.4 0.9 %copy-start.6 = (bf16[1024,64]{0,1:T(8,128)(2,1)S(1)}, bf16[1024,64]{0,1:T(8,128)(2,1)}, u32[]{:S(2)}) copy-start(bf16[1024,64]{0,1:T(8,128)(2,1)} %param.9) | copy-start | bytes 393220
  3.3 7.9 %copy-start.3 = (s32[1024,27]{0,1:T(8,128)S(1)}, s32[1024,27]{0,1:T(8,128)}, u32[]{:S(2)}) copy-start(s32[1024,27]{0,1:T(8,128)} %param.8) | copy-start | bytes 331780
  3.3 7.9 %copy-start.5 = (bf16[1024,64]{0,1:T(8,128)(2,1)S(1)}, bf16[1024,64]{0,1:T(8,128)(2,1)}, u32[]{:S(2)}) copy-start(bf16[1024,64]{0,1:T(8,128)(2,1)} %param.5) | copy-start | bytes 393220
  3.3 7.9 %copy-start.7 = (bf16[1024,64]{0,1:T(8,128)(2,1)S(1)}, bf16[1024,64]{0,1:T(8,128)(2,1)}, u32[]{:S(2)}) copy-start(bf16[1024,64]{0,1:T(8,128)(2,1)} %param.9) | copy-start | bytes 393220
  3.4 3.8 %collective-permute-start = (bf16[144,512]{1,0:T(8,128)(2,1)S(1)}, bf16[144,512]{1,0:T(8,128)(2,1)S(1)}, u32[]{:S(2)}, u32[]{:S(2)}) collective-permute-start(bf16[144,512]{1,0:T(8,128)(2,1)S(1)} %get-tuple-element.7), channel_id=1, source_target_pairs={{0,1},{1,2},{2,3},{3,4},{4,5},{5,6},{6,7},{7,8},{8,9},{9,10},{10,1... | collective-permute-start | bytes 442376 | tf_op jit(solution)/shard_map/ppermute | solution.py:178
  5.9 5.4 %collective-permute-start.1 = (bf16[144,512]{1,0:T(8,128)(2,1)S(1)}, bf16[144,512]{1,0:T(8,128)(2,1)S(1)}, u32[]{:S(2)}, u32[]{:S(2)}) collective-permute-start(bf16[144,512]{1,0:T(8,128)(2,1)S(1)} %get-tuple-element.8), channel_id=1, source_target_pairs={{1,0},{2,1},{3,2},{4,3},{5,4},{6,5},{7,6},{8,7},{9,8},{10,9},{11,1... | collective-permute-start | bytes 442376 | tf_op jit(solution)/shard_map/ppermute | solution.py:179
  11.3 1.0 %copy-start = (bf16[27,64,64]{2,1,0:T(8,128)(2,1)S(1)}, bf16[27,64,64]{2,1,0:T(8,128)(2,1)}, u32[]{:S(2)}) copy-start(bf16[27,64,64]{2,1,0:T(8,128)(2,1)} %w1_ref.3) | copy-start | bytes 663556
  12.3 1.0 %copy-start.8 = (bf16[27,64,64]{2,1,0:T(8,128)(2,1)S(1)}, bf16[27,64,64]{2,1,0:T(8,128)(2,1)}, u32[]{:S(2)}) copy-start(bf16[27,64,64]{2,1,0:T(8,128)(2,1)} %w2_ref.1) | copy-start | bytes 663556
  17.8 4.9 %collective-permute-start.2 = (bf16[864,128]{1,0:T(8,128)(2,1)S(1)}, bf16[864,128]{1,0:T(8,128)(2,1)S(1)}, u32[]{:S(2)}, u32[]{:S(2)}) collective-permute-start(bf16[864,128]{1,0:T(8,128)(2,1)S(1)} %select_convert_fusion), channel_id=1, source_target_pairs={{0,1},{1,0},{2,3},{3,2},{4,5},{5,4},{6,7},{7,6},{8,9},{9,8},{10,11... | collective-permute-start | bytes 663560 | tf_op jit(solution)/shard_map/ppermute | solution.py:145
  22.8 6.1 %collective-permute-start.3 = (bf16[432,128]{1,0:T(8,128)(2,1)S(1)}, bf16[432,128]{1,0:T(8,128)(2,1)S(1)}, u32[]{:S(2)}, u32[]{:S(2)}) collective-permute-start(bf16[432,128]{1,0:T(8,128)(2,1)S(1)} %select_convert_fusion.1), channel_id=1, source_target_pairs={{0,2},{1,3},{2,0},{3,1},{4,6},{5,7},{6,4},{7,5},{8,10},{9,11},{10,... | collective-permute-start | bytes 331784 | tf_op jit(solution)/shard_map/ppermute | solution.py:145
  28.9 4.8 %collective-permute-start.4 = (bf16[432,128]{1,0:T(8,128)(2,1)S(1)}, bf16[432,128]{1,0:T(8,128)(2,1)S(1)}, u32[]{:S(2)}, u32[]{:S(2)}) collective-permute-start(bf16[432,128]{1,0:T(8,128)(2,1)S(1)} %add_convert_fusion.2), channel_id=1, source_target_pairs={{0,4},{1,5},{2,6},{3,7},{4,0},{5,1},{6,2},{7,3},{8,12},{9,13},{10,... | collective-permute-start | bytes 331784 | tf_op jit(solution)/shard_map/ppermute | solution.py:145
  33.7 6.9 %collective-permute-start.5 = (bf16[432,128]{1,0:T(8,128)(2,1)S(1)}, bf16[432,128]{1,0:T(8,128)(2,1)S(1)}, u32[]{:S(2)}, u32[]{:S(2)}) collective-permute-start(bf16[432,128]{1,0:T(8,128)(2,1)S(1)} %add_convert_fusion.1), channel_id=1, source_target_pairs={{0,8},{1,9},{2,10},{3,11},{4,12},{5,13},{6,14},{7,15},{8,0},{9,1},... | collective-permute-start | bytes 331784 | tf_op jit(solution)/shard_map/ppermute | solution.py:145
  40.7 5.0 %copy-start.1 = (bf16[27,64,64]{2,1,0:T(8,128)(2,1)S(1)}, bf16[27,64,64]{2,1,0:T(8,128)(2,1)}, u32[]{:S(2)}) copy-start(bf16[27,64,64]{2,1,0:T(8,128)(2,1)} %w1_ref.3) | copy-start | bytes 663556
  40.7 4.8 %collective-permute-start.6 = (bf16[432,128]{1,0:T(8,128)(2,1)S(1)}, bf16[432,128]{1,0:T(8,128)(2,1)S(1)}, u32[]{:S(2)}, u32[]{:S(2)}) collective-permute-start(bf16[432,128]{1,0:T(8,128)(2,1)S(1)} %add_convert_fusion), channel_id=1, source_target_pairs={{0,2},{1,3},{2,0},{3,1},{4,6},{5,7},{6,4},{7,5},{8,10},{9,11},{10,... | collective-permute-start | bytes 331784 | tf_op jit(solution)/shard_map/ppermute | solution.py:145
  45.6 1.7 %collective-permute-start.7 = (bf16[864,128]{1,0:T(8,128)(2,1)S(1)}, bf16[864,128]{1,0:T(8,128)(2,1)S(1)}, u32[]{:S(2)}, u32[]{:S(2)}) collective-permute-start(bf16[864,128]{1,0:T(8,128)(2,1)S(1)} %pad_maximum_fusion.1), channel_id=1, source_target_pairs={{0,1},{1,0},{2,3},{3,2},{4,5},{5,4},{6,7},{7,6},{8,9},{9,8},{10,11... | collective-permute-start | bytes 663560 | tf_op jit(solution)/shard_map/ppermute | solution.py:145

commit v2 on v1

v2 whole, which is shorter than its diff:
```python
import functools

import jax
import jax.numpy as jnp
from jax import lax
from jax.experimental import pallas as pl
from jax.experimental.pallas import tpu as pltpu
from jax.sharding import PartitionSpec as P

SIDE = 16
RIM = SIDE * SIDE
BF = jnp.bfloat16
F32 = jnp.float32
OFFSETS = [dy * SIDE + dx for dy in (-1, 0, 1) for dx in (-1, 0, 1)]


def edge_masks(length):
    lane = lax.broadcasted_iota(jnp.int32, (1, length), 1)
    x, y = lane % SIDE, (lane // SIDE) % SIDE
    inside = {}
    for dy in (-1, 0, 1):
        for dx in (-1, 0, 1):
            ok = (x + dx >= 0) & (x + dx < SIDE) & (y + dy >= 0) & (y + dy < SIDE)
            inside[dy * SIDE + dx] = jnp.where(ok, 1.0, 0.0).astype(BF)
    return inside


def write_shifts(dst, values):
    length = values.shape[1]
    inside = edge_masks(length)
    chans = values.shape[0]
    for j, off in enumerate(OFFSETS):
        moved = values if off == 0 else pltpu.roll(values, (-off) % length, 1) * inside[off]
        dst[j * chans : (j + 1) * chans, :] = moved


def dot(a, b, ca, cb):
    return lax.dot_general(a, b, (((ca,), (cb,)), ((), ())), preferred_element_type=F32)


def join_planes(terms, chans):
    n = terms.shape[1]
    return (
        terms[:chans, : n - 2 * RIM]
        + terms[chans : 2 * chans, RIM : n - RIM]
        + terms[2 * chans :, 2 * RIM :]
    )


def backward_weights(w_ref, dst, chans):
    for dz in range(3):
        for j in range(9):
            dst[dz * chans : (dz + 1) * chans, j * chans : (j + 1) * chans] = w_ref[26 - (dz * 9 + j)]


def forward_weights(w_ref, dst, chans):
    for dz in range(3):
        for j in range(9):
            dst[j * chans : (j + 1) * chans, dz * chans : (dz + 1) * chans] = w_ref[dz * 9 + j]


def prep_kernel(odd_ref, f_hbm, c_hbm, r_hbm, near_ref, far_ref, f_ref, c_ref, m_ref, rules, sems):
    chans, n = f_ref.shape
    copies = [
        pltpu.make_async_copy(r_hbm.at[8:16, :], rules, sems.at[0]),
        pltpu.make_async_copy(f_hbm, f_ref, sems.at[1]),
        pltpu.make_async_copy(c_hbm, c_ref, sems.at[2]),
    ]
    for copy in copies:
        copy.start()
    copies[0].wait()
    mask = jnp.where(rules[5:6, :] >= 0, 1.0, 0.0).astype(BF)
    m_ref[...] = jnp.broadcast_to(mask, m_ref.shape)
    for copy in copies[1:]:
        copy.wait()
    f_ref[...] = f_ref[...] * mask
    c_ref[...] = c_ref[...] * mask
    odd = odd_ref[0] % 2

    def fill(ref, lanes):
        ref[:chans, :] = f_ref[:, lanes]
        ref[chans:, :] = c_ref[:, lanes]

    first, last = slice(0, RIM), slice(n - RIM, n)

    @pl.when(odd == 0)
    def _():
        fill(near_ref, last)
        fill(far_ref, first)

    @pl.when(odd != 0)
    def _():
        fill(near_ref, first)
        fill(far_ref, last)


def own_kernel(f_ref, c_ref, w1_hbm, w2_hbm, s_f, s_c, wf, wb, pre_ref, hg_ref, w1, w2, sems):
    chans, n = f_ref.shape
    copies = [
        pltpu.make_async_copy(w1_hbm, w1, sems.at[0]),
        pltpu.make_async_copy(w2_hbm, w2, sems.at[1]),
    ]
    for copy in copies:
        copy.start()
    write_shifts(s_f, f_ref[...])
    write_shifts(s_c, c_ref[...])
    copies[0].wait()
    forward_weights(w1, wf, chans)
    spread_terms(pre_ref, dot(wf[...], s_f[...], 0, 0), chans)
    copies[1].wait()
    backward_weights(w2, wb, chans)
    spread_terms(hg_ref, dot(wb[...], s_c[...], 1, 0), chans)


def spread_terms(out_ref, terms, chans):
    n = terms.shape[1]
    low, mid, high = terms[:chans], terms[chans : 2 * chans], terms[2 * chans :]
    out_ref[:, :RIM] = high[:, :RIM]
    out_ref[:, RIM : 2 * RIM] = mid[:, :RIM] + high[:, RIM : 2 * RIM]
    out_ref[:, 2 * RIM : n] = mid[:, RIM : n - RIM] + high[:, 2 * RIM :] + low[:, : n - 2 * RIM]
    out_ref[:, n : n + RIM] = mid[:, n - RIM :] + low[:, n - 2 * RIM : n - RIM]
    out_ref[:, n + RIM :] = low[:, n - RIM :]


def sides(odd_ref, near, far):
    far = jnp.where(odd_ref[0] >= 2, far, jnp.zeros_like(far))
    even = odd_ref[0] % 2 == 0
    return jnp.where(even, far, near), jnp.where(even, near, far)


def slope(hg, pre, mask):
    sig = 1.0 / (1.0 + jnp.exp(-pre))
    return pre * sig * mask, (hg * mask * sig * (1.0 + pre * (1.0 - sig))).astype(BF)


def grads_kernel(odd_ref, far_ref, near_ref, m_ref, s_f, s_c, wf, wb, pre_ref, hg_ref,
                 keep_ref, send_ref, far_pg_ref, pg_ref, r_f, r_c, grads_ref):
    chans = pg_ref.shape[0]
    n = s_f.shape[1]
    both = jnp.concatenate(sides(odd_ref, near_ref[...], far_ref[...]), 1)
    write_shifts(r_f, both[:chans, :])
    write_shifts(r_c, both[chans:, :])
    rim = slice(0, RIM)
    end = slice(RIM, 2 * RIM)
    low_pre = dot(wf[:, :chans], r_f[:, rim], 0, 0)
    high_pre = dot(wf[:, 2 * chans :], r_f[:, end], 0, 0)
    low_hg = dot(wb[:chans, :], r_c[:, rim], 1, 0)
    high_hg = dot(wb[2 * chans :, :], r_c[:, end], 1, 0)
    mask = m_ref[0:1, :].astype(F32)

    def own(ref, low, high):
        mid = ref[:, RIM : RIM + n]
        return jnp.concatenate([mid[:, :RIM] + low, mid[:, RIM : n - RIM], mid[:, n - RIM :] + high], 1)

    hidden, pg = slope(own(hg_ref, low_hg, high_hg), own(pre_ref, low_pre, high_pre), mask)
    pg_ref[...] = pg
    hidden = hidden.astype(BF)
    blank = jnp.zeros((chans, RIM), BF)

    def fan(v):
        return jnp.concatenate(
            [jnp.concatenate([v[:, RIM:], blank], 1), v, jnp.concatenate([blank, v[:, : n - RIM]], 1)], 0
        )

    g1 = dot(s_f[...], fan(pg), 1, 1)
    g1_low = dot(r_f[:, rim], pg[:, :RIM], 1, 1)
    g1_high = dot(r_f[:, end], pg[:, n - RIM :], 1, 1)
    g2 = dot(fan(hidden), s_c[...], 1, 1)
    g2_low = dot(hidden[:, :RIM], r_c[:, rim], 1, 1)
    g2_high = dot(hidden[:, n - RIM :], r_c[:, end], 1, 1)
    for dz in range(3):
        for j in range(9):
            k = dz * 9 + j
            bz, bj = 2 - dz, 8 - j
            rows = slice(j * chans, (j + 1) * chans)
            one = g1[rows, dz * chans : (dz + 1) * chans]
            cols = slice(bj * chans, (bj + 1) * chans)
            two = g2[bz * chans : (bz + 1) * chans, cols]
            if dz == 0:
                one = one + g1_low[rows, :]
                two = two + g2_high[:, cols]
            if dz == 2:
                one = one + g1_high[rows, :]
                two = two + g2_low[:, cols]
            grads_ref[k * chans : (k + 1) * chans, :chans] = one
            grads_ref[k * chans : (k + 1) * chans, chans:] = two


    half = keep_ref.shape[0]

    def part_with(mine, yours, near_plane, far_plane):
        keep_ref[...] = grads_ref[mine, :]
        send_ref[:half, :] = grads_ref[yours, :].astype(BF)
        for i in range(RIM // (2 * chans)):
            lanes = slice(near_plane + 2 * i * chans, near_plane + 2 * (i + 1) * chans)
            send_ref[half + i * chans : half + (i + 1) * chans, :] = pg[:, lanes]
        far_pg_ref[...] = pg[:, far_plane : far_plane + RIM]

    lower, upper = slice(0, half), slice(half, 2 * half)

    @pl.when(odd_ref[0] % 2 == 0)
    def _():
        part_with(lower, upper, n - RIM, 0)

    @pl.when(odd_ref[0] % 2 != 0)
    def _():
        part_with(upper, lower, 0, n - RIM)


def last_kernel(odd_ref, near_ref, far_ref, m_ref, pg_ref, w1_hbm, _, out_ref, zero_ref, s_p, wb, w1, sems):
    chans, n = pg_ref.shape
    weights = pltpu.make_async_copy(w1_hbm, w1, sems.at[0])
    weights.start()
    zero_ref[...] = jnp.zeros_like(zero_ref)
    first = near_ref.shape[0] - RIM // 2
    near = jnp.concatenate(
        [near_ref[first + i * chans : first + (i + 1) * chans, :] for i in range(RIM // (2 * chans))], 1
    )
    left, right = sides(odd_ref, near, far_ref[...])
    write_shifts(s_p, jnp.concatenate([left, pg_ref[...], right], 1))
    weights.wait()
    backward_weights(w1, wb, chans)
    out = join_planes(dot(wb[...], s_p[...], 1, 0), chans) * m_ref[0:1, :].astype(F32)
    out_ref[...] = out.astype(BF)


def whole(shape):
    return pl.BlockSpec(shape, lambda i: (0,) * len(shape))


HBM = pl.BlockSpec(memory_space=pltpu.HBM)
SCALAR = pl.BlockSpec(memory_space=pltpu.SMEM)


def call(kernel, args, outs, scratch=(), specs=None, flops=0):
    specs = specs or {}
    args = [
        pltpu.with_memory_space_constraint(x, pltpu.HBM) if specs.get(i) is HBM else x
        for i, x in enumerate(args)
    ]
    return pl.pallas_call(
        kernel,
        grid=(1,),
        in_specs=[specs.get(i, whole(x.shape)) for i, x in enumerate(args)],
        out_specs=[whole(o.shape) for o in outs],
        out_shape=outs,
        scratch_shapes=list(scratch),
        compiler_params=pltpu.CompilerParams(vmem_limit_bytes=40 * 1024 * 1024),
        cost_estimate=pl.CostEstimate(flops=flops, bytes_accessed=0, transcendentals=0) if flops else None,
    )(*args)


def all_sum(keep, send, axis, beside):
    count = lax.axis_size(axis)
    me = lax.axis_index(axis)

    def swap(x, bit):
        return lax.ppermute(x, axis, [(i, i ^ bit) for i in range(count)])

    came = swap(send, 1)
    cur = keep + came[: keep.shape[0]].astype(F32)
    halved, bit = [1], 2
    while bit < count and len(halved) < 2:
        n = cur.shape[0] // 2
        upper = (me & bit) > 0
        low, high = cur[:n], cur[n:]
        cur = jnp.where(upper, high, low) + swap(jnp.where(upper, low, high).astype(BF), bit).astype(F32)
        halved.append(bit)
        bit *= 2
    zero = None
    while bit < count:
        sent = cur.astype(BF)
        other = swap(sent, bit)
        bit *= 2
        if bit >= count:
            zero = beside(came, sent)
        cur = sent.astype(F32) + other.astype(F32)
    if zero is None:
        zero = beside(came, cur.astype(BF))
    cur = (cur + zero).astype(BF)
    for bit in reversed(halved):
        upper = (me & bit) > 0
        other = swap(cur, bit)
        cur = jnp.concatenate([jnp.where(upper, other, cur), jnp.where(upper, cur, other)], 0)
    return cur


def far_partners(parts, count):
    pairs = []
    for part in range(parts):
        base = part * count
        for i in range(1, count - 1, 2):
            pairs += [(base + i, base + i + 1), (base + i + 1, base + i)]
        other = part ^ 1
        if other < parts:
            pairs += [(base, other * count), (base + count - 1, other * count + count - 1)]
    return pairs


def on_device(features, weight_one, weight_two, rules, cotangent):
    rows, chans = features.shape
    koff = rules.shape[1]
    ft, ct, rt = features.T, cotangent.T, rules.T
    count = lax.axis_size("slab")
    me = lax.axis_index("slab")
    inner = (me > 0) & (me < count - 1)
    odd = (me % 2 + 2 * inner.astype(me.dtype)).astype(jnp.int32).reshape(1)

    def array(*shape, kind=BF):
        return jax.ShapeDtypeStruct(shape, kind)

    def dma(n):
        return pltpu.SemaphoreType.DMA((n,))

    halo = (2 * chans, RIM)
    taps = 9 * chans
    weights = pltpu.VMEM(weight_one.shape, BF)
    near, far, f, c, m = call(
        prep_kernel,
        (odd, ft, ct, rt),
        [array(*halo), array(*halo), array(chans, rows), array(chans, rows), array(16, rows)],
        [pltpu.VMEM((8, rows), jnp.int32), dma(3)],
        {0: SCALAR, 1: HBM, 2: HBM, 3: HBM},
    )
    far_pairs = far_partners(lax.axis_size("parts"), count)
    near_pairs = [(i, i ^ 1) for i in range(count)]
    near_in = lax.ppermute(near, "slab", near_pairs)
    far_in = lax.ppermute(far, ("parts", "slab"), far_pairs)
    s_f, s_c, wf, wb, pre, hg = call(
        own_kernel,
        (f, c, weight_one, weight_two),
        [array(taps, rows), array(taps, rows), array(taps, 3 * chans), array(3 * chans, taps),
         array(chans, rows + 2 * RIM, kind=F32), array(chans, rows + 2 * RIM, kind=F32)],
        [weights, weights, dma(2)],
        {2: HBM, 3: HBM},
        flops=2 * 2 * rows * koff * chans * chans,
    )
    half = koff * chans // 2
    keep, send, far_pg, pg = call(
        grads_kernel,
        (odd, far_in, near_in, m, s_f, s_c, wf, wb, pre, hg),
        [array(half, 2 * chans, kind=F32), array(half + RIM // 2, 2 * chans), array(chans, RIM), array(chans, rows)],
        [pltpu.VMEM((taps, 2 * RIM), BF), pltpu.VMEM((taps, 2 * RIM), BF), pltpu.VMEM((2 * half, 2 * chans), F32)],
        {0: SCALAR},
        flops=2 * 2 * rows * koff * chans * chans,
    )
    far_pg = lax.ppermute(far_pg, ("parts", "slab"), far_pairs)
    done = []

    def beside(came, sent):
        fg, zero = call(
            last_kernel,
            (odd, came, far_pg, m, pg, weight_one, sent),
            [array(chans, rows), array(8, 2 * chans, kind=F32)],
            [pltpu.VMEM((taps, rows + 2 * RIM), BF), pltpu.VMEM((3 * chans, taps), BF), weights, dma(1)],
            {0: SCALAR, 5: HBM, 6: pl.BlockSpec(memory_space=pl.ANY)},
            flops=2 * 2 * rows * koff * chans * chans,
        )
        done.append(fg)
        return zero[:1]

    total = all_sum(keep, send, "slab", beside).reshape(koff, chans, 2 * chans)
    return done[0].T, total[:, :, :chans].astype(F32), total[:, :, chans:].astype(F32)


def solution(mesh):
    return jax.shard_map(
        on_device,
        mesh=mesh,
        in_specs=(
            P(("parts", "slab"), None),
            P(),
            P(),
            P(("parts", "slab"), None),
            P(("parts", "slab"), None),
        ),
        out_specs=(P(("parts", "slab"), None), P("parts", None, None), P("parts", None, None)),
        check_vma=False,
    )
```

time: 49.1 us -> 37.2 us (0.76)
  starting transfers between devices: 16.2 us -> 10.7 us
  local copies, waits for them, and re-layouts: 4.74 us -> 0.01 us
  waiting for transfers between devices: 19.3 us -> 15.2 us
  Pallas kernels: 6.03 us -> 8.63 us
    ppermute x6, starting transfers between devices: 12.4 us -> 6.03 us  [swap(): return lax.ppermute(x, axis, [(i, i ^ bit) for i in range(count)])]
    unnamed x18 -> x0, local copies, waits for them, and re-layouts: 4.74 us -> none
    ppermute x2 -> x3, waiting for transfers between devices: 4.08 us -> 0.01 us  [the longest x1 0.01 us: on_device(): near_in = lax.ppermute(near, 'slab', near_pairs)]
    pallas_call x3 -> x4, Pallas kernels: 6.03 us -> 8.63 us  [call(): pl.pallas_call(kernel, grid=(1,), in_specs=[specs.get(i, whole(x.shape))...]
    ppermute x2 -> x3, starting transfers between devices: 3.79 us -> 4.64 us  [the longest x1 3 us: on_device(): far_in = lax.ppermute(far, ('parts', 'slab'), far_pairs)]
  transfers between devices with their start and end apart: 8 -> 9, of which waited for: 6 -> 6; matrix products, arithmetic and copies ran while one was open for 0% -> 0% of each run, Pallas kernels for 3% -> 16%
where the time goes in v2:
time: 37.2 us; the launch traced here: 37 us
  waiting for transfers between devices  15.2 us (41%)
  starting transfers between devices  10.7 us (29%)
  Pallas kernels  8.63 us (23%)
  other arithmetic  1.76 us (5%)
  between operations  0.77 us (2%)
    ppermute x6, waiting for transfers between devices, swap(): return lax.ppermute(x, axis, [(i, i ^ bit) for i in range(count)])  15.1 us
    pallas_call x4, Pallas kernels, call(): pl.pallas_call(kernel, grid=(1,), in_specs=[specs.get(i, whole(x.shape))...  8.63 us
    ppermute x6, starting transfers between devices, swap(): return lax.ppermute(x, axis, [(i, i ^ bit) for i in range(count)])  6.03 us
    ppermute x1, starting transfers between devices, on_device(): far_in = lax.ppermute(far, ('parts', 'slab'), far_pairs)  3 us
    ppermute x1, starting transfers between devices, on_device(): far_pg = lax.ppermute(far_pg, ('parts', 'slab'), far_pairs)  1.49 us
    convert_element_type x1, other arithmetic, on_device(): total[:, :, chans:].astype(F32)  1.43 us
  transfers between devices with their start and end apart: 9, of which 6 were waited for; matrix products, arithmetic and copies ran while one was open for 0% of the time, Pallas kernels for 16%

profile of v2, /device:TPU:0, one launch (start us, length us, event | category | flops | bytes accessed | tf_op | source)
XLA Modules:
  0.0 37.0 jit_solution(8718931729506143301)
XLA Ops:
  0.7 1.0 %shard_map.76 = (bf16[128,256]{1,0:T(8,128)(2,1)S(1)}, bf16[128,256]{1,0:T(8,128)(2,1)S(1)}, bf16[64,1024]{1,0:T(8,128)(2,1)S(1)}, bf16[64,1024]{1,0:T(8,128)(2,1)S(1)}, bf16[16,1024]{1,0:T(8,128)(2,1)S(1)}) custom-call(s32[1]{0:T(128)} %bitcast.odd_ref, bf16[64,1024]{1,0:T(8,128)(2,1)} %bitcast.9, bf16[64,1024]{1,0:T(8,128)(2,1)} %bitcast.10, ...), custom_call_target="tpu_custom_call" | custom-call | tf_op jit(solution)/shard_map/pallas_call | solution.py:241
  1.7 3.0 %collective-permute-start = (bf16[128,256]{1,0:T(8,128)(2,1)S(1)}, bf16[128,256]{1,0:T(8,128)(2,1)S(1)}, u32[]{:S(2)}, u32[]{:S(2)}) collective-permute-start(bf16[128,256]{1,0:T(8,128)(2,1)S(1)} %get-tuple-element.20), channel_id=1, source_target_pairs={{1,2},{2,1},{3,4},{4,3},{5,6},{6,5},{7,8},{8,7},{9,10},{10,9},{11,... | collective-permute-start | bytes 196616 | tf_op jit(solution)/shard_map/ppermute | solution.py:328
  4.7 0.1 collective-permute-start.1
  4.8 3.4 %shard_map.77 = (bf16[576,1024]{1,0:T(8,128)(2,1)S(1)}, bf16[576,1024]{1,0:T(8,128)(2,1)S(1)}, bf16[576,192]{1,0:T(8,128)(2,1)S(1)}, bf16[192,576]{1,0:T(8,128)(...) custom-call(bf16[64,1024]{1,0:T(8,128)(2,1)S(1)} %get-tuple-element.23.f_ref, ...), custom_call_target="tpu_custom_call" | custom-call | flops 452984832 | tf_op jit(solution)/shard_map/pallas_call | solution.py:241
  8.2 0.0 collective-permute-done.far_ref
  8.3 0.0 collective-permute-done.1.near_ref
  8.3 1.8 %shard_map.78 = (f32[864,128]{1,0:T(8,128)S(1)}, bf16[992,128]{1,0:T(8,128)(2,1)S(1)}, bf16[64,256]{1,0:T(8,128)(2,1)S(1)}, bf16[64,1024]{1,0:T(8,128)(2,1)S(1)}) custom-call(s32[1]{0:T(128)} %bitcast.odd_ref, bf16[128,256]{1,0:T(8,128)(2,1)S(1)} %collective-permute-done.far_ref, bf16[128,256]{1,0:T(8,128)(2,1)S(1)} %collective-permute-done.1.near_ref, ...), custom_call_target="tpu_custom_call" | custom-call | flops 452984832 | tf_op jit(solution)/shard_map/pallas_call | solution.py:241
  10.1 0.5 %collective-permute-start.2 = (bf16[992,128]{1,0:T(8,128)(2,1)S(1)}, bf16[992,128]{1,0:T(8,128)(2,1)S(1)}, u32[]{:S(2)}, u32[]{:S(2)}) collective-permute-start(bf16[992,128]{1,0:T(8,128)(2,1)S(1)} %get-tuple-element.31), channel_id=1, source_target_pairs={{0,1},{1,0},{2,3},{3,2},{4,5},{5,4},{6,7},{7,6},{8,9},{9,8},{10,11... | collective-permute-start | bytes 761864 | tf_op jit(solution)/shard_map/ppermute | solution.py:258
  10.6 1.2 %collective-permute-done.2.near_ref = bf16[992,128]{1,0:T(8,128)(2,1)S(1)} collective-permute-done((bf16[992,128]{1,0:T(8,128)(2,1)S(1)}, bf16[992,128]{1,0:T(8,128)(2,1)S(1)}, u32[]{:S(2)}, u32[]{:S(2)}) %collective-permute-start.2) | collective-permute-done | bytes 253984 | tf_op jit(solution)/shard_map/ppermute | solution.py:258
  11.8 1.6 %collective-permute-start.4 = (bf16[432,128]{1,0:T(8,128)(2,1)S(1)}, bf16[432,128]{1,0:T(8,128)(2,1)S(1)}, u32[]{:S(2)}, u32[]{:S(2)}) collective-permute-start(bf16[432,128]{1,0:T(8,128)(2,1)S(1)} %select_convert_fusion), channel_id=1, source_target_pairs={{0,2},{1,3},{2,0},{3,1},{4,6},{5,7},{6,4},{7,5},{8,10},{9,11},{10,... | collective-permute-start | bytes 331784 | tf_op jit(solution)/shard_map/ppermute | solution.py:258
  13.4 3.8 %collective-permute-done.4 = bf16[432,128]{1,0:T(8,128)(2,1)S(1)} collective-permute-done((bf16[432,128]{1,0:T(8,128)(2,1)S(1)}, bf16[432,128]{1,0:T(8,128)(2,1)S(1)}, u32[]{:S(2)}, u32[]{:S(2)}) %collective-permute-start.4) | collective-permute-done | bytes 110624 | tf_op jit(solution)/shard_map/ppermute | solution.py:258
  17.2 1.4 %collective-permute-start.5 = (bf16[432,128]{1,0:T(8,128)(2,1)S(1)}, bf16[432,128]{1,0:T(8,128)(2,1)S(1)}, u32[]{:S(2)}, u32[]{:S(2)}) collective-permute-start(bf16[432,128]{1,0:T(8,128)(2,1)S(1)} %add_convert_fusion.2), channel_id=1, source_target_pairs={{0,4},{1,5},{2,6},{3,7},{4,0},{5,1},{6,2},{7,3},{8,12},{9,13},{10,... | collective-permute-start | bytes 331784 | tf_op jit(solution)/shard_map/ppermute | solution.py:258
  18.6 1.5 %collective-permute-start.3 = (bf16[64,256]{1,0:T(8,128)(2,1)S(1)}, bf16[64,256]{1,0:T(8,128)(2,1)S(1)}, u32[]{:S(2)}, u32[]{:S(2)}) collective-permute-start(bf16[64,256]{1,0:T(8,128)(2,1)S(1)} %get-tuple-element.32), channel_id=1, source_target_pairs={{1,2},{2,1},{3,4},{4,3},{5,6},{6,5},{7,8},{8,7},{9,10},{10,9},{11,... | collective-permute-start | bytes 98312 | tf_op jit(solution)/shard_map/ppermute | solution.py:347
  20.1 1.9 %collective-permute-done.5 = bf16[432,128]{1,0:T(8,128)(2,1)S(1)} collective-permute-done((bf16[432,128]{1,0:T(8,128)(2,1)S(1)}, bf16[432,128]{1,0:T(8,128)(2,1)S(1)}, u32[]{:S(2)}, u32[]{:S(2)}) %collective-permute-start.5) | collective-permute-done | bytes 110624 | tf_op jit(solution)/shard_map/ppermute | solution.py:258
  22.1 2.4 %collective-permute-start.6 = (bf16[432,128]{1,0:T(8,128)(2,1)S(1)}, bf16[432,128]{1,0:T(8,128)(2,1)S(1)}, u32[]{:S(2)}, u32[]{:S(2)}) collective-permute-start(bf16[432,128]{1,0:T(8,128)(2,1)S(1)} %add_convert_fusion.1._), channel_id=1, source_target_pairs={{0,8},{1,9},{2,10},{3,11},{4,12},{5,13},{6,14},{7,15},{8,0},{9,1},... | collective-permute-start | bytes 331784 | tf_op jit(solution)/shard_map/ppermute | solution.py:258
  24.5 0.0 collective-permute-done.3.far_ref
  24.5 2.4 %shard_map.79 = (bf16[64,1024]{1,0:T(8,128)(2,1)}, f32[8,128]{1,0:T(8,128)S(1)}) custom-call(s32[1]{0:T(128)} %bitcast.odd_ref, bf16[992,128]{1,0:T(8,128)(2,1)S(1)} %collective-permute-done.2.near_ref, bf16[64,256]{1,0:T(8,128)(2,1)S(1)} %collective-permute-done.3.far_ref, bf16[16,1024]{1,0:T(8,128)(2,1)S(1)} %get-tuple-element.22.m_ref, ...), custom_call_target="tpu_custom_call" | custom-call | flops 452984832 | tf_op jit(solution)/shard_map/pallas_call | solution.py:241
  26.9 2.1 %collective-permute-done.6 = bf16[432,128]{1,0:T(8,128)(2,1)S(1)} collective-permute-done((bf16[432,128]{1,0:T(8,128)(2,1)S(1)}, bf16[432,128]{1,0:T(8,128)(2,1)S(1)}, u32[]{:S(2)}, u32[]{:S(2)}) %collective-permute-start.6) | collective-permute-done | bytes 110624 | tf_op jit(solution)/shard_map/ppermute | solution.py:258
  29.0 0.1 collective-permute-start.7
  29.2 4.7 %collective-permute-done.7 = bf16[432,128]{1,0:T(8,128)(2,1)S(1)} collective-permute-done((bf16[432,128]{1,0:T(8,128)(2,1)S(1)}, bf16[432,128]{1,0:T(8,128)(2,1)S(1)}, u32[]{:S(2)}, u32[]{:S(2)}) %collective-permute-start.7) | collective-permute-done | bytes 110624 | tf_op jit(solution)/shard_map/ppermute | solution.py:258
  33.9 0.1 collective-permute-start.8
  34.0 1.5 %collective-permute-done.8 = bf16[864,128]{1,0:T(8,128)(2,1)S(1)} collective-permute-done((bf16[864,128]{1,0:T(8,128)(2,1)S(1)}, bf16[864,128]{1,0:T(8,128)(2,1)S(1)}, u32[]{:S(2)}, u32[]{:S(2)}) %collective-permute-start.8) | collective-permute-done | bytes 221216 | tf_op jit(solution)/shard_map/ppermute | solution.py:258
  35.4 0.1 broadcast_select_fusion.1
  35.6 1.4 %slice_convert_fusion = (f32[27,64,64]{2,1,0:T(8,128)}, f32[27,64,64]{2,1,0:T(8,128)}) fusion(bf16[27,64,128]{2,1,0:T(8,128)(2,1)S(1)} %bitcast.8), kind=kLoop, calls=%fused_computation | loop fusion | flops 221184 | bytes 1327104 | tf_op jit(solution)/shard_map/convert_element_type | solution.py:363
  (9 shorter events, 0.2 us)
Async XLA Ops:
  1.7 6.5 %collective-permute-start = (bf16[128,256]{1,0:T(8,128)(2,1)S(1)}, bf16[128,256]{1,0:T(8,128)(2,1)S(1)}, u32[]{:S(2)}, u32[]{:S(2)}) collective-permute-start(bf16[128,256]{1,0:T(8,128)(2,1)S(1)} %get-tuple-element.20), channel_id=1, source_target_pairs={{1,2},{2,1},{3,4},{4,3},{5,6},{6,5},{7,8},{8,7},{9,10},{10,9},{11,... | collective-permute-start | bytes 196616 | tf_op jit(solution)/shard_map/ppermute | solution.py:328
  4.7 3.6 %collective-permute-start.1 = (bf16[128,256]{1,0:T(8,128)(2,1)S(1)}, bf16[128,256]{1,0:T(8,128)(2,1)S(1)}, u32[]{:S(2)}, u32[]{:S(2)}) collective-permute-start(bf16[128,256]{1,0:T(8,128)(2,1)S(1)} %get-tuple-element.21), channel_id=1, source_target_pairs={{0,1},{1,0},{2,3},{3,2},{4,5},{5,4},{6,7},{7,6},{8,9},{9,8},{10,11... | collective-permute-start | bytes 196616 | tf_op jit(solution)/shard_map/ppermute | solution.py:327
  10.1 1.6 %collective-permute-start.2 = (bf16[992,128]{1,0:T(8,128)(2,1)S(1)}, bf16[992,128]{1,0:T(8,128)(2,1)S(1)}, u32[]{:S(2)}, u32[]{:S(2)}) collective-permute-start(bf16[992,128]{1,0:T(8,128)(2,1)S(1)} %get-tuple-element.31), channel_id=1, source_target_pairs={{0,1},{1,0},{2,3},{3,2},{4,5},{5,4},{6,7},{7,6},{8,9},{9,8},{10,11... | collective-permute-start | bytes 761864 | tf_op jit(solution)/shard_map/ppermute | solution.py:258
  11.8 5.4 %collective-permute-start.4 = (bf16[432,128]{1,0:T(8,128)(2,1)S(1)}, bf16[432,128]{1,0:T(8,128)(2,1)S(1)}, u32[]{:S(2)}, u32[]{:S(2)}) collective-permute-start(bf16[432,128]{1,0:T(8,128)(2,1)S(1)} %select_convert_fusion), channel_id=1, source_target_pairs={{0,2},{1,3},{2,0},{3,1},{4,6},{5,7},{6,4},{7,5},{8,10},{9,11},{10,... | collective-permute-start | bytes 331784 | tf_op jit(solution)/shard_map/ppermute | solution.py:258
  17.2 4.8 %collective-permute-start.5 = (bf16[432,128]{1,0:T(8,128)(2,1)S(1)}, bf16[432,128]{1,0:T(8,128)(2,1)S(1)}, u32[]{:S(2)}, u32[]{:S(2)}) collective-permute-start(bf16[432,128]{1,0:T(8,128)(2,1)S(1)} %add_convert_fusion.2), channel_id=1, source_target_pairs={{0,4},{1,5},{2,6},{3,7},{4,0},{5,1},{6,2},{7,3},{8,12},{9,13},{10,... | collective-permute-start | bytes 331784 | tf_op jit(solution)/shard_map/ppermute | solution.py:258
  18.6 5.9 %collective-permute-start.3 = (bf16[64,256]{1,0:T(8,128)(2,1)S(1)}, bf16[64,256]{1,0:T(8,128)(2,1)S(1)}, u32[]{:S(2)}, u32[]{:S(2)}) collective-permute-start(bf16[64,256]{1,0:T(8,128)(2,1)S(1)} %get-tuple-element.32), channel_id=1, source_target_pairs={{1,2},{2,1},{3,4},{4,3},{5,6},{6,5},{7,8},{8,7},{9,10},{10,9},{11,... | collective-permute-start | bytes 98312 | tf_op jit(solution)/shard_map/ppermute | solution.py:347
  22.1 6.9 %collective-permute-start.6 = (bf16[432,128]{1,0:T(8,128)(2,1)S(1)}, bf16[432,128]{1,0:T(8,128)(2,1)S(1)}, u32[]{:S(2)}, u32[]{:S(2)}) collective-permute-start(bf16[432,128]{1,0:T(8,128)(2,1)S(1)} %add_convert_fusion.1._), channel_id=1, source_target_pairs={{0,8},{1,9},{2,10},{3,11},{4,12},{5,13},{6,14},{7,15},{8,0},{9,1},... | collective-permute-start | bytes 331784 | tf_op jit(solution)/shard_map/ppermute | solution.py:258
  29.0 4.8 %collective-permute-start.7 = (bf16[432,128]{1,0:T(8,128)(2,1)S(1)}, bf16[432,128]{1,0:T(8,128)(2,1)S(1)}, u32[]{:S(2)}, u32[]{:S(2)}) collective-permute-start(bf16[432,128]{1,0:T(8,128)(2,1)S(1)} %add_convert_fusion), channel_id=1, source_target_pairs={{0,2},{1,3},{2,0},{3,1},{4,6},{5,7},{6,4},{7,5},{8,10},{9,11},{10,... | collective-permute-start | bytes 331784 | tf_op jit(solution)/shard_map/ppermute | solution.py:258
  33.9 1.5 %collective-permute-start.8 = (bf16[864,128]{1,0:T(8,128)(2,1)S(1)}, bf16[864,128]{1,0:T(8,128)(2,1)S(1)}, u32[]{:S(2)}, u32[]{:S(2)}) collective-permute-start(bf16[864,128]{1,0:T(8,128)(2,1)S(1)} %pad_maximum_fusion.1), channel_id=1, source_target_pairs={{0,1},{1,0},{2,3},{3,2},{4,5},{5,4},{6,7},{7,6},{8,9},{9,8},{10,11... | collective-permute-start | bytes 663560 | tf_op jit(solution)/shard_map/ppermute | solution.py:258

commit v3 on v2

--- a/solution.py
+++ b/solution.py
@@ -94,7 +94,7 @@
         fill(far_ref, last)
 
 
-def own_kernel(f_ref, c_ref, w1_hbm, w2_hbm, s_f, s_c, wf, wb, pre_ref, hg_ref, w1, w2, sems):
+def own_kernel(f_ref, c_ref, w1_hbm, w2_hbm, s_f, s_c, wf, wb, pre_ref, hg_ref, w1, w2, turned, sems):
     chans, n = f_ref.shape
     copies = [
         pltpu.make_async_copy(w1_hbm, w1, sems.at[0]),
@@ -102,12 +102,13 @@
     ]
     for copy in copies:
         copy.start()
+    for copy in copies:
+        copy.wait()
     write_shifts(s_f, f_ref[...])
     write_shifts(s_c, c_ref[...])
-    copies[0].wait()
-    forward_weights(w1, wf, chans)
-    spread_terms(pre_ref, dot(wf[...], s_f[...], 0, 0), chans)
-    copies[1].wait()
+    forward_weights(w1, turned, chans)
+    wf[...] = turned[...].T
+    spread_terms(pre_ref, dot(wf[...], s_f[...], 1, 0), chans)
     backward_weights(w2, wb, chans)
     spread_terms(hg_ref, dot(wb[...], s_c[...], 1, 0), chans)
 
@@ -134,7 +135,7 @@
 
 
 def grads_kernel(odd_ref, far_ref, near_ref, m_ref, s_f, s_c, wf, wb, pre_ref, hg_ref,
-                 keep_ref, send_ref, far_pg_ref, pg_ref, r_f, r_c, grads_ref):
+                 keep_ref, send_ref, far_pg_ref, pg_ref, r_f, r_c, one_ref, two_ref):
     chans = pg_ref.shape[0]
     n = s_f.shape[1]
     both = jnp.concatenate(sides(odd_ref, near_ref[...], far_ref[...]), 1)
@@ -142,8 +143,8 @@
     write_shifts(r_c, both[chans:, :])
     rim = slice(0, RIM)
     end = slice(RIM, 2 * RIM)
-    low_pre = dot(wf[:, :chans], r_f[:, rim], 0, 0)
-    high_pre = dot(wf[:, 2 * chans :], r_f[:, end], 0, 0)
+    low_pre = dot(wf[:chans, :], r_f[:, rim], 1, 0)
+    high_pre = dot(wf[2 * chans :, :], r_f[:, end], 1, 0)
     low_hg = dot(wb[:chans, :], r_c[:, rim], 1, 0)
     high_hg = dot(wb[2 * chans :, :], r_c[:, end], 1, 0)
     mask = m_ref[0:1, :].astype(F32)
@@ -162,49 +163,109 @@
             [jnp.concatenate([v[:, RIM:], blank], 1), v, jnp.concatenate([blank, v[:, : n - RIM]], 1)], 0
         )
 
-    g1 = dot(s_f[...], fan(pg), 1, 1)
-    g1_low = dot(r_f[:, rim], pg[:, :RIM], 1, 1)
-    g1_high = dot(r_f[:, end], pg[:, n - RIM :], 1, 1)
-    g2 = dot(fan(hidden), s_c[...], 1, 1)
-    g2_low = dot(hidden[:, :RIM], r_c[:, rim], 1, 1)
-    g2_high = dot(hidden[:, n - RIM :], r_c[:, end], 1, 1)
-    for dz in range(3):
-        for j in range(9):
-            k = dz * 9 + j
-            bz, bj = 2 - dz, 8 - j
-            rows = slice(j * chans, (j + 1) * chans)
-            one = g1[rows, dz * chans : (dz + 1) * chans]
-            cols = slice(bj * chans, (bj + 1) * chans)
-            two = g2[bz * chans : (bz + 1) * chans, cols]
-            if dz == 0:
-                one = one + g1_low[rows, :]
-                two = two + g2_high[:, cols]
-            if dz == 2:
-                one = one + g1_high[rows, :]
-                two = two + g2_low[:, cols]
-            grads_ref[k * chans : (k + 1) * chans, :chans] = one
-            grads_ref[k * chans : (k + 1) * chans, chans:] = two
-
-
+    def rim_fan(v, low, high):
+        parts = [jnp.concatenate([v[:, :RIM], blank], 1), jnp.concatenate([blank, v[:, n - RIM :]], 1)]
+        none = jnp.zeros((chans, 2 * RIM), BF)
+        return jnp.concatenate([parts[low], none, parts[high]], 0)
+
+    one_ref[...] = dot(s_f[...], fan(pg), 1, 1) + dot(r_f[...], rim_fan(pg, 0, 1), 1, 1)
+    two_ref[...] = dot(fan(hidden), s_c[...], 1, 1) + dot(rim_fan(hidden, 0, 1), r_c[...], 1, 1)
     half = keep_ref.shape[0]
 
-    def part_with(mine, yours, near_plane, far_plane):
-        keep_ref[...] = grads_ref[mine, :]
-        send_ref[:half, :] = grads_ref[yours, :].astype(BF)
+    def part_with(pack_mine, pack_yours, near_plane, far_plane):
+        pack_mine(keep_ref)
+        pack_yours(send_ref)
         for i in range(RIM // (2 * chans)):
             lanes = slice(near_plane + 2 * i * chans, near_plane + 2 * (i + 1) * chans)
             send_ref[half + i * chans : half + (i + 1) * chans, :] = pg[:, lanes]
         far_pg_ref[...] = pg[:, far_plane : far_plane + RIM]
 
-    lower, upper = slice(0, half), slice(half, 2 * half)
-
     @pl.when(odd_ref[0] % 2 == 0)
     def _():
-        part_with(lower, upper, n - RIM, 0)
+        part_with(lambda ref: pack_one(ref, one_ref), lambda ref: pack_two(ref, two_ref), n - RIM, 0)
 
     @pl.when(odd_ref[0] % 2 != 0)
     def _():
-        part_with(upper, lower, 0, n - RIM)
+        part_with(lambda ref: pack_two(ref, two_ref), lambda ref: pack_one(ref, one_ref), 0, n - RIM)
+
+
+def pack_one(ref, one_ref):
+    taps, chans = one_ref.shape[0], one_ref.shape[1] // 3
+    fold = taps // 2
+    ref[:taps, :] = one_ref[:, : 2 * chans].astype(ref.dtype)
+    last = one_ref[:, 2 * chans :].astype(ref.dtype)
+    ref[taps : taps + fold, :chans] = last[:fold]
+    ref[taps : taps + fold, chans:] = last[fold:]
+
+
+def pack_two(ref, two_ref):
+    deep, chans = two_ref.shape[0], two_ref.shape[0] // 3
+    fold = deep // 2
+    for t in range(4):
+        ref[t * deep : (t + 1) * deep, :] = two_ref[:, 2 * t * chans : 2 * (t + 1) * chans].astype(ref.dtype)
+    last = two_ref[:, 8 * chans :].astype(ref.dtype)
+    ref[4 * deep : 4 * deep + fold, :chans] = last[:fold]
+    ref[4 * deep : 4 * deep + fold, chans:] = last[fold:]
+
+
+def unpack_one(src, dst, dz):
+    chans = dst.shape[1]
+    taps = 9 * chans
+    fold = taps // 2
+    for j in range(9):
+        first, k = j * chans, dz * 9 + j
+        if dz < 2:
+            dst[k] = src[first : first + chans, dz * chans : (dz + 1) * chans].astype(F32)
+            continue
+        for begin in range(first, first + chans, chans // 2):
+            row, lane = taps + begin % fold, begin // fold * chans
+            at = begin - first
+            dst[k, at : at + chans // 2, :] = src[row : row + chans // 2, lane : lane + chans].astype(F32)
+
+
+def unpack_two(src, dst, dz):
+    chans = dst.shape[1]
+    deep = 3 * chans
+    fold = deep // 2
+    first = (2 - dz) * chans
+    for j in range(9):
+        mirror, k = 8 - j, dz * 9 + j
+        if mirror < 8:
+            row, lane = mirror // 2 * deep + first, mirror % 2 * chans
+            dst[k] = src[row : row + chans, lane : lane + chans].astype(F32)
+            continue
+        for begin in range(first, first + chans, chans // 2):
+            row, lane = 4 * deep + begin % fold, begin // fold * chans
+            at = begin - first
+            dst[k, at : at + chans // 2, :] = src[row : row + chans // 2, lane : lane + chans].astype(F32)
+
+
+def write_half(src, one_hbm, two_hbm, wide, sems, is_one):
+    def write(unpack, out):
+        copies = []
+        for dz in range(3):
+            unpack(src, wide, dz)
+            third = pl.ds(dz * 9, 9)
+            copies.append(pltpu.make_async_copy(wide.at[third], out.at[third], sems.at[dz]))
+            copies[-1].start()
+        for copy in copies:
+            copy.wait()
+
+    @pl.when(is_one)
+    def _():
+        write(unpack_one, one_hbm)
+
+    @pl.when(jnp.logical_not(is_one))
+    def _():
+        write(unpack_two, two_hbm)
+
+
+def mine_kernel(odd_ref, src, one_hbm, two_hbm, wide, sems):
+    write_half(src, one_hbm, two_hbm, wide, sems, odd_ref[0] % 2 == 0)
+
+
+def yours_kernel(odd_ref, src, _one, _two, one_hbm, two_hbm, wide, sems):
+    write_half(src, one_hbm, two_hbm, wide, sems, odd_ref[0] % 2 != 0)
 
 
 def last_kernel(odd_ref, near_ref, far_ref, m_ref, pg_ref, w1_hbm, _, out_ref, zero_ref, s_p, wb, w1, sems):
@@ -229,10 +290,11 @@
 
 
 HBM = pl.BlockSpec(memory_space=pltpu.HBM)
+ANY = pl.BlockSpec(memory_space=pl.ANY)
 SCALAR = pl.BlockSpec(memory_space=pltpu.SMEM)
 
 
-def call(kernel, args, outs, scratch=(), specs=None, flops=0):
+def call(kernel, args, outs, scratch=(), specs=None, flops=0, out_specs=None, aliases=None):
     specs = specs or {}
     args = [
         pltpu.with_memory_space_constraint(x, pltpu.HBM) if specs.get(i) is HBM else x
@@ -242,7 +304,8 @@
         kernel,
         grid=(1,),
         in_specs=[specs.get(i, whole(x.shape)) for i, x in enumerate(args)],
-        out_specs=[whole(o.shape) for o in outs],
+        out_specs=out_specs or [whole(o.shape) for o in outs],
+        input_output_aliases=aliases or {},
         out_shape=outs,
         scratch_shapes=list(scratch),
         compiler_params=pltpu.CompilerParams(vmem_limit_bytes=40 * 1024 * 1024),
@@ -253,36 +316,33 @@
 def all_sum(keep, send, axis, beside):
     count = lax.axis_size(axis)
     me = lax.axis_index(axis)
-
-    def swap(x, bit):
-        return lax.ppermute(x, axis, [(i, i ^ bit) for i in range(count)])
-
-    came = swap(send, 1)
+    is_odd = (me & 1) > 0
+    bits = [1 << i for i in range(1, count.bit_length() - 1)]
+    even_bits, odd_bits = bits, bits[1:] + bits[:1]
+
+    def swap(x, step):
+        bit = (even_bits[step], odd_bits[step])
+        return lax.ppermute(x, axis, [(i, i ^ bit[i & 1]) for i in range(count)])
+
+    def neighbour(x):
+        return lax.ppermute(x, axis, [(i, i ^ 1) for i in range(count)])
+
+    came = neighbour(send)
     cur = keep + came[: keep.shape[0]].astype(F32)
-    halved, bit = [1], 2
-    while bit < count and len(halved) < 2:
-        n = cur.shape[0] // 2
-        upper = (me & bit) > 0
-        low, high = cur[:n], cur[n:]
-        cur = jnp.where(upper, high, low) + swap(jnp.where(upper, low, high).astype(BF), bit).astype(F32)
-        halved.append(bit)
-        bit *= 2
-    zero = None
-    while bit < count:
+    upper = (me & jnp.where(is_odd, odd_bits[0], even_bits[0])) > 0
+    n = cur.shape[0] // 2
+    low, high = cur[:n], cur[n:]
+    cur = jnp.where(upper, high, low) + swap(jnp.where(upper, low, high).astype(BF), 0).astype(F32)
+    for step in range(1, len(bits)):
         sent = cur.astype(BF)
-        other = swap(sent, bit)
-        bit *= 2
-        if bit >= count:
+        other = swap(sent, step)
+        if step == len(bits) - 1:
             zero = beside(came, sent)
         cur = sent.astype(F32) + other.astype(F32)
-    if zero is None:
-        zero = beside(came, cur.astype(BF))
     cur = (cur + zero).astype(BF)
-    for bit in reversed(halved):
-        upper = (me & bit) > 0
-        other = swap(cur, bit)
-        cur = jnp.concatenate([jnp.where(upper, other, cur), jnp.where(upper, cur, other)], 0)
-    return cur
+    other = swap(cur, 0)
+    cur = jnp.concatenate([jnp.where(upper, other, cur), jnp.where(upper, cur, other)], 0)
+    return cur, neighbour(cur)
 
 
 def far_partners(parts, count):
@@ -329,9 +389,9 @@
     s_f, s_c, wf, wb, pre, hg = call(
         own_kernel,
         (f, c, weight_one, weight_two),
-        [array(taps, rows), array(taps, rows), array(taps, 3 * chans), array(3 * chans, taps),
+        [array(taps, rows), array(taps, rows), array(3 * chans, taps), array(3 * chans, taps),
          array(chans, rows + 2 * RIM, kind=F32), array(chans, rows + 2 * RIM, kind=F32)],
-        [weights, weights, dma(2)],
+        [weights, weights, pltpu.VMEM((taps, 3 * chans), BF), dma(2)],
         {2: HBM, 3: HBM},
         flops=2 * 2 * rows * koff * chans * chans,
     )
@@ -340,7 +400,7 @@
         grads_kernel,
         (odd, far_in, near_in, m, s_f, s_c, wf, wb, pre, hg),
         [array(half, 2 * chans, kind=F32), array(half + RIM // 2, 2 * chans), array(chans, RIM), array(chans, rows)],
-        [pltpu.VMEM((taps, 2 * RIM), BF), pltpu.VMEM((taps, 2 * RIM), BF), pltpu.VMEM((2 * half, 2 * chans), F32)],
+        [pltpu.VMEM((taps, 2 * RIM), BF), pltpu.VMEM((taps, 2 * RIM), BF), pltpu.VMEM((taps, 3 * chans), F32), pltpu.VMEM((3 * chans, taps), F32)],
         {0: SCALAR},
         flops=2 * 2 * rows * koff * chans * chans,
     )
@@ -353,14 +413,24 @@
             (odd, came, far_pg, m, pg, weight_one, sent),
             [array(chans, rows), array(8, 2 * chans, kind=F32)],
             [pltpu.VMEM((taps, rows + 2 * RIM), BF), pltpu.VMEM((3 * chans, taps), BF), weights, dma(1)],
-            {0: SCALAR, 5: HBM, 6: pl.BlockSpec(memory_space=pl.ANY)},
+            {0: SCALAR, 5: HBM, 6: ANY},
             flops=2 * 2 * rows * koff * chans * chans,
         )
         done.append(fg)
         return zero[:1]
 
-    total = all_sum(keep, send, "slab", beside).reshape(koff, chans, 2 * chans)
-    return done[0].T, total[:, :, :chans].astype(F32), total[:, :, chans:].astype(F32)
+    mine, yours = all_sum(keep, send, "slab", beside)
+    grads = [array(koff, chans, chans, kind=F32)] * 2
+    scratch = [pltpu.VMEM((koff, chans, chans), F32), dma(3)]
+    grads_out = call(
+        mine_kernel, (odd, mine), grads, scratch, {0: SCALAR}, flops=2 * rows * koff * chans * chans,
+        out_specs=[ANY, ANY],
+    )
+    grad_one, grad_two = call(
+        yours_kernel, (odd, yours, *grads_out), grads, scratch, {0: SCALAR, 2: ANY, 3: ANY},
+        out_specs=[ANY, ANY], aliases={2: 0, 3: 1},
+    )
+    return done[0].T, grad_one, grad_two
 
 
 def solution(mesh):

time: 37.2 us -> 34.7 us (0.933)
  waiting for transfers between devices: 15.2 us -> 11.3 us
  starting transfers between devices: 10.7 us -> 12.4 us
  other arithmetic: 1.76 us -> 0.21 us
  Pallas kernels: 8.63 us -> 9.8 us
    ppermute x6, waiting for transfers between devices: 15.1 us -> 11.2 us  [the longest x4 9.61 us: swap(): return lax.ppermute(x, axis, [(i, i ^ bit[i & 1]) for i in range(count)])]
    ppermute x6, starting transfers between devices: 6.03 us -> 7.79 us  [the longest x4 7.29 us: swap(): return lax.ppermute(x, axis, [(i, i ^ bit[i & 1]) for i in range(count)])]
    convert_element_type x1 -> x0, other arithmetic: 1.43 us -> none  [on_device(): total[:, :, chans:].astype(F32)]
    pallas_call x4 -> x6, Pallas kernels: 8.63 us -> 9.8 us  [call(): pl.pallas_call(kernel, grid=(1,), in_specs=[specs.get(i, whole(x.shape))...]
  transfers between devices with their start and end apart: 9 -> 9, of which waited for: 6 -> 6; matrix products, arithmetic and copies ran while one was open for 0% -> 0% of each run, Pallas kernels for 16% -> 17%
where the time goes in v3:
time: 34.7 us; the launch traced here: 34.5 us
  starting transfers between devices  12.4 us (36%)
  waiting for transfers between devices  11.3 us (33%)
  Pallas kernels  9.8 us (28%)
  between operations  0.76 us (2%)
    pallas_call x6, Pallas kernels, call(): pl.pallas_call(kernel, grid=(1,), in_specs=[specs.get(i, whole(x.shape))...  9.8 us
    ppermute x4, waiting for transfers between devices, swap(): return lax.ppermute(x, axis, [(i, i ^ bit[i & 1]) for i in range(count)])  9.61 us
    ppermute x4, starting transfers between devices, swap(): return lax.ppermute(x, axis, [(i, i ^ bit[i & 1]) for i in range(count)])  7.29 us
    ppermute x1, starting transfers between devices, on_device(): far_in = lax.ppermute(far, ('parts', 'slab'), far_pairs)  3 us
    ppermute x2, waiting for transfers between devices, neighbour(): return lax.ppermute(x, axis, [(i, i ^ 1) for i in range(count)])  1.64 us
    ppermute x1, starting transfers between devices, on_device(): far_pg = lax.ppermute(far_pg, ('parts', 'slab'), far_pairs)  1.49 us
  transfers between devices with their start and end apart: 9, of which 6 were waited for; matrix products, arithmetic and copies ran while one was open for 0% of the time, Pallas kernels for 17%

profile of v3, /device:TPU:0, one launch (start us, length us, event | category | flops | bytes accessed | tf_op | source)
XLA Modules:
  0.0 34.5 jit_solution(11420086056438927660)
XLA Ops:
  0.7 1.0 %shard_map.76 = (bf16[128,256]{1,0:T(8,128)(2,1)S(1)}, bf16[128,256]{1,0:T(8,128)(2,1)S(1)}, bf16[64,1024]{1,0:T(8,128)(2,1)S(1)}, bf16[64,1024]{1,0:T(8,128)(2,1)S(1)}, bf16[16,1024]{1,0:T(8,128)(2,1)S(1)}) custom-call(s32[1]{0:T(128)} %bitcast.odd_ref, bf16[64,1024]{1,0:T(8,128)(2,1)} %bitcast.7, bf16[64,1024]{1,0:T(8,128)(2,1)} %bitcast.8, s32[27,1024]{1,0:T(8,128)} %bitcast.9), custom_call_target="tpu_custom_call" | custom-call | tf_op jit(solution)/shard_map/pallas_call | solution.py:303
  1.7 3.0 %collective-permute-start = (bf16[128,256]{1,0:T(8,128)(2,1)S(1)}, bf16[128,256]{1,0:T(8,128)(2,1)S(1)}, u32[]{:S(2)}, u32[]{:S(2)}) collective-permute-start(bf16[128,256]{1,0:T(8,128)(2,1)S(1)} %get-tuple-element.24), channel_id=1, source_target_pairs={{1,2},{2,1},{3,4},{4,3},{5,6},{6,5},{7,8},{8,7},{9,10},{10,9},{11,... | collective-permute-start | bytes 196616 | tf_op jit(solution)/shard_map/ppermute | solution.py:388
  4.7 0.1 collective-permute-start.1
  4.8 2.6 %shard_map.77 = (bf16[576,1024]{1,0:T(8,128)(2,1)S(1)}, bf16[576,1024]{1,0:T(8,128)(2,1)S(1)}, bf16[192,576]{1,0:T(8,128)(2,1)S(1)}, bf16[192,576]{1,0:T(8,128)(...) custom-call(bf16[64,1024]{1,0:T(8,128)(2,1)S(1)} %get-tuple-element.27.f_ref, ...), custom_call_target="tpu_custom_call" | custom-call | flops 452984832 | tf_op jit(solution)/shard_map/pallas_call | solution.py:303
  7.5 0.0 collective-permute-done.far_ref
  7.5 0.0 collective-permute-done.1.near_ref
  7.5 1.8 %shard_map.78 = (f32[864,128]{1,0:T(8,128)S(1)}, bf16[992,128]{1,0:T(8,128)(2,1)S(1)}, bf16[64,256]{1,0:T(8,128)(2,1)S(1)}, bf16[64,1024]{1,0:T(8,128)(2,1)S(1)}) custom-call(s32[1]{0:T(128)} %bitcast.odd_ref, bf16[128,256]{1,0:T(8,128)(2,1)S(1)} %collective-permute-done.far_ref, bf16[128,256]{1,0:T(8,128)(2,1)S(1)} %collective-permute-done.1.near_ref, ...), custom_call_target="tpu_custom_call" | custom-call | flops 452984832 | tf_op jit(solution)/shard_map/pallas_call | solution.py:303
  9.3 0.4 %collective-permute-start.2 = (bf16[992,128]{1,0:T(8,128)(2,1)S(1)}, bf16[992,128]{1,0:T(8,128)(2,1)S(1)}, u32[]{:S(2)}, u32[]{:S(2)}) collective-permute-start(bf16[992,128]{1,0:T(8,128)(2,1)S(1)} %get-tuple-element.35), channel_id=1, source_target_pairs={{0,1},{1,0},{2,3},{3,2},{4,5},{5,4},{6,7},{7,6},{8,9},{9,8},{10,11... | collective-permute-start | bytes 761864 | tf_op jit(solution)/shard_map/ppermute | solution.py:328
  9.7 1.2 %collective-permute-done.2.near_ref = bf16[992,128]{1,0:T(8,128)(2,1)S(1)} collective-permute-done((bf16[992,128]{1,0:T(8,128)(2,1)S(1)}, bf16[992,128]{1,0:T(8,128)(2,1)S(1)}, u32[]{:S(2)}, u32[]{:S(2)}) %collective-permute-start.2) | collective-permute-done | bytes 253984 | tf_op jit(solution)/shard_map/ppermute | solution.py:328
  10.9 1.6 %collective-permute-start.4 = (bf16[432,128]{1,0:T(8,128)(2,1)S(1)}, bf16[432,128]{1,0:T(8,128)(2,1)S(1)}, u32[]{:S(2)}, u32[]{:S(2)}) collective-permute-start(bf16[432,128]{1,0:T(8,128)(2,1)S(1)} %select_convert_fusion), channel_id=1, source_target_pairs={{0,2},{1,5},{2,0},{3,7},{4,6},{5,1},{6,4},{7,3},{8,10},{9,13},{10,... | collective-permute-start | bytes 331784 | tf_op jit(solution)/shard_map/ppermute | solution.py:325
  12.5 3.2 %collective-permute-done.4 = bf16[432,128]{1,0:T(8,128)(2,1)S(1)} collective-permute-done((bf16[432,128]{1,0:T(8,128)(2,1)S(1)}, bf16[432,128]{1,0:T(8,128)(2,1)S(1)}, u32[]{:S(2)}, u32[]{:S(2)}) %collective-permute-start.4) | collective-permute-done | bytes 110624 | tf_op jit(solution)/shard_map/ppermute | solution.py:325
  15.8 1.9 %collective-permute-start.5 = (bf16[432,128]{1,0:T(8,128)(2,1)S(1)}, bf16[432,128]{1,0:T(8,128)(2,1)S(1)}, u32[]{:S(2)}, u32[]{:S(2)}) collective-permute-start(bf16[432,128]{1,0:T(8,128)(2,1)S(1)} %add_convert_fusion.2), channel_id=1, source_target_pairs={{0,4},{1,9},{2,6},{3,11},{4,0},{5,13},{6,2},{7,15},{8,12},{9,1},{1... | collective-permute-start | bytes 331784 | tf_op jit(solution)/shard_map/ppermute | solution.py:325
  17.7 1.5 %collective-permute-start.3 = (bf16[64,256]{1,0:T(8,128)(2,1)S(1)}, bf16[64,256]{1,0:T(8,128)(2,1)S(1)}, u32[]{:S(2)}, u32[]{:S(2)}) collective-permute-start(bf16[64,256]{1,0:T(8,128)(2,1)S(1)} %get-tuple-element.36), channel_id=1, source_target_pairs={{1,2},{2,1},{3,4},{4,3},{5,6},{6,5},{7,8},{8,7},{9,10},{10,9},{11,... | collective-permute-start | bytes 98312 | tf_op jit(solution)/shard_map/ppermute | solution.py:407
  19.2 2.0 %collective-permute-done.5 = bf16[432,128]{1,0:T(8,128)(2,1)S(1)} collective-permute-done((bf16[432,128]{1,0:T(8,128)(2,1)S(1)}, bf16[432,128]{1,0:T(8,128)(2,1)S(1)}, u32[]{:S(2)}, u32[]{:S(2)}) %collective-permute-start.5) | collective-permute-done | bytes 110624 | tf_op jit(solution)/shard_map/ppermute | solution.py:325
  21.3 2.5 %collective-permute-start.6 = (bf16[432,128]{1,0:T(8,128)(2,1)S(1)}, bf16[432,128]{1,0:T(8,128)(2,1)S(1)}, u32[]{:S(2)}, u32[]{:S(2)}) collective-permute-start(bf16[432,128]{1,0:T(8,128)(2,1)S(1)} %add_convert_fusion.1._), channel_id=1, source_target_pairs={{0,8},{1,3},{2,10},{3,1},{4,12},{5,7},{6,14},{7,5},{8,0},{9,11},{1... | collective-permute-start | bytes 331784 | tf_op jit(solution)/shard_map/ppermute | solution.py:325
  23.7 0.0 collective-permute-done.3.far_ref
  23.7 2.4 %shard_map.79 = (bf16[64,1024]{1,0:T(8,128)(2,1)}, f32[8,128]{1,0:T(8,128)S(1)}) custom-call(s32[1]{0:T(128)} %bitcast.odd_ref, bf16[992,128]{1,0:T(8,128)(2,1)S(1)} %collective-permute-done.2.near_ref, bf16[64,256]{1,0:T(8,128)(2,1)S(1)} %collective-permute-done.3.far_ref, bf16[16,1024]{1,0:T(8,128)(2,1)S(1)} %get-tuple-element.26.m_ref, ...), custom_call_target="tpu_custom_call" | custom-call | flops 452984832 | tf_op jit(solution)/shard_map/pallas_call | solution.py:303
  26.1 0.8 %collective-permute-done.6 = bf16[432,128]{1,0:T(8,128)(2,1)S(1)} collective-permute-done((bf16[432,128]{1,0:T(8,128)(2,1)S(1)}, bf16[432,128]{1,0:T(8,128)(2,1)S(1)}, u32[]{:S(2)}, u32[]{:S(2)}) %collective-permute-start.6) | collective-permute-done | bytes 110624 | tf_op jit(solution)/shard_map/ppermute | solution.py:325
  27.0 1.3 %collective-permute-start.7 = (bf16[432,128]{1,0:T(8,128)(2,1)S(1)}, bf16[432,128]{1,0:T(8,128)(2,1)S(1)}, u32[]{:S(2)}, u32[]{:S(2)}) collective-permute-start(bf16[432,128]{1,0:T(8,128)(2,1)S(1)} %add_convert_fusion), channel_id=1, source_target_pairs={{0,2},{1,5},{2,0},{3,7},{4,6},{5,1},{6,4},{7,3},{8,10},{9,13},{10,... | collective-permute-start | bytes 331784 | tf_op jit(solution)/shard_map/ppermute | solution.py:325
  28.3 3.5 %collective-permute-done.7 = bf16[432,128]{1,0:T(8,128)(2,1)S(1)} collective-permute-done((bf16[432,128]{1,0:T(8,128)(2,1)S(1)}, bf16[432,128]{1,0:T(8,128)(2,1)S(1)}, u32[]{:S(2)}, u32[]{:S(2)}) %collective-permute-start.7) | collective-permute-done | bytes 110624 | tf_op jit(solution)/shard_map/ppermute | solution.py:325
  31.9 0.1 collective-permute-start.8
  32.0 1.0 %shard_map.80 = (f32[27,64,64]{2,1,0:T(8,128)}, f32[27,64,64]{2,1,0:T(8,128)}) custom-call(s32[1]{0:T(128)} %bitcast.odd_ref, bf16[864,128]{1,0:T(8,128)(2,1)S(1)} %pad_maximum_fusion.src), custom_call_target="tpu_custom_call" | custom-call | flops 226492416 | tf_op jit(solution)/shard_map/pallas_call | solution.py:303
  33.0 0.5 %collective-permute-done.8.src = bf16[864,128]{1,0:T(8,128)(2,1)S(1)} collective-permute-done((bf16[864,128]{1,0:T(8,128)(2,1)S(1)}, bf16[864,128]{1,0:T(8,128)(2,1)S(1)}, u32[]{:S(2)}, u32[]{:S(2)}) %collective-permute-start.8) | collective-permute-done | bytes 221216 | tf_op jit(solution)/shard_map/ppermute | solution.py:328
  33.4 1.0 %shard_map.81 = (f32[27,64,64]{2,1,0:T(8,128)}, f32[27,64,64]{2,1,0:T(8,128)}) custom-call(s32[1]{0:T(128)} %bitcast.odd_ref, bf16[864,128]{1,0:T(8,128)(2,1)S(1)} %collective-permute-done.8.src, f32[27,64,64]{2,1,0:T(8,128)} %get-tuple-element.41._one, f32[27,64,64]{2,1,0:T(8,128)} %get-tuple-element.42._two), custom_call_target="tpu_custom_call", output_to_operand_aliasing={{0}: (2, {}), {1}: (3, {})} | custom-call | tf_op jit(solution)/shard_map/pallas_call | solution.py:303
  (8 shorter events, 0.2 us)
Async XLA Ops:
  1.7 5.8 %collective-permute-start = (bf16[128,256]{1,0:T(8,128)(2,1)S(1)}, bf16[128,256]{1,0:T(8,128)(2,1)S(1)}, u32[]{:S(2)}, u32[]{:S(2)}) collective-permute-start(bf16[128,256]{1,0:T(8,128)(2,1)S(1)} %get-tuple-element.24), channel_id=1, source_target_pairs={{1,2},{2,1},{3,4},{4,3},{5,6},{6,5},{7,8},{8,7},{9,10},{10,9},{11,... | collective-permute-start | bytes 196616 | tf_op jit(solution)/shard_map/ppermute | solution.py:388
  4.7 2.8 %collective-permute-start.1 = (bf16[128,256]{1,0:T(8,128)(2,1)S(1)}, bf16[128,256]{1,0:T(8,128)(2,1)S(1)}, u32[]{:S(2)}, u32[]{:S(2)}) collective-permute-start(bf16[128,256]{1,0:T(8,128)(2,1)S(1)} %get-tuple-element.25), channel_id=1, source_target_pairs={{0,1},{1,0},{2,3},{3,2},{4,5},{5,4},{6,7},{7,6},{8,9},{9,8},{10,11... | collective-permute-start | bytes 196616 | tf_op jit(solution)/shard_map/ppermute | solution.py:387
  9.3 1.6 %collective-permute-start.2 = (bf16[992,128]{1,0:T(8,128)(2,1)S(1)}, bf16[992,128]{1,0:T(8,128)(2,1)S(1)}, u32[]{:S(2)}, u32[]{:S(2)}) collective-permute-start(bf16[992,128]{1,0:T(8,128)(2,1)S(1)} %get-tuple-element.35), channel_id=1, source_target_pairs={{0,1},{1,0},{2,3},{3,2},{4,5},{5,4},{6,7},{7,6},{8,9},{9,8},{10,11... | collective-permute-start | bytes 761864 | tf_op jit(solution)/shard_map/ppermute | solution.py:328
  10.9 4.8 %collective-permute-start.4 = (bf16[432,128]{1,0:T(8,128)(2,1)S(1)}, bf16[432,128]{1,0:T(8,128)(2,1)S(1)}, u32[]{:S(2)}, u32[]{:S(2)}) collective-permute-start(bf16[432,128]{1,0:T(8,128)(2,1)S(1)} %select_convert_fusion), channel_id=1, source_target_pairs={{0,2},{1,5},{2,0},{3,7},{4,6},{5,1},{6,4},{7,3},{8,10},{9,13},{10,... | collective-permute-start | bytes 331784 | tf_op jit(solution)/shard_map/ppermute | solution.py:325
  15.8 5.4 %collective-permute-start.5 = (bf16[432,128]{1,0:T(8,128)(2,1)S(1)}, bf16[432,128]{1,0:T(8,128)(2,1)S(1)}, u32[]{:S(2)}, u32[]{:S(2)}) collective-permute-start(bf16[432,128]{1,0:T(8,128)(2,1)S(1)} %add_convert_fusion.2), channel_id=1, source_target_pairs={{0,4},{1,9},{2,6},{3,11},{4,0},{5,13},{6,2},{7,15},{8,12},{9,1},{1... | collective-permute-start | bytes 331784 | tf_op jit(solution)/shard_map/ppermute | solution.py:325
  17.7 6.0 %collective-permute-start.3 = (bf16[64,256]{1,0:T(8,128)(2,1)S(1)}, bf16[64,256]{1,0:T(8,128)(2,1)S(1)}, u32[]{:S(2)}, u32[]{:S(2)}) collective-permute-start(bf16[64,256]{1,0:T(8,128)(2,1)S(1)} %get-tuple-element.36), channel_id=1, source_target_pairs={{1,2},{2,1},{3,4},{4,3},{5,6},{6,5},{7,8},{8,7},{9,10},{10,9},{11,... | collective-permute-start | bytes 98312 | tf_op jit(solution)/shard_map/ppermute | solution.py:407
  21.3 5.7 %collective-permute-start.6 = (bf16[432,128]{1,0:T(8,128)(2,1)S(1)}, bf16[432,128]{1,0:T(8,128)(2,1)S(1)}, u32[]{:S(2)}, u32[]{:S(2)}) collective-permute-start(bf16[432,128]{1,0:T(8,128)(2,1)S(1)} %add_convert_fusion.1._), channel_id=1, source_target_pairs={{0,8},{1,3},{2,10},{3,1},{4,12},{5,7},{6,14},{7,5},{8,0},{9,11},{1... | collective-permute-start | bytes 331784 | tf_op jit(solution)/shard_map/ppermute | solution.py:325
  27.0 4.8 %collective-permute-start.7 = (bf16[432,128]{1,0:T(8,128)(2,1)S(1)}, bf16[432,128]{1,0:T(8,128)(2,1)S(1)}, u32[]{:S(2)}, u32[]{:S(2)}) collective-permute-start(bf16[432,128]{1,0:T(8,128)(2,1)S(1)} %add_convert_fusion), channel_id=1, source_target_pairs={{0,2},{1,5},{2,0},{3,7},{4,6},{5,1},{6,4},{7,3},{8,10},{9,13},{10,... | collective-permute-start | bytes 331784 | tf_op jit(solution)/shard_map/ppermute | solution.py:325
  31.9 1.5 %collective-permute-start.8 = (bf16[864,128]{1,0:T(8,128)(2,1)S(1)}, bf16[864,128]{1,0:T(8,128)(2,1)S(1)}, u32[]{:S(2)}, u32[]{:S(2)}) collective-permute-start(bf16[864,128]{1,0:T(8,128)(2,1)S(1)} %pad_maximum_fusion.src), channel_id=1, source_target_pairs={{0,1},{1,0},{2,3},{3,2},{4,5},{5,4},{6,7},{7,6},{8,9},{9,8},{10,11... | collective-permute-start | bytes 663560 | tf_op jit(solution)/shard_map/ppermute | solution.py:328

commit v4 on v3

--- a/solution.py
+++ b/solution.py
@@ -94,7 +94,7 @@
         fill(far_ref, last)
 
 
-def own_kernel(f_ref, c_ref, w1_hbm, w2_hbm, s_f, s_c, wf, wb, pre_ref, hg_ref, w1, w2, turned, sems):
+def own_kernel(odd_ref, f_ref, c_ref, w1_hbm, w2_hbm, s_keep, s_send, wf, wb, pre_ref, hg_ref, w1, w2, turned, sems):
     chans, n = f_ref.shape
     copies = [
         pltpu.make_async_copy(w1_hbm, w1, sems.at[0]),
@@ -104,13 +104,23 @@
         copy.start()
     for copy in copies:
         copy.wait()
-    write_shifts(s_f, f_ref[...])
-    write_shifts(s_c, c_ref[...])
-    forward_weights(w1, turned, chans)
-    wf[...] = turned[...].T
-    spread_terms(pre_ref, dot(wf[...], s_f[...], 1, 0), chans)
-    backward_weights(w2, wb, chans)
-    spread_terms(hg_ref, dot(wb[...], s_c[...], 1, 0), chans)
+
+    def work(s_f, s_c):
+        write_shifts(s_f, f_ref[...])
+        write_shifts(s_c, c_ref[...])
+        forward_weights(w1, turned, chans)
+        wf[...] = turned[...].T
+        spread_terms(pre_ref, dot(wf[...], s_f[...], 1, 0), chans)
+        backward_weights(w2, wb, chans)
+        spread_terms(hg_ref, dot(wb[...], s_c[...], 1, 0), chans)
+
+    @pl.when(odd_ref[0] % 2 == 0)
+    def _():
+        work(s_keep, s_send)
+
+    @pl.when(odd_ref[0] % 2 != 0)
+    def _():
+        work(s_send, s_keep)
 
 
 def spread_terms(out_ref, terms, chans):
@@ -134,59 +144,84 @@
     return pre * sig * mask, (hg * mask * sig * (1.0 + pre * (1.0 - sig))).astype(BF)
 
 
-def grads_kernel(odd_ref, far_ref, near_ref, m_ref, s_f, s_c, wf, wb, pre_ref, hg_ref,
-                 keep_ref, send_ref, far_pg_ref, pg_ref, r_f, r_c, one_ref, two_ref):
-    chans = pg_ref.shape[0]
-    n = s_f.shape[1]
-    both = jnp.concatenate(sides(odd_ref, near_ref[...], far_ref[...]), 1)
-    write_shifts(r_f, both[:chans, :])
-    write_shifts(r_c, both[chans:, :])
+def fan(v):
+    blank = jnp.zeros((v.shape[0], RIM), BF)
+    after = jnp.concatenate([v[:, RIM:], blank], 1)
+    before = jnp.concatenate([blank, v[:, : v.shape[1] - RIM]], 1)
+    return jnp.concatenate([after, v, before], 0)
+
+
+def rim_fan(v):
+    blank = jnp.zeros((v.shape[0], RIM), BF)
+    first = jnp.concatenate([v[:, :RIM], blank], 1)
+    last = jnp.concatenate([blank, v[:, v.shape[1] - RIM :]], 1)
+    return jnp.concatenate([first, jnp.zeros_like(first), last], 0)
+
+
+def grad_one(ref, s_f, r_f, pg, one_ref):
+    one_ref[...] = dot(s_f[...], fan(pg), 1, 1) + dot(r_f[...], rim_fan(pg), 1, 1)
+    pack_one(ref, one_ref)
+
+
+def grad_two(ref, s_c, r_c, hidden, two_ref):
+    two_ref[...] = dot(fan(hidden), s_c[...], 1, 1) + dot(rim_fan(hidden), r_c[...], 1, 1)
+    pack_two(ref, two_ref)
+
+
+def send_kernel(odd_ref, far_ref, near_ref, m_ref, s_send, wf, wb, pre_ref, hg_ref,
+                send_ref, far_pg_ref, pg_ref, kept_ref, r_keep, r_send, one_ref, two_ref):
+    chans, n = pg_ref.shape
     rim = slice(0, RIM)
     end = slice(RIM, 2 * RIM)
-    low_pre = dot(wf[:chans, :], r_f[:, rim], 1, 0)
-    high_pre = dot(wf[2 * chans :, :], r_f[:, end], 1, 0)
-    low_hg = dot(wb[:chans, :], r_c[:, rim], 1, 0)
-    high_hg = dot(wb[2 * chans :, :], r_c[:, end], 1, 0)
-    mask = m_ref[0:1, :].astype(F32)
+    first = send_ref.shape[0] - RIM // 2
 
     def own(ref, low, high):
         mid = ref[:, RIM : RIM + n]
         return jnp.concatenate([mid[:, :RIM] + low, mid[:, RIM : n - RIM], mid[:, n - RIM :] + high], 1)
 
-    hidden, pg = slope(own(hg_ref, low_hg, high_hg), own(pre_ref, low_pre, high_pre), mask)
-    pg_ref[...] = pg
-    hidden = hidden.astype(BF)
-    blank = jnp.zeros((chans, RIM), BF)
-
-    def fan(v):
-        return jnp.concatenate(
-            [jnp.concatenate([v[:, RIM:], blank], 1), v, jnp.concatenate([blank, v[:, : n - RIM]], 1)], 0
-        )
-
-    def rim_fan(v, low, high):
-        parts = [jnp.concatenate([v[:, :RIM], blank], 1), jnp.concatenate([blank, v[:, n - RIM :]], 1)]
-        none = jnp.zeros((chans, 2 * RIM), BF)
-        return jnp.concatenate([parts[low], none, parts[high]], 0)
-
-    one_ref[...] = dot(s_f[...], fan(pg), 1, 1) + dot(r_f[...], rim_fan(pg, 0, 1), 1, 1)
-    two_ref[...] = dot(fan(hidden), s_c[...], 1, 1) + dot(rim_fan(hidden, 0, 1), r_c[...], 1, 1)
-    half = keep_ref.shape[0]
-
-    def part_with(pack_mine, pack_yours, near_plane, far_plane):
-        pack_mine(keep_ref)
-        pack_yours(send_ref)
+    def work(even, r_f, r_c):
+        far = jnp.where(odd_ref[0] >= 2, far_ref[...], jnp.zeros_like(far_ref))
+        near = near_ref[...]
+        both = jnp.concatenate([far, near] if even else [near, far], 1)
+        write_shifts(r_f, both[:chans, :])
+        write_shifts(r_c, both[chans:, :])
+        low_pre = dot(wf[:chans, :], r_f[:, rim], 1, 0)
+        high_pre = dot(wf[2 * chans :, :], r_f[:, end], 1, 0)
+        low_hg = dot(wb[:chans, :], r_c[:, rim], 1, 0)
+        high_hg = dot(wb[2 * chans :, :], r_c[:, end], 1, 0)
+        mask = m_ref[0:1, :].astype(F32)
+        hidden, pg = slope(own(hg_ref, low_hg, high_hg), own(pre_ref, low_pre, high_pre), mask)
+        hidden = hidden.astype(BF)
+        pg_ref[...] = pg
+        if even:
+            kept_ref[...] = pg
+            grad_two(send_ref, s_send, r_c, hidden, two_ref)
+        else:
+            kept_ref[...] = hidden
+            grad_one(send_ref, s_send, r_f, pg, one_ref)
+        near_plane, far_plane = (n - RIM, 0) if even else (0, n - RIM)
         for i in range(RIM // (2 * chans)):
             lanes = slice(near_plane + 2 * i * chans, near_plane + 2 * (i + 1) * chans)
-            send_ref[half + i * chans : half + (i + 1) * chans, :] = pg[:, lanes]
+            send_ref[first + i * chans : first + (i + 1) * chans, :] = pg[:, lanes]
         far_pg_ref[...] = pg[:, far_plane : far_plane + RIM]
 
     @pl.when(odd_ref[0] % 2 == 0)
     def _():
-        part_with(lambda ref: pack_one(ref, one_ref), lambda ref: pack_two(ref, two_ref), n - RIM, 0)
+        work(True, r_keep, r_send)
 
     @pl.when(odd_ref[0] % 2 != 0)
     def _():
-        part_with(lambda ref: pack_two(ref, two_ref), lambda ref: pack_one(ref, one_ref), 0, n - RIM)
+        work(False, r_send, r_keep)
+
+
+def keep_kernel(odd_ref, s_keep, rims, kept_ref, keep_ref, one_ref, two_ref):
+    @pl.when(odd_ref[0] % 2 == 0)
+    def _():
+        grad_one(keep_ref, s_keep, rims, kept_ref[...], one_ref)
+
+    @pl.when(odd_ref[0] % 2 != 0)
+    def _():
+        grad_two(keep_ref, s_keep, rims, kept_ref[...], two_ref)
 
 
 def pack_one(ref, one_ref):
@@ -318,7 +353,7 @@
     me = lax.axis_index(axis)
     is_odd = (me & 1) > 0
     bits = [1 << i for i in range(1, count.bit_length() - 1)]
-    even_bits, odd_bits = bits, bits[1:] + bits[:1]
+    even_bits, odd_bits = bits, bits[-1:] + bits[:-1]
 
     def swap(x, step):
         bit = (even_bits[step], odd_bits[step])
@@ -386,23 +421,33 @@
     near_pairs = [(i, i ^ 1) for i in range(count)]
     near_in = lax.ppermute(near, "slab", near_pairs)
     far_in = lax.ppermute(far, ("parts", "slab"), far_pairs)
-    s_f, s_c, wf, wb, pre, hg = call(
+    s_keep, s_send, wf, wb, pre, hg = call(
         own_kernel,
-        (f, c, weight_one, weight_two),
+        (odd, f, c, weight_one, weight_two),
         [array(taps, rows), array(taps, rows), array(3 * chans, taps), array(3 * chans, taps),
          array(chans, rows + 2 * RIM, kind=F32), array(chans, rows + 2 * RIM, kind=F32)],
         [weights, weights, pltpu.VMEM((taps, 3 * chans), BF), dma(2)],
-        {2: HBM, 3: HBM},
+        {0: SCALAR, 3: HBM, 4: HBM},
         flops=2 * 2 * rows * koff * chans * chans,
     )
     half = koff * chans // 2
-    keep, send, far_pg, pg = call(
-        grads_kernel,
-        (odd, far_in, near_in, m, s_f, s_c, wf, wb, pre, hg),
-        [array(half, 2 * chans, kind=F32), array(half + RIM // 2, 2 * chans), array(chans, RIM), array(chans, rows)],
-        [pltpu.VMEM((taps, 2 * RIM), BF), pltpu.VMEM((taps, 2 * RIM), BF), pltpu.VMEM((taps, 3 * chans), F32), pltpu.VMEM((3 * chans, taps), F32)],
+    grad_scratch = [pltpu.VMEM((taps, 3 * chans), F32), pltpu.VMEM((3 * chans, taps), F32)]
+    send, far_pg, pg, kept, rims = call(
+        send_kernel,
+        (odd, far_in, near_in, m, s_send, wf, wb, pre, hg),
+        [array(half + RIM // 2, 2 * chans), array(chans, RIM), array(chans, rows), array(chans, rows),
+         array(taps, 2 * RIM)],
+        [pltpu.VMEM((taps, 2 * RIM), BF), *grad_scratch],
         {0: SCALAR},
         flops=2 * 2 * rows * koff * chans * chans,
+    )
+    (keep,) = call(
+        keep_kernel,
+        (odd, s_keep, rims, kept),
+        [array(half, 2 * chans, kind=F32)],
+        grad_scratch,
+        {0: SCALAR},
+        flops=2 * rows * koff * chans * chans,
     )
     far_pg = lax.ppermute(far_pg, ("parts", "slab"), far_pairs)
     done = []
@@ -426,11 +471,11 @@
         mine_kernel, (odd, mine), grads, scratch, {0: SCALAR}, flops=2 * rows * koff * chans * chans,
         out_specs=[ANY, ANY],
     )
-    grad_one, grad_two = call(
+    first_grad, second_grad = call(
         yours_kernel, (odd, yours, *grads_out), grads, scratch, {0: SCALAR, 2: ANY, 3: ANY},
         out_specs=[ANY, ANY], aliases={2: 0, 3: 1},
     )
-    return done[0].T, grad_one, grad_two
+    return done[0].T, first_grad, second_grad
 
 
 def solution(mesh):

time: 34.7 us -> 33.7 us (0.971)
  waiting for transfers between devices: 11.3 us -> 8.92 us
  starting transfers between devices: 12.4 us -> 13.4 us
    ppermute x4, waiting for transfers between devices: 9.61 us -> 8.28 us  [swap(): return lax.ppermute(x, axis, [(i, i ^ bit[i & 1]) for i in range(count)])]
    ppermute x2, waiting for transfers between devices: 1.64 us -> 0.64 us  [neighbour(): return lax.ppermute(x, axis, [(i, i ^ 1) for i in range(count)])]
    ppermute x4, starting transfers between devices: 7.29 us -> 7.99 us  [swap(): return lax.ppermute(x, axis, [(i, i ^ bit[i & 1]) for i in range(count)])]
    pallas_call x6 -> x7, Pallas kernels: 9.8 us -> 10 us  [call(): pl.pallas_call(kernel, grid=(1,), in_specs=[specs.get(i, whole(x.shape))...]
  transfers between devices with their start and end apart: 9 -> 9, of which waited for: 6 -> 6; matrix products, arithmetic and copies ran while one was open for 0% -> 0% of each run, Pallas kernels for 17% -> 20%
where the time goes in v4:
time: 33.7 us; the launch traced here: 33.4 us
  starting transfers between devices  13.4 us (40%)
  Pallas kernels  10 us (30%)
  waiting for transfers between devices  8.92 us (26%)
  between operations  0.75 us (2%)
    pallas_call x7, Pallas kernels, call(): pl.pallas_call(kernel, grid=(1,), in_specs=[specs.get(i, whole(x.shape))...  10 us
    ppermute x4, waiting for transfers between devices, swap(): return lax.ppermute(x, axis, [(i, i ^ bit[i & 1]) for i in range(count)])  8.28 us
    ppermute x4, starting transfers between devices, swap(): return lax.ppermute(x, axis, [(i, i ^ bit[i & 1]) for i in range(count)])  7.99 us
    ppermute x1, starting transfers between devices, on_device(): far_in = lax.ppermute(far, ('parts', 'slab'), far_pairs)  3 us
    ppermute x1, starting transfers between devices, on_device(): far_pg = lax.ppermute(far_pg, ('parts', 'slab'), far_pairs)  1.49 us
    ppermute x2, starting transfers between devices, neighbour(): return lax.ppermute(x, axis, [(i, i ^ 1) for i in range(count)])  0.79 us
  transfers between devices with their start and end apart: 9, of which 6 were waited for; matrix products, arithmetic and copies ran while one was open for 0% of the time, Pallas kernels for 20%

profile of v4, /device:TPU:0, one launch (start us, length us, event | category | flops | bytes accessed | tf_op | source)
XLA Modules:
  0.0 33.4 jit_solution(17158854505796063554)
XLA Ops:
  0.7 1.0 %shard_map.76 = (bf16[128,256]{1,0:T(8,128)(2,1)S(1)}, bf16[128,256]{1,0:T(8,128)(2,1)S(1)}, bf16[64,1024]{1,0:T(8,128)(2,1)S(1)}, bf16[64,1024]{1,0:T(8,128)(2,1)S(1)}, bf16[16,1024]{1,0:T(8,128)(2,1)S(1)}) custom-call(s32[1]{0:T(128)} %bitcast.odd_ref, bf16[64,1024]{1,0:T(8,128)(2,1)} %bitcast.7, bf16[64,1024]{1,0:T(8,128)(2,1)} %bitcast.8, s32[27,1024]{1,0:T(8,128)} %bitcast.9), custom_call_target="tpu_custom_call" | custom-call | tf_op jit(solution)/shard_map/pallas_call | solution.py:338
  1.7 3.0 %collective-permute-start = (bf16[128,256]{1,0:T(8,128)(2,1)S(1)}, bf16[128,256]{1,0:T(8,128)(2,1)S(1)}, u32[]{:S(2)}, u32[]{:S(2)}) collective-permute-start(bf16[128,256]{1,0:T(8,128)(2,1)S(1)} %get-tuple-element.25), channel_id=1, source_target_pairs={{1,2},{2,1},{3,4},{4,3},{5,6},{6,5},{7,8},{8,7},{9,10},{10,9},{11,... | collective-permute-start | bytes 196616 | tf_op jit(solution)/shard_map/ppermute | solution.py:423
  4.7 0.1 collective-permute-start.1
  4.8 2.7 %shard_map.77 = (bf16[576,1024]{1,0:T(8,128)(2,1)S(1)}, bf16[576,1024]{1,0:T(8,128)(2,1)S(1)}, bf16[192,576]{1,0:T(8,128)(2,1)S(1)}, bf16[192,576]{1,0:T(8,128)(...) custom-call(s32[1]{0:T(128)} %bitcast.odd_ref, bf16[64,1024]{1,0:T(8,128)(2,1)S(1)} %get-tuple-element.28.f_ref, ...), custom_call_target="tpu_custom_call" | custom-call | flops 452984832 | tf_op jit(solution)/shard_map/pallas_call | solution.py:338
  7.5 0.0 collective-permute-done.far_ref
  7.5 0.0 collective-permute-done.1.near_ref
  7.5 1.3 %shard_map.78 = (bf16[992,128]{1,0:T(8,128)(2,1)S(1)}, bf16[64,256]{1,0:T(8,128)(2,1)S(1)}, bf16[64,1024]{1,0:T(8,128)(2,1)S(1)}, bf16[64,1024]{1,0:T(8,128)(2,1)S(1)}, bf16[576,512]{1,0:T(8,128)(2,1)S(1)}) custom-call(s32[1]{0:T(128)} %bitcast.odd_ref, bf16[128,256]{1,0:T(8,128)(2,1)S(1)} %collective-permute-done.far_ref, ...), custom_call_target="tpu_custom_call" | custom-call | flops 452984832 | tf_op jit(solution)/shard_map/pallas_call | solution.py:338
  8.8 0.4 %collective-permute-start.2 = (bf16[992,128]{1,0:T(8,128)(2,1)S(1)}, bf16[992,128]{1,0:T(8,128)(2,1)S(1)}, u32[]{:S(2)}, u32[]{:S(2)}) collective-permute-start(bf16[992,128]{1,0:T(8,128)(2,1)S(1)} %get-tuple-element.35), channel_id=1, source_target_pairs={{0,1},{1,0},{2,3},{3,2},{4,5},{5,4},{6,7},{7,6},{8,9},{9,8},{10,11... | collective-permute-start | bytes 761864 | tf_op jit(solution)/shard_map/ppermute | solution.py:363
  9.2 0.7 %shard_map.79 = f32[864,128]{1,0:T(8,128)S(1)} custom-call(s32[1]{0:T(128)} %bitcast.odd_ref, bf16[576,1024]{1,0:T(8,128)(2,1)S(1)} %get-tuple-element.38.s_keep, bf16[576,512]{1,0:T(8,128)(2,1)S(1)} %get-tuple-element.39.rims, bf16[64,1024]{1,0:T(8,128)(2,1)S(1)} %get-tuple-element.40.kept_ref), custom_call_target="tpu_custom_call" | custom-call | flops 226492416 | tf_op jit(solution)/shard_map/pallas_call | solution.py:338
  9.9 0.4 %collective-permute-done.2.near_ref = bf16[992,128]{1,0:T(8,128)(2,1)S(1)} collective-permute-done((bf16[992,128]{1,0:T(8,128)(2,1)S(1)}, bf16[992,128]{1,0:T(8,128)(2,1)S(1)}, u32[]{:S(2)}, u32[]{:S(2)}) %collective-permute-start.2) | collective-permute-done | bytes 253984 | tf_op jit(solution)/shard_map/ppermute | solution.py:363
  10.4 0.1 convert_add_fusion
  10.5 1.6 %collective-permute-start.4 = (bf16[432,128]{1,0:T(8,128)(2,1)S(1)}, bf16[432,128]{1,0:T(8,128)(2,1)S(1)}, u32[]{:S(2)}, u32[]{:S(2)}) collective-permute-start(bf16[432,128]{1,0:T(8,128)(2,1)S(1)} %select_convert_fusion), channel_id=1, source_target_pairs={{0,2},{1,9},{2,0},{3,11},{4,6},{5,13},{6,4},{7,15},{8,10},{9,1},{1... | collective-permute-start | bytes 331784 | tf_op jit(solution)/shard_map/ppermute | solution.py:360
  12.1 3.2 %collective-permute-done.4 = bf16[432,128]{1,0:T(8,128)(2,1)S(1)} collective-permute-done((bf16[432,128]{1,0:T(8,128)(2,1)S(1)}, bf16[432,128]{1,0:T(8,128)(2,1)S(1)}, u32[]{:S(2)}, u32[]{:S(2)}) %collective-permute-start.4) | collective-permute-done | bytes 110624 | tf_op jit(solution)/shard_map/ppermute | solution.py:360
  15.3 1.9 %collective-permute-start.5 = (bf16[432,128]{1,0:T(8,128)(2,1)S(1)}, bf16[432,128]{1,0:T(8,128)(2,1)S(1)}, u32[]{:S(2)}, u32[]{:S(2)}) collective-permute-start(bf16[432,128]{1,0:T(8,128)(2,1)S(1)} %add_convert_fusion.2), channel_id=1, source_target_pairs={{0,4},{1,3},{2,6},{3,1},{4,0},{5,7},{6,2},{7,5},{8,12},{9,11},{10,... | collective-permute-start | bytes 331784 | tf_op jit(solution)/shard_map/ppermute | solution.py:360
  17.2 1.5 %collective-permute-start.3 = (bf16[64,256]{1,0:T(8,128)(2,1)S(1)}, bf16[64,256]{1,0:T(8,128)(2,1)S(1)}, u32[]{:S(2)}, u32[]{:S(2)}) collective-permute-start(bf16[64,256]{1,0:T(8,128)(2,1)S(1)} %get-tuple-element.36), channel_id=1, source_target_pairs={{1,2},{2,1},{3,4},{4,3},{5,6},{6,5},{7,8},{8,7},{9,10},{10,9},{11,... | collective-permute-start | bytes 98312 | tf_op jit(solution)/shard_map/ppermute | solution.py:452
  18.7 1.4 %collective-permute-done.5 = bf16[432,128]{1,0:T(8,128)(2,1)S(1)} collective-permute-done((bf16[432,128]{1,0:T(8,128)(2,1)S(1)}, bf16[432,128]{1,0:T(8,128)(2,1)S(1)}, u32[]{:S(2)}, u32[]{:S(2)}) %collective-permute-start.5) | collective-permute-done | bytes 110624 | tf_op jit(solution)/shard_map/ppermute | solution.py:360
  20.2 2.9 %collective-permute-start.6 = (bf16[432,128]{1,0:T(8,128)(2,1)S(1)}, bf16[432,128]{1,0:T(8,128)(2,1)S(1)}, u32[]{:S(2)}, u32[]{:S(2)}) collective-permute-start(bf16[432,128]{1,0:T(8,128)(2,1)S(1)} %add_convert_fusion.1._), channel_id=1, source_target_pairs={{0,8},{1,5},{2,10},{3,7},{4,12},{5,1},{6,14},{7,3},{8,0},{9,13},{1... | collective-permute-start | bytes 331784 | tf_op jit(solution)/shard_map/ppermute | solution.py:360
  23.1 0.0 collective-permute-done.3.far_ref
  23.1 2.4 %shard_map.80 = (bf16[64,1024]{1,0:T(8,128)(2,1)}, f32[8,128]{1,0:T(8,128)S(1)}) custom-call(s32[1]{0:T(128)} %bitcast.odd_ref, bf16[992,128]{1,0:T(8,128)(2,1)S(1)} %collective-permute-done.2.near_ref, bf16[64,256]{1,0:T(8,128)(2,1)S(1)} %collective-permute-done.3.far_ref, bf16[16,1024]{1,0:T(8,128)(2,1)S(1)} %get-tuple-element.27.m_ref, ...), custom_call_target="tpu_custom_call" | custom-call | flops 452984832 | tf_op jit(solution)/shard_map/pallas_call | solution.py:338
  25.5 0.4 %collective-permute-done.6 = bf16[432,128]{1,0:T(8,128)(2,1)S(1)} collective-permute-done((bf16[432,128]{1,0:T(8,128)(2,1)S(1)}, bf16[432,128]{1,0:T(8,128)(2,1)S(1)}, u32[]{:S(2)}, u32[]{:S(2)}) %collective-permute-start.6) | collective-permute-done | bytes 110624 | tf_op jit(solution)/shard_map/ppermute | solution.py:360
  25.9 1.6 %collective-permute-start.7 = (bf16[432,128]{1,0:T(8,128)(2,1)S(1)}, bf16[432,128]{1,0:T(8,128)(2,1)S(1)}, u32[]{:S(2)}, u32[]{:S(2)}) collective-permute-start(bf16[432,128]{1,0:T(8,128)(2,1)S(1)} %add_convert_fusion), channel_id=1, source_target_pairs={{0,2},{1,9},{2,0},{3,11},{4,6},{5,13},{6,4},{7,15},{8,10},{9,1},{1... | collective-permute-start | bytes 331784 | tf_op jit(solution)/shard_map/ppermute | solution.py:360
  27.5 3.2 %collective-permute-done.7 = bf16[432,128]{1,0:T(8,128)(2,1)S(1)} collective-permute-done((bf16[432,128]{1,0:T(8,128)(2,1)S(1)}, bf16[432,128]{1,0:T(8,128)(2,1)S(1)}, u32[]{:S(2)}, u32[]{:S(2)}) %collective-permute-start.7) | collective-permute-done | bytes 110624 | tf_op jit(solution)/shard_map/ppermute | solution.py:360
  30.8 0.4 %collective-permute-start.8 = (bf16[864,128]{1,0:T(8,128)(2,1)S(1)}, bf16[864,128]{1,0:T(8,128)(2,1)S(1)}, u32[]{:S(2)}, u32[]{:S(2)}) collective-permute-start(bf16[864,128]{1,0:T(8,128)(2,1)S(1)} %pad_maximum_fusion.src), channel_id=1, source_target_pairs={{0,1},{1,0},{2,3},{3,2},{4,5},{5,4},{6,7},{7,6},{8,9},{9,8},{10,11... | collective-permute-start | bytes 663560 | tf_op jit(solution)/shard_map/ppermute | solution.py:363
  31.2 1.0 %shard_map.81 = (f32[27,64,64]{2,1,0:T(8,128)}, f32[27,64,64]{2,1,0:T(8,128)}) custom-call(s32[1]{0:T(128)} %bitcast.odd_ref, bf16[864,128]{1,0:T(8,128)(2,1)S(1)} %pad_maximum_fusion.src), custom_call_target="tpu_custom_call" | custom-call | flops 226492416 | tf_op jit(solution)/shard_map/pallas_call | solution.py:338
  32.2 0.2 collective-permute-done.8.src
  32.3 1.0 %shard_map.82 = (f32[27,64,64]{2,1,0:T(8,128)}, f32[27,64,64]{2,1,0:T(8,128)}) custom-call(s32[1]{0:T(128)} %bitcast.odd_ref, bf16[864,128]{1,0:T(8,128)(2,1)S(1)} %collective-permute-done.8.src, f32[27,64,64]{2,1,0:T(8,128)} %get-tuple-element.43._one, f32[27,64,64]{2,1,0:T(8,128)} %get-tuple-element.44._two), custom_call_target="tpu_custom_call", output_to_operand_aliasing={{0}: (2, {}), {1}: (3, {})} | custom-call | tf_op jit(solution)/shard_map/pallas_call | solution.py:338
  (7 shorter events, 0.2 us)
Async XLA Ops:
  1.7 5.8 %collective-permute-start = (bf16[128,256]{1,0:T(8,128)(2,1)S(1)}, bf16[128,256]{1,0:T(8,128)(2,1)S(1)}, u32[]{:S(2)}, u32[]{:S(2)}) collective-permute-start(bf16[128,256]{1,0:T(8,128)(2,1)S(1)} %get-tuple-element.25), channel_id=1, source_target_pairs={{1,2},{2,1},{3,4},{4,3},{5,6},{6,5},{7,8},{8,7},{9,10},{10,9},{11,... | collective-permute-start | bytes 196616 | tf_op jit(solution)/shard_map/ppermute | solution.py:423
  4.7 2.8 %collective-permute-start.1 = (bf16[128,256]{1,0:T(8,128)(2,1)S(1)}, bf16[128,256]{1,0:T(8,128)(2,1)S(1)}, u32[]{:S(2)}, u32[]{:S(2)}) collective-permute-start(bf16[128,256]{1,0:T(8,128)(2,1)S(1)} %get-tuple-element.26), channel_id=1, source_target_pairs={{0,1},{1,0},{2,3},{3,2},{4,5},{5,4},{6,7},{7,6},{8,9},{9,8},{10,11... | collective-permute-start | bytes 196616 | tf_op jit(solution)/shard_map/ppermute | solution.py:422
  8.8 1.6 %collective-permute-start.2 = (bf16[992,128]{1,0:T(8,128)(2,1)S(1)}, bf16[992,128]{1,0:T(8,128)(2,1)S(1)}, u32[]{:S(2)}, u32[]{:S(2)}) collective-permute-start(bf16[992,128]{1,0:T(8,128)(2,1)S(1)} %get-tuple-element.35), channel_id=1, source_target_pairs={{0,1},{1,0},{2,3},{3,2},{4,5},{5,4},{6,7},{7,6},{8,9},{9,8},{10,11... | collective-permute-start | bytes 761864 | tf_op jit(solution)/shard_map/ppermute | solution.py:363
  10.5 4.8 %collective-permute-start.4 = (bf16[432,128]{1,0:T(8,128)(2,1)S(1)}, bf16[432,128]{1,0:T(8,128)(2,1)S(1)}, u32[]{:S(2)}, u32[]{:S(2)}) collective-permute-start(bf16[432,128]{1,0:T(8,128)(2,1)S(1)} %select_convert_fusion), channel_id=1, source_target_pairs={{0,2},{1,9},{2,0},{3,11},{4,6},{5,13},{6,4},{7,15},{8,10},{9,1},{1... | collective-permute-start | bytes 331784 | tf_op jit(solution)/shard_map/ppermute | solution.py:360
  15.3 4.8 %collective-permute-start.5 = (bf16[432,128]{1,0:T(8,128)(2,1)S(1)}, bf16[432,128]{1,0:T(8,128)(2,1)S(1)}, u32[]{:S(2)}, u32[]{:S(2)}) collective-permute-start(bf16[432,128]{1,0:T(8,128)(2,1)S(1)} %add_convert_fusion.2), channel_id=1, source_target_pairs={{0,4},{1,3},{2,6},{3,1},{4,0},{5,7},{6,2},{7,5},{8,12},{9,11},{10,... | collective-permute-start | bytes 331784 | tf_op jit(solution)/shard_map/ppermute | solution.py:360
  17.2 5.9 %collective-permute-start.3 = (bf16[64,256]{1,0:T(8,128)(2,1)S(1)}, bf16[64,256]{1,0:T(8,128)(2,1)S(1)}, u32[]{:S(2)}, u32[]{:S(2)}) collective-permute-start(bf16[64,256]{1,0:T(8,128)(2,1)S(1)} %get-tuple-element.36), channel_id=1, source_target_pairs={{1,2},{2,1},{3,4},{4,3},{5,6},{6,5},{7,8},{8,7},{9,10},{10,9},{11,... | collective-permute-start | bytes 98312 | tf_op jit(solution)/shard_map/ppermute | solution.py:452
  20.2 5.7 %collective-permute-start.6 = (bf16[432,128]{1,0:T(8,128)(2,1)S(1)}, bf16[432,128]{1,0:T(8,128)(2,1)S(1)}, u32[]{:S(2)}, u32[]{:S(2)}) collective-permute-start(bf16[432,128]{1,0:T(8,128)(2,1)S(1)} %add_convert_fusion.1._), channel_id=1, source_target_pairs={{0,8},{1,5},{2,10},{3,7},{4,12},{5,1},{6,14},{7,3},{8,0},{9,13},{1... | collective-permute-start | bytes 331784 | tf_op jit(solution)/shard_map/ppermute | solution.py:360
  25.9 4.8 %collective-permute-start.7 = (bf16[432,128]{1,0:T(8,128)(2,1)S(1)}, bf16[432,128]{1,0:T(8,128)(2,1)S(1)}, u32[]{:S(2)}, u32[]{:S(2)}) collective-permute-start(bf16[432,128]{1,0:T(8,128)(2,1)S(1)} %add_convert_fusion), channel_id=1, source_target_pairs={{0,2},{1,9},{2,0},{3,11},{4,6},{5,13},{6,4},{7,15},{8,10},{9,1},{1... | collective-permute-start | bytes 331784 | tf_op jit(solution)/shard_map/ppermute | solution.py:360
  30.8 1.5 %collective-permute-start.8 = (bf16[864,128]{1,0:T(8,128)(2,1)S(1)}, bf16[864,128]{1,0:T(8,128)(2,1)S(1)}, u32[]{:S(2)}, u32[]{:S(2)}) collective-permute-start(bf16[864,128]{1,0:T(8,128)(2,1)S(1)} %pad_maximum_fusion.src), channel_id=1, source_target_pairs={{0,1},{1,0},{2,3},{3,2},{4,5},{5,4},{6,7},{7,6},{8,9},{9,8},{10,11... | collective-permute-start | bytes 663560 | tf_op jit(solution)/shard_map/ppermute | solution.py:363

commit v5 on v4

--- a/solution.py
+++ b/solution.py
@@ -81,17 +81,22 @@
         ref[:chans, :] = f_ref[:, lanes]
         ref[chans:, :] = c_ref[:, lanes]
 
+    def fill_far(lanes, next_lanes):
+        fill(far_ref.at[: 2 * chans, :], lanes)
+        fill(far_ref.at[2 * chans : 4 * chans, :], next_lanes)
+        far_ref[4 * chans :, :] = m_ref[:, lanes]
+
     first, last = slice(0, RIM), slice(n - RIM, n)
 
     @pl.when(odd == 0)
     def _():
         fill(near_ref, last)
-        fill(far_ref, first)
+        fill_far(first, slice(RIM, 2 * RIM))
 
     @pl.when(odd != 0)
     def _():
         fill(near_ref, first)
-        fill(far_ref, last)
+        fill_far(last, slice(n - 2 * RIM, n - RIM))
 
 
 def own_kernel(odd_ref, f_ref, c_ref, w1_hbm, w2_hbm, s_keep, s_send, wf, wb, pre_ref, hg_ref, w1, w2, turned, sems):
@@ -169,7 +174,7 @@
 
 
 def send_kernel(odd_ref, far_ref, near_ref, m_ref, s_send, wf, wb, pre_ref, hg_ref,
-                send_ref, far_pg_ref, pg_ref, kept_ref, r_keep, r_send, one_ref, two_ref):
+                send_ref, side_ref, pg_ref, kept_ref, r_keep, r_send, one_ref, two_ref):
     chans, n = pg_ref.shape
     rim = slice(0, RIM)
     end = slice(RIM, 2 * RIM)
@@ -180,7 +185,8 @@
         return jnp.concatenate([mid[:, :RIM] + low, mid[:, RIM : n - RIM], mid[:, n - RIM :] + high], 1)
 
     def work(even, r_f, r_c):
-        far = jnp.where(odd_ref[0] >= 2, far_ref[...], jnp.zeros_like(far_ref))
+        far = far_ref[: 2 * chans, :]
+        far = jnp.where(odd_ref[0] >= 2, far, jnp.zeros_like(far))
         near = near_ref[...]
         both = jnp.concatenate([far, near] if even else [near, far], 1)
         write_shifts(r_f, both[:chans, :])
@@ -199,11 +205,12 @@
         else:
             kept_ref[...] = hidden
             grad_one(send_ref, s_send, r_f, pg, one_ref)
-        near_plane, far_plane = (n - RIM, 0) if even else (0, n - RIM)
+        near_plane, beyond = (n - RIM, 0) if even else (0, n + RIM)
+        side_ref[:chans, :] = pre_ref[:, beyond : beyond + RIM]
+        side_ref[chans:, :] = hg_ref[:, beyond : beyond + RIM]
         for i in range(RIM // (2 * chans)):
             lanes = slice(near_plane + 2 * i * chans, near_plane + 2 * (i + 1) * chans)
             send_ref[first + i * chans : first + (i + 1) * chans, :] = pg[:, lanes]
-        far_pg_ref[...] = pg[:, far_plane : far_plane + RIM]
 
     @pl.when(odd_ref[0] % 2 == 0)
     def _():
@@ -212,6 +219,31 @@
     @pl.when(odd_ref[0] % 2 != 0)
     def _():
         work(False, r_send, r_keep)
+
+
+def far_kernel(odd_ref, far_ref, side_ref, wf, wb, _, plane_ref, s_near, s_off):
+    chans = plane_ref.shape[0]
+    own, twice = slice(0, chans), slice(chans, 2 * chans)
+
+    def work(even):
+        edge = slice(0, chans) if even else slice(2 * chans, 3 * chans)
+
+        def terms(w, rows):
+            write_shifts(s_near, far_ref[rows, :])
+            write_shifts(s_off, far_ref[rows.start + 2 * chans : rows.stop + 2 * chans, :])
+            return side_ref[rows, :] + dot(w[edge, :], s_off[...], 1, 0) + dot(w[twice, :], s_near[...], 1, 0)
+
+        mask = far_ref[4 * chans : 4 * chans + 1, :].astype(F32)
+        pre = terms(wf, own)
+        _, plane_ref[...] = slope(terms(wb, twice), pre, mask)
+
+    @pl.when(odd_ref[0] % 2 == 0)
+    def _():
+        work(True)
+
+    @pl.when(odd_ref[0] % 2 != 0)
+    def _():
+        work(False)
 
 
 def keep_kernel(odd_ref, s_keep, rims, kept_ref, keep_ref, one_ref, two_ref):
@@ -295,12 +327,21 @@
         write(unpack_two, two_hbm)
 
 
-def mine_kernel(odd_ref, src, one_hbm, two_hbm, wide, sems):
-    write_half(src, one_hbm, two_hbm, wide, sems, odd_ref[0] % 2 == 0)
-
-
-def yours_kernel(odd_ref, src, _one, _two, one_hbm, two_hbm, wide, sems):
-    write_half(src, one_hbm, two_hbm, wide, sems, odd_ref[0] % 2 != 0)
+def join(joined, parts):
+    first = 0
+    for part in parts:
+        joined[first : first + part.shape[0], :] = part[...]
+        first += part.shape[0]
+
+
+def mine_kernel(odd_ref, part, rest, one_hbm, two_hbm, joined, wide, sems):
+    join(joined, (part, rest))
+    write_half(joined, one_hbm, two_hbm, wide, sems, odd_ref[0] % 2 == 0)
+
+
+def yours_kernel(odd_ref, part, rest, _one, _two, one_hbm, two_hbm, joined, wide, sems):
+    join(joined, (part, rest))
+    write_half(joined, one_hbm, two_hbm, wide, sems, odd_ref[0] % 2 != 0)
 
 
 def last_kernel(odd_ref, near_ref, far_ref, m_ref, pg_ref, w1_hbm, _, out_ref, zero_ref, s_p, wb, w1, sems):
@@ -350,8 +391,6 @@
 
 def all_sum(keep, send, axis, beside):
     count = lax.axis_size(axis)
-    me = lax.axis_index(axis)
-    is_odd = (me & 1) > 0
     bits = [1 << i for i in range(1, count.bit_length() - 1)]
     even_bits, odd_bits = bits, bits[-1:] + bits[:-1]
 
@@ -363,21 +402,20 @@
         return lax.ppermute(x, axis, [(i, i ^ 1) for i in range(count)])
 
     came = neighbour(send)
-    cur = keep + came[: keep.shape[0]].astype(F32)
-    upper = (me & jnp.where(is_odd, odd_bits[0], even_bits[0])) > 0
-    n = cur.shape[0] // 2
-    low, high = cur[:n], cur[n:]
-    cur = jnp.where(upper, high, low) + swap(jnp.where(upper, low, high).astype(BF), 0).astype(F32)
-    for step in range(1, len(bits)):
-        sent = cur.astype(BF)
-        other = swap(sent, step)
-        if step == len(bits) - 1:
-            zero = beside(came, sent)
-        cur = sent.astype(F32) + other.astype(F32)
-    cur = (cur + zero).astype(BF)
-    other = swap(cur, 0)
-    cur = jnp.concatenate([jnp.where(upper, other, cur), jnp.where(upper, cur, other)], 0)
-    return cur, neighbour(cur)
+    rows = keep.shape[0]
+    split = rows * 9 // 16 // 16 * 16
+    whole_half = keep + came[:rows].astype(F32)
+    parts = [whole_half[:split], whole_half[split:]]
+    lasts = [None, None]
+    for step in range(len(bits)):
+        for i, part in enumerate(parts):
+            sent = part.astype(BF)
+            other = swap(sent, step)
+            parts[i] = sent.astype(F32) + other.astype(F32)
+            lasts[i] = sent
+    zero = beside(came, lasts[0])
+    parts = [(parts[0] + zero).astype(BF), parts[1].astype(BF)]
+    return parts, [neighbour(part) for part in parts]
 
 
 def far_partners(parts, count):
@@ -413,7 +451,7 @@
     near, far, f, c, m = call(
         prep_kernel,
         (odd, ft, ct, rt),
-        [array(*halo), array(*halo), array(chans, rows), array(chans, rows), array(16, rows)],
+        [array(*halo), array(4 * chans + 16, RIM), array(chans, rows), array(chans, rows), array(16, rows)],
         [pltpu.VMEM((8, rows), jnp.int32), dma(3)],
         {0: SCALAR, 1: HBM, 2: HBM, 3: HBM},
     )
@@ -432,10 +470,10 @@
     )
     half = koff * chans // 2
     grad_scratch = [pltpu.VMEM((taps, 3 * chans), F32), pltpu.VMEM((3 * chans, taps), F32)]
-    send, far_pg, pg, kept, rims = call(
+    send, side, pg, kept, rims = call(
         send_kernel,
         (odd, far_in, near_in, m, s_send, wf, wb, pre, hg),
-        [array(half + RIM // 2, 2 * chans), array(chans, RIM), array(chans, rows), array(chans, rows),
+        [array(half + RIM // 2, 2 * chans), array(2 * chans, RIM, kind=F32), array(chans, rows), array(chans, rows),
          array(taps, 2 * RIM)],
         [pltpu.VMEM((taps, 2 * RIM), BF), *grad_scratch],
         {0: SCALAR},
@@ -449,13 +487,20 @@
         {0: SCALAR},
         flops=2 * rows * koff * chans * chans,
     )
-    far_pg = lax.ppermute(far_pg, ("parts", "slab"), far_pairs)
     done = []
 
     def beside(came, sent):
+        (plane,) = call(
+            far_kernel,
+            (odd, far_in, side, wf, wb, sent),
+            [array(chans, RIM)],
+            [pltpu.VMEM((taps, RIM), BF), pltpu.VMEM((taps, RIM), BF)],
+            {0: SCALAR, 5: ANY},
+            flops=2 * RIM * koff * chans * chans,
+        )
         fg, zero = call(
             last_kernel,
-            (odd, came, far_pg, m, pg, weight_one, sent),
+            (odd, came, plane, m, pg, weight_one, sent),
             [array(chans, rows), array(8, 2 * chans, kind=F32)],
             [pltpu.VMEM((taps, rows + 2 * RIM), BF), pltpu.VMEM((3 * chans, taps), BF), weights, dma(1)],
             {0: SCALAR, 5: HBM, 6: ANY},
@@ -466,14 +511,14 @@
 
     mine, yours = all_sum(keep, send, "slab", beside)
     grads = [array(koff, chans, chans, kind=F32)] * 2
-    scratch = [pltpu.VMEM((koff, chans, chans), F32), dma(3)]
+    scratch = [pltpu.VMEM((half, 2 * chans), BF), pltpu.VMEM((koff, chans, chans), F32), dma(3)]
     grads_out = call(
-        mine_kernel, (odd, mine), grads, scratch, {0: SCALAR}, flops=2 * rows * koff * chans * chans,
+        mine_kernel, (odd, *mine), grads, scratch, {0: SCALAR}, flops=2 * rows * koff * chans * chans,
         out_specs=[ANY, ANY],
     )
     first_grad, second_grad = call(
-        yours_kernel, (odd, yours, *grads_out), grads, scratch, {0: SCALAR, 2: ANY, 3: ANY},
-        out_specs=[ANY, ANY], aliases={2: 0, 3: 1},
+        yours_kernel, (odd, *yours, *grads_out), grads, scratch, {0: SCALAR, 3: ANY, 4: ANY},
+        out_specs=[ANY, ANY], aliases={3: 0, 4: 1},
     )
     return done[0].T, first_grad, second_grad
 

time: 33.7 us -> 33.3 us (0.988)
  the two profiles are of different devices: /device:TPU:0 before, /device:TPU:7 now
where the time goes in v5:
time: 33.3 us; the launch traced here: 33.1 us
  starting transfers between devices  11.2 us (34%)
  Pallas kernels  10.7 us (32%)
  waiting for transfers between devices  10.2 us (31%)
  between operations  0.77 us (2%)
    pallas_call x8, Pallas kernels, call(): pl.pallas_call(kernel, grid=(1,), in_specs=[specs.get(i, whole(x.shape))...  10.7 us
    ppermute x6, waiting for transfers between devices, swap(): return lax.ppermute(x, axis, [(i, i ^ bit[i & 1]) for i in range(count)])  8.64 us
    ppermute x3, starting transfers between devices, neighbour(): return lax.ppermute(x, axis, [(i, i ^ 1) for i in range(count)])  4.96 us
    ppermute x6, starting transfers between devices, swap(): return lax.ppermute(x, axis, [(i, i ^ bit[i & 1]) for i in range(count)])  4.36 us
    ppermute x1, starting transfers between devices, on_device(): far_in = lax.ppermute(far, ('parts', 'slab'), far_pairs)  1.86 us
    ppermute x1, waiting for transfers between devices, on_device(): far_in = lax.ppermute(far, ('parts', 'slab'), far_pairs)  1.01 us
  transfers between devices with their start and end apart: 11, of which 7 were waited for; matrix products, arithmetic and copies ran while one was open for 1% of the time, Pallas kernels for 23%

profile of v5, /device:TPU:7, one launch (start us, length us, event | category | flops | bytes accessed | tf_op | source)
XLA Modules:
  0.0 33.1 jit_solution(1034164916115465961)
XLA Ops:
  0.6 1.1 %shard_map.76 = (bf16[128,256]{1,0:T(8,128)(2,1)S(1)}, bf16[272,256]{1,0:T(8,128)(2,1)S(1)}, bf16[64,1024]{1,0:T(8,128)(2,1)S(1)}, bf16[64,1024]{1,0:T(8,128)(2,1)S(1)}, bf16[16,1024]{1,0:T(8,128)(2,1)S(1)}) custom-call(s32[1]{0:T(128)} %bitcast.odd_ref, bf16[64,1024]{1,0:T(8,128)(2,1)} %bitcast.7, bf16[64,1024]{1,0:T(8,128)(2,1)} %bitcast.8, s32[27,1024]{1,0:T(8,128)} %bitcast.9), custom_call_target="tpu_custom_call" | custom-call | tf_op jit(solution)/shard_map/pallas_call | solution.py:379
  1.7 1.9 %collective-permute-start = (bf16[272,256]{1,0:T(8,128)(2,1)S(1)}, bf16[272,256]{1,0:T(8,128)(2,1)S(1)}, u32[]{:S(2)}, u32[]{:S(2)}) collective-permute-start(bf16[272,256]{1,0:T(8,128)(2,1)S(1)} %get-tuple-element.25), channel_id=1, source_target_pairs={{1,2},{2,1},{3,4},{4,3},{5,6},{6,5},{7,8},{8,7},{9,10},{10,9},{11,... | collective-permute-start | bytes 417800 | tf_op jit(solution)/shard_map/ppermute | solution.py:461
  3.6 0.0 collective-permute-start.1
  3.6 2.7 %shard_map.77 = (bf16[576,1024]{1,0:T(8,128)(2,1)S(1)}, bf16[576,1024]{1,0:T(8,128)(2,1)S(1)}, bf16[192,576]{1,0:T(8,128)(2,1)S(1)}, bf16[192,576]{1,0:T(8,128)(...) custom-call(s32[1]{0:T(128)} %bitcast.odd_ref, bf16[64,1024]{1,0:T(8,128)(2,1)S(1)} %get-tuple-element.28.f_ref, ...), custom_call_target="tpu_custom_call" | custom-call | flops 452984832 | tf_op jit(solution)/shard_map/pallas_call | solution.py:379
  6.2 0.0 collective-permute-done.1.near_ref
  6.2 1.0 %collective-permute-done.far_ref = bf16[272,256]{1,0:T(8,128)(2,1)S(1)} collective-permute-done((bf16[272,256]{1,0:T(8,128)(2,1)S(1)}, bf16[272,256]{1,0:T(8,128)(2,1)S(1)}, u32[]{:S(2)}, u32[]{:S(2)}) %collective-permute-start) | collective-permute-done | bytes 139296 | tf_op jit(solution)/shard_map/ppermute | solution.py:461
  7.3 1.2 %shard_map.78 = (bf16[992,128]{1,0:T(8,128)(2,1)S(1)}, f32[128,256]{1,0:T(8,128)S(1)}, bf16[64,1024]{1,0:T(8,128)(2,1)S(1)}, bf16[64,1024]{1,0:T(8,128)(2,1)S(1)}, bf16[576,512]{1,0:T(8,128)(2,1)S(1)}) custom-call(s32[1]{0:T(128)} %bitcast.odd_ref, bf16[272,256]{1,0:T(8,128)(2,1)S(1)} %collective-permute-done.far_ref, ...), custom_call_target="tpu_custom_call" | custom-call | flops 452984832 | tf_op jit(solution)/shard_map/pallas_call | solution.py:379
  8.5 1.3 %collective-permute-start.2 = (bf16[992,128]{1,0:T(8,128)(2,1)S(1)}, bf16[992,128]{1,0:T(8,128)(2,1)S(1)}, u32[]{:S(2)}, u32[]{:S(2)}) collective-permute-start(bf16[992,128]{1,0:T(8,128)(2,1)S(1)} %get-tuple-element.35), channel_id=1, source_target_pairs={{0,1},{1,0},{2,3},{3,2},{4,5},{5,4},{6,7},{7,6},{8,9},{9,8},{10,11... | collective-permute-start | bytes 761864 | tf_op jit(solution)/shard_map/ppermute | solution.py:402
  9.7 0.9 %shard_map.79 = f32[864,128]{1,0:T(8,128)S(1)} custom-call(s32[1]{0:T(128)} %bitcast.odd_ref, bf16[576,1024]{1,0:T(8,128)(2,1)S(1)} %get-tuple-element.37.s_keep, bf16[576,512]{1,0:T(8,128)(2,1)S(1)} %get-tuple-element.38.rims, bf16[64,1024]{1,0:T(8,128)(2,1)S(1)} %get-tuple-element.39.kept_ref), custom_call_target="tpu_custom_call" | custom-call | flops 226492416 | tf_op jit(solution)/shard_map/pallas_call | solution.py:379
  10.6 0.3 collective-permute-done.2.near_ref
  11.0 2.4 %collective-permute-start.7 = (bf16[384,128]{1,0:T(8,128)(2,1)S(1)}, bf16[384,128]{1,0:T(8,128)(2,1)S(1)}, u32[]{:S(2)}, u32[]{:S(2)}) collective-permute-start(bf16[384,128]{1,0:T(8,128)(2,1)S(1)} %slice.20), channel_id=1, source_target_pairs={{0,2},{1,9},{2,0},{3,11},{4,6},{5,13},{6,4},{7,15},{8,10},{9,1},{1... | collective-permute-start | bytes 294920 | tf_op jit(solution)/shard_map/ppermute | solution.py:399
  13.4 0.1 collective-permute-start.3
  13.5 1.9 %collective-permute-done.7 = bf16[384,128]{1,0:T(8,128)(2,1)S(1)} collective-permute-done((bf16[384,128]{1,0:T(8,128)(2,1)S(1)}, bf16[384,128]{1,0:T(8,128)(2,1)S(1)}, u32[]{:S(2)}, u32[]{:S(2)}) %collective-permute-start.7) | collective-permute-done | bytes 98336 | tf_op jit(solution)/shard_map/ppermute | solution.py:399
  15.4 0.1 collective-permute-start.8
  15.5 3.6 %collective-permute-done.3 = bf16[480,128]{1,0:T(8,128)(2,1)S(1)} collective-permute-done((bf16[480,128]{1,0:T(8,128)(2,1)S(1)}, bf16[480,128]{1,0:T(8,128)(2,1)S(1)}, u32[]{:S(2)}, u32[]{:S(2)}) %collective-permute-start.3) | collective-permute-done | bytes 122912 | tf_op jit(solution)/shard_map/ppermute | solution.py:399
  19.1 0.4 %collective-permute-start.4 = (bf16[480,128]{1,0:T(8,128)(2,1)S(1)}, bf16[480,128]{1,0:T(8,128)(2,1)S(1)}, u32[]{:S(2)}, u32[]{:S(2)}) collective-permute-start(bf16[480,128]{1,0:T(8,128)(2,1)S(1)} %add_convert_fusion.3), channel_id=1, source_target_pairs={{0,4},{1,3},{2,6},{3,1},{4,0},{5,7},{6,2},{7,5},{8,12},{9,11},{10,... | collective-permute-start | bytes 368648 | tf_op jit(solution)/shard_map/ppermute | solution.py:399
  19.5 0.0 collective-permute-done.8
  19.5 1.3 %collective-permute-start.9 = (bf16[384,128]{1,0:T(8,128)(2,1)S(1)}, bf16[384,128]{1,0:T(8,128)(2,1)S(1)}, u32[]{:S(2)}, u32[]{:S(2)}) collective-permute-start(bf16[384,128]{1,0:T(8,128)(2,1)S(1)} %add_convert_fusion.5), channel_id=1, source_target_pairs={{0,8},{1,5},{2,10},{3,7},{4,12},{5,1},{6,14},{7,3},{8,0},{9,13},{1... | collective-permute-start | bytes 294920 | tf_op jit(solution)/shard_map/ppermute | solution.py:399
  20.9 2.0 %collective-permute-done.4 = bf16[480,128]{1,0:T(8,128)(2,1)S(1)} collective-permute-done((bf16[480,128]{1,0:T(8,128)(2,1)S(1)}, bf16[480,128]{1,0:T(8,128)(2,1)S(1)}, u32[]{:S(2)}, u32[]{:S(2)}) %collective-permute-start.4) | collective-permute-done | bytes 122912 | tf_op jit(solution)/shard_map/ppermute | solution.py:399
  23.0 0.1 collective-permute-start.5
  23.0 0.5 %shard_map.80.far_ref = bf16[64,256]{1,0:T(8,128)(2,1)S(1)} custom-call(s32[1]{0:T(128)} %bitcast.odd_ref, bf16[272,256]{1,0:T(8,128)(2,1)S(1)} %collective-permute-done.far_ref, f32[128,256]{1,0:T(8,128)S(1)} %get-tuple-element.36.side_ref, bf16[192,576]{1,0:T(8,128)(2,1)S(1)} %get-tuple-element.31.wf, bf16[192,576]{1,0:T(8,128)(2,1)S(1)} %get-tuple-element.32.wb, ...), custom_call_target="tpu_custom_call" | custom-call | flops 56623104 | tf_op jit(solution)/shard_map/pallas_call | solution.py:379
  23.6 2.4 %shard_map.81 = (bf16[64,1024]{1,0:T(8,128)(2,1)}, f32[8,128]{1,0:T(8,128)S(1)}) custom-call(s32[1]{0:T(128)} %bitcast.odd_ref, bf16[992,128]{1,0:T(8,128)(2,1)S(1)} %collective-permute-done.2.near_ref, bf16[64,256]{1,0:T(8,128)(2,1)S(1)} %shard_map.80.far_ref, bf16[16,1024]{1,0:T(8,128)(2,1)S(1)} %get-tuple-element.27.m_ref, ...), custom_call_target="tpu_custom_call" | custom-call | flops 452984832 | tf_op jit(solution)/shard_map/pallas_call | solution.py:379
  26.0 1.1 %collective-permute-done.5 = bf16[480,128]{1,0:T(8,128)(2,1)S(1)} collective-permute-done((bf16[480,128]{1,0:T(8,128)(2,1)S(1)}, bf16[480,128]{1,0:T(8,128)(2,1)S(1)}, u32[]{:S(2)}, u32[]{:S(2)}) %collective-permute-start.5) | collective-permute-done | bytes 122912 | tf_op jit(solution)/shard_map/ppermute | solution.py:399
  27.1 3.6 %collective-permute-start.6 = (bf16[480,128]{1,0:T(8,128)(2,1)S(1)}, bf16[480,128]{1,0:T(8,128)(2,1)S(1)}, u32[]{:S(2)}, u32[]{:S(2)}) collective-permute-start(bf16[480,128]{1,0:T(8,128)(2,1)S(1)} %add_convert_fusion.1.part), channel_id=1, source_target_pairs={{0,1},{1,0},{2,3},{3,2},{4,5},{5,4},{6,7},{7,6},{8,9},{9,8},{10,11... | collective-permute-start | bytes 368648 | tf_op jit(solution)/shard_map/ppermute | solution.py:402
  30.7 0.0 collective-permute-done.9
  30.7 0.1 collective-permute-start.10
  30.8 1.0 %shard_map.82 = (f32[27,64,64]{2,1,0:T(8,128)}, f32[27,64,64]{2,1,0:T(8,128)}) custom-call(s32[1]{0:T(128)} %bitcast.odd_ref, bf16[480,128]{1,0:T(8,128)(2,1)S(1)} %add_convert_fusion.1.part, bf16[384,128]{1,0:T(8,128)(2,1)S(1)} %add_convert_fusion.4.rest), custom_call_target="tpu_custom_call" | custom-call | flops 226492416 | tf_op jit(solution)/shard_map/pallas_call | solution.py:379
  31.9 0.2 collective-permute-done.10.rest
  32.1 0.0 collective-permute-done.6.part
  32.1 1.0 %shard_map.83 = (f32[27,64,64]{2,1,0:T(8,128)}, f32[27,64,64]{2,1,0:T(8,128)}) custom-call(s32[1]{0:T(128)} %bitcast.odd_ref, bf16[480,128]{1,0:T(8,128)(2,1)S(1)} %collective-permute-done.6.part, bf16[384,128]{1,0:T(8,128)(2,1)S(1)} %collective-permute-done.10.rest, ...), custom_call_target="tpu_custom_call", output_to_operand_aliasing={{0}: (3, {}), {1}: (4, {})} | custom-call | tf_op jit(solution)/shard_map/pallas_call | solution.py:379
  (10 shorter events, 0.3 us)
Async XLA Ops:
  1.7 5.6 %collective-permute-start = (bf16[272,256]{1,0:T(8,128)(2,1)S(1)}, bf16[272,256]{1,0:T(8,128)(2,1)S(1)}, u32[]{:S(2)}, u32[]{:S(2)}) collective-permute-start(bf16[272,256]{1,0:T(8,128)(2,1)S(1)} %get-tuple-element.25), channel_id=1, source_target_pairs={{1,2},{2,1},{3,4},{4,3},{5,6},{6,5},{7,8},{8,7},{9,10},{10,9},{11,... | collective-permute-start | bytes 417800 | tf_op jit(solution)/shard_map/ppermute | solution.py:461
  3.6 2.7 %collective-permute-start.1 = (bf16[128,256]{1,0:T(8,128)(2,1)S(1)}, bf16[128,256]{1,0:T(8,128)(2,1)S(1)}, u32[]{:S(2)}, u32[]{:S(2)}) collective-permute-start(bf16[128,256]{1,0:T(8,128)(2,1)S(1)} %get-tuple-element.26), channel_id=1, source_target_pairs={{0,1},{1,0},{2,3},{3,2},{4,5},{5,4},{6,7},{7,6},{8,9},{9,8},{10,11... | collective-permute-start | bytes 196616 | tf_op jit(solution)/shard_map/ppermute | solution.py:460
  8.5 2.4 %collective-permute-start.2 = (bf16[992,128]{1,0:T(8,128)(2,1)S(1)}, bf16[992,128]{1,0:T(8,128)(2,1)S(1)}, u32[]{:S(2)}, u32[]{:S(2)}) collective-permute-start(bf16[992,128]{1,0:T(8,128)(2,1)S(1)} %get-tuple-element.35), channel_id=1, source_target_pairs={{0,1},{1,0},{2,3},{3,2},{4,5},{5,4},{6,7},{7,6},{8,9},{9,8},{10,11... | collective-permute-start | bytes 761864 | tf_op jit(solution)/shard_map/ppermute | solution.py:402
  11.0 4.4 %collective-permute-start.7 = (bf16[384,128]{1,0:T(8,128)(2,1)S(1)}, bf16[384,128]{1,0:T(8,128)(2,1)S(1)}, u32[]{:S(2)}, u32[]{:S(2)}) collective-permute-start(bf16[384,128]{1,0:T(8,128)(2,1)S(1)} %slice.20), channel_id=1, source_target_pairs={{0,2},{1,9},{2,0},{3,11},{4,6},{5,13},{6,4},{7,15},{8,10},{9,1},{1... | collective-permute-start | bytes 294920 | tf_op jit(solution)/shard_map/ppermute | solution.py:399
  13.4 5.7 %collective-permute-start.3 = (bf16[480,128]{1,0:T(8,128)(2,1)S(1)}, bf16[480,128]{1,0:T(8,128)(2,1)S(1)}, u32[]{:S(2)}, u32[]{:S(2)}) collective-permute-start(bf16[480,128]{1,0:T(8,128)(2,1)S(1)} %slice.19), channel_id=1, source_target_pairs={{0,2},{1,9},{2,0},{3,11},{4,6},{5,13},{6,4},{7,15},{8,10},{9,1},{1... | collective-permute-start | bytes 368648 | tf_op jit(solution)/shard_map/ppermute | solution.py:399
  15.4 4.1 %collective-permute-start.8 = (bf16[384,128]{1,0:T(8,128)(2,1)S(1)}, bf16[384,128]{1,0:T(8,128)(2,1)S(1)}, u32[]{:S(2)}, u32[]{:S(2)}) collective-permute-start(bf16[384,128]{1,0:T(8,128)(2,1)S(1)} %add_convert_fusion.6), channel_id=1, source_target_pairs={{0,4},{1,3},{2,6},{3,1},{4,0},{5,7},{6,2},{7,5},{8,12},{9,11},{10,... | collective-permute-start | bytes 294920 | tf_op jit(solution)/shard_map/ppermute | solution.py:399
  19.1 3.8 %collective-permute-start.4 = (bf16[480,128]{1,0:T(8,128)(2,1)S(1)}, bf16[480,128]{1,0:T(8,128)(2,1)S(1)}, u32[]{:S(2)}, u32[]{:S(2)}) collective-permute-start(bf16[480,128]{1,0:T(8,128)(2,1)S(1)} %add_convert_fusion.3), channel_id=1, source_target_pairs={{0,4},{1,3},{2,6},{3,1},{4,0},{5,7},{6,2},{7,5},{8,12},{9,11},{10,... | collective-permute-start | bytes 368648 | tf_op jit(solution)/shard_map/ppermute | solution.py:399
  19.5 11.2 %collective-permute-start.9 = (bf16[384,128]{1,0:T(8,128)(2,1)S(1)}, bf16[384,128]{1,0:T(8,128)(2,1)S(1)}, u32[]{:S(2)}, u32[]{:S(2)}) collective-permute-start(bf16[384,128]{1,0:T(8,128)(2,1)S(1)} %add_convert_fusion.5), channel_id=1, source_target_pairs={{0,8},{1,5},{2,10},{3,7},{4,12},{5,1},{6,14},{7,3},{8,0},{9,13},{1... | collective-permute-start | bytes 294920 | tf_op jit(solution)/shard_map/ppermute | solution.py:399
  23.0 4.1 %collective-permute-start.5 = (bf16[480,128]{1,0:T(8,128)(2,1)S(1)}, bf16[480,128]{1,0:T(8,128)(2,1)S(1)}, u32[]{:S(2)}, u32[]{:S(2)}) collective-permute-start(bf16[480,128]{1,0:T(8,128)(2,1)S(1)} %add_convert_fusion.2._), channel_id=1, source_target_pairs={{0,8},{1,5},{2,10},{3,7},{4,12},{5,1},{6,14},{7,3},{8,0},{9,13},{1... | collective-permute-start | bytes 368648 | tf_op jit(solution)/shard_map/ppermute | solution.py:399
  27.1 5.0 %collective-permute-start.6 = (bf16[480,128]{1,0:T(8,128)(2,1)S(1)}, bf16[480,128]{1,0:T(8,128)(2,1)S(1)}, u32[]{:S(2)}, u32[]{:S(2)}) collective-permute-start(bf16[480,128]{1,0:T(8,128)(2,1)S(1)} %add_convert_fusion.1.part), channel_id=1, source_target_pairs={{0,1},{1,0},{2,3},{3,2},{4,5},{5,4},{6,7},{7,6},{8,9},{9,8},{10,11... | collective-permute-start | bytes 368648 | tf_op jit(solution)/shard_map/ppermute | solution.py:402
  30.7 1.4 %collective-permute-start.10 = (bf16[384,128]{1,0:T(8,128)(2,1)S(1)}, bf16[384,128]{1,0:T(8,128)(2,1)S(1)}, u32[]{:S(2)}, u32[]{:S(2)}) collective-permute-start(bf16[384,128]{1,0:T(8,128)(2,1)S(1)} %add_convert_fusion.4.rest), channel_id=1, source_target_pairs={{0,1},{1,0},{2,3},{3,2},{4,5},{5,4},{6,7},{7,6},{8,9},{9,8},{10,11... | collective-permute-start | bytes 294920 | tf_op jit(solution)/shard_map/ppermute | solution.py:402

commit v6 on v5

--- a/solution.py
+++ b/solution.py
@@ -173,31 +173,66 @@
     pack_two(ref, two_ref)
 
 
-def send_kernel(odd_ref, far_ref, near_ref, m_ref, s_send, wf, wb, pre_ref, hg_ref,
+def near_kernel(odd_ref, near_ref, m_ref, wf, wb, pre_ref, hg_ref, r_keep, r_send, hid_ref, pg_ref):
+    chans, n = pg_ref.shape
+
+    def work(even, r_f, r_c):
+        write_shifts(r_f, near_ref[:chans, :])
+        write_shifts(r_c, near_ref[chans:, :])
+        edge = slice(2 * chans, 3 * chans) if even else slice(0, chans)
+        first = RIM if even else 0
+
+        def own(ref, more):
+            part = ref[:, RIM + first : first + n]
+            if even:
+                return jnp.concatenate([part[:, : n - 2 * RIM], part[:, n - 2 * RIM :] + more], 1)
+            return jnp.concatenate([part[:, :RIM] + more, part[:, RIM:]], 1)
+
+        pre = own(pre_ref, dot(wf[edge, :], r_f[...], 1, 0))
+        hg = own(hg_ref, dot(wb[edge, :], r_c[...], 1, 0))
+        lanes = slice(first, first + n - RIM)
+        hidden, pg = slope(hg, pre, m_ref[0:1, lanes].astype(F32))
+        far = slice(0, RIM) if even else slice(n - RIM, n)
+        hid_ref[:, lanes] = hidden.astype(BF)
+        pg_ref[:, lanes] = pg
+        hid_ref[:, far] = jnp.zeros((chans, RIM), BF)
+        pg_ref[:, far] = jnp.zeros((chans, RIM), BF)
+
+    @pl.when(odd_ref[0] % 2 == 0)
+    def _():
+        work(True, r_keep, r_send)
+
+    @pl.when(odd_ref[0] % 2 != 0)
+    def _():
+        work(False, r_send, r_keep)
+
+
+def send_kernel(odd_ref, far_ref, m_ref, s_send, wf, wb, pre_ref, hg_ref, near_keep, near_send, hid_part, pg_part,
                 send_ref, side_ref, pg_ref, kept_ref, r_keep, r_send, one_ref, two_ref):
     chans, n = pg_ref.shape
-    rim = slice(0, RIM)
-    end = slice(RIM, 2 * RIM)
     first = send_ref.shape[0] - RIM // 2
 
-    def own(ref, low, high):
-        mid = ref[:, RIM : RIM + n]
-        return jnp.concatenate([mid[:, :RIM] + low, mid[:, RIM : n - RIM], mid[:, n - RIM :] + high], 1)
-
     def work(even, r_f, r_c):
+        rim, end = slice(0, RIM), slice(RIM, 2 * RIM)
+        far_lanes, near_lanes = (rim, end) if even else (end, rim)
         far = far_ref[: 2 * chans, :]
         far = jnp.where(odd_ref[0] >= 2, far, jnp.zeros_like(far))
-        near = near_ref[...]
-        both = jnp.concatenate([far, near] if even else [near, far], 1)
-        write_shifts(r_f, both[:chans, :])
-        write_shifts(r_c, both[chans:, :])
-        low_pre = dot(wf[:chans, :], r_f[:, rim], 1, 0)
-        high_pre = dot(wf[2 * chans :, :], r_f[:, end], 1, 0)
-        low_hg = dot(wb[:chans, :], r_c[:, rim], 1, 0)
-        high_hg = dot(wb[2 * chans :, :], r_c[:, end], 1, 0)
-        mask = m_ref[0:1, :].astype(F32)
-        hidden, pg = slope(own(hg_ref, low_hg, high_hg), own(pre_ref, low_pre, high_pre), mask)
+        write_shifts(r_f.at[:, far_lanes], far[:chans, :])
+        write_shifts(r_c.at[:, far_lanes], far[chans:, :])
+        r_keep[:, near_lanes] = near_keep[...]
+        r_send[:, near_lanes] = near_send[...]
+        edge = slice(0, chans) if even else slice(2 * chans, 3 * chans)
+        own = slice(RIM, 2 * RIM) if even else slice(n, n + RIM)
+        pre = pre_ref[:, own] + dot(wf[edge, :], r_f[:, far_lanes], 1, 0)
+        hg = hg_ref[:, own] + dot(wb[edge, :], r_c[:, far_lanes], 1, 0)
+        hidden, pg = slope(hg, pre, m_ref[0:1, own.start - RIM : own.stop - RIM].astype(F32))
         hidden = hidden.astype(BF)
+        if even:
+            hidden = jnp.concatenate([hidden, hid_part[:, RIM:]], 1)
+            pg = jnp.concatenate([pg, pg_part[:, RIM:]], 1)
+        else:
+            hidden = jnp.concatenate([hid_part[:, : n - RIM], hidden], 1)
+            pg = jnp.concatenate([pg_part[:, : n - RIM], pg], 1)
         pg_ref[...] = pg
         if even:
             kept_ref[...] = pg
@@ -221,39 +256,32 @@
         work(False, r_send, r_keep)
 
 
-def far_kernel(odd_ref, far_ref, side_ref, wf, wb, _, plane_ref, s_near, s_off):
+def far_plane(even, far_ref, side_ref, wf, wb, plane_ref, s_near, s_off):
     chans = plane_ref.shape[0]
     own, twice = slice(0, chans), slice(chans, 2 * chans)
-
-    def work(even):
-        edge = slice(0, chans) if even else slice(2 * chans, 3 * chans)
-
-        def terms(w, rows):
-            write_shifts(s_near, far_ref[rows, :])
-            write_shifts(s_off, far_ref[rows.start + 2 * chans : rows.stop + 2 * chans, :])
-            return side_ref[rows, :] + dot(w[edge, :], s_off[...], 1, 0) + dot(w[twice, :], s_near[...], 1, 0)
-
-        mask = far_ref[4 * chans : 4 * chans + 1, :].astype(F32)
-        pre = terms(wf, own)
-        _, plane_ref[...] = slope(terms(wb, twice), pre, mask)
-
+    edge = slice(0, chans) if even else slice(2 * chans, 3 * chans)
+
+    def terms(w, rows):
+        write_shifts(s_near, far_ref[rows, :])
+        write_shifts(s_off, far_ref[rows.start + 2 * chans : rows.stop + 2 * chans, :])
+        return side_ref[rows, :] + dot(w[edge, :], s_off[...], 1, 0) + dot(w[twice, :], s_near[...], 1, 0)
+
+    mask = far_ref[4 * chans : 4 * chans + 1, :].astype(F32)
+    pre = terms(wf, own)
+    _, plane_ref[...] = slope(terms(wb, twice), pre, mask)
+
+
+def keep_kernel(odd_ref, s_keep, rims, kept_ref, far_ref, side_ref, wf, wb, keep_ref, plane_ref,
+                one_ref, two_ref, s_near, s_off):
     @pl.when(odd_ref[0] % 2 == 0)
     def _():
-        work(True)
+        grad_one(keep_ref, s_keep, rims, kept_ref[...], one_ref)
+        far_plane(True, far_ref, side_ref, wf, wb, plane_ref, s_near, s_off)
 
     @pl.when(odd_ref[0] % 2 != 0)
     def _():
-        work(False)
-
-
-def keep_kernel(odd_ref, s_keep, rims, kept_ref, keep_ref, one_ref, two_ref):
-    @pl.when(odd_ref[0] % 2 == 0)
-    def _():
-        grad_one(keep_ref, s_keep, rims, kept_ref[...], one_ref)
-
-    @pl.when(odd_ref[0] % 2 != 0)
-    def _():
         grad_two(keep_ref, s_keep, rims, kept_ref[...], two_ref)
+        far_plane(False, far_ref, side_ref, wf, wb, plane_ref, s_near, s_off)
 
 
 def pack_one(ref, one_ref):
@@ -359,6 +387,10 @@
     backward_weights(w1, wb, chans)
     out = join_planes(dot(wb[...], s_p[...], 1, 0), chans) * m_ref[0:1, :].astype(F32)
     out_ref[...] = out.astype(BF)
+
+
+def zeros_after(_, zero_ref):
+    zero_ref[...] = jnp.zeros_like(zero_ref)
 
 
 def whole(shape):
@@ -406,16 +438,18 @@
     split = rows * 9 // 16 // 16 * 16
     whole_half = keep + came[:rows].astype(F32)
     parts = [whole_half[:split], whole_half[split:]]
-    lasts = [None, None]
     for step in range(len(bits)):
         for i, part in enumerate(parts):
             sent = part.astype(BF)
             other = swap(sent, step)
+            if step == len(bits) - 1 and i == 0:
+                zero = beside(came, sent)
             parts[i] = sent.astype(F32) + other.astype(F32)
-            lasts[i] = sent
-    zero = beside(came, lasts[0])
-    parts = [(parts[0] + zero).astype(BF), parts[1].astype(BF)]
-    return parts, [neighbour(part) for part in parts]
+    second = parts[1].astype(BF)
+    near_second = neighbour(second)
+    (later,) = call(zeros_after, (near_second,), [jax.ShapeDtypeStruct((8, keep.shape[1]), F32)], specs={0: ANY})
+    first = (parts[0] + zero + later[:1]).astype(BF)
+    return [first, second], [neighbour(first), near_second]
 
 
 def far_partners(parts, count):
@@ -470,34 +504,33 @@
     )
     half = koff * chans // 2
     grad_scratch = [pltpu.VMEM((taps, 3 * chans), F32), pltpu.VMEM((3 * chans, taps), F32)]
+    near_keep, near_send, hid, pg = call(
+        near_kernel,
+        (odd, near_in, m, wf, wb, pre, hg),
+        [array(taps, RIM), array(taps, RIM), array(chans, rows), array(chans, rows)],
+        specs={0: SCALAR},
+        flops=2 * RIM * koff * chans * chans,
+    )
     send, side, pg, kept, rims = call(
         send_kernel,
-        (odd, far_in, near_in, m, s_send, wf, wb, pre, hg),
+        (odd, far_in, m, s_send, wf, wb, pre, hg, near_keep, near_send, hid, pg),
         [array(half + RIM // 2, 2 * chans), array(2 * chans, RIM, kind=F32), array(chans, rows), array(chans, rows),
          array(taps, 2 * RIM)],
         [pltpu.VMEM((taps, 2 * RIM), BF), *grad_scratch],
         {0: SCALAR},
         flops=2 * 2 * rows * koff * chans * chans,
     )
-    (keep,) = call(
+    keep, plane = call(
         keep_kernel,
-        (odd, s_keep, rims, kept),
-        [array(half, 2 * chans, kind=F32)],
-        grad_scratch,
+        (odd, s_keep, rims, kept, far_in, side, wf, wb),
+        [array(half, 2 * chans, kind=F32), array(chans, RIM)],
+        [*grad_scratch, pltpu.VMEM((taps, RIM), BF), pltpu.VMEM((taps, RIM), BF)],
         {0: SCALAR},
         flops=2 * rows * koff * chans * chans,
     )
     done = []
 
     def beside(came, sent):
-        (plane,) = call(
-            far_kernel,
-            (odd, far_in, side, wf, wb, sent),
-            [array(chans, RIM)],
-            [pltpu.VMEM((taps, RIM), BF), pltpu.VMEM((taps, RIM), BF)],
-            {0: SCALAR, 5: ANY},
-            flops=2 * RIM * koff * chans * chans,
-        )
         fg, zero = call(
             last_kernel,
             (odd, came, plane, m, pg, weight_one, sent),

time: 33.3 us -> 32.9 us (0.988)
  the two profiles are of different devices: /device:TPU:7 before, /device:TPU:0 now
where the time goes in v6:
time: 32.9 us; the launch traced here: 32.6 us
  starting transfers between devices  15 us (46%)
  Pallas kernels  10.6 us (32%)
  waiting for transfers between devices  5.89 us (18%)
  between operations  0.79 us (2%)
    ppermute x6, starting transfers between devices, swap(): return lax.ppermute(x, axis, [(i, i ^ bit[i & 1]) for i in range(count)])  11.2 us
    pallas_call x9, Pallas kernels, call(): pl.pallas_call(kernel, grid=(1,), in_specs=[specs.get(i, whole(x.shape))...  10.6 us
    ppermute x6, waiting for transfers between devices, swap(): return lax.ppermute(x, axis, [(i, i ^ bit[i & 1]) for i in range(count)])  4.06 us
    ppermute x1, starting transfers between devices, on_device(): far_in = lax.ppermute(far, ('parts', 'slab'), far_pairs)  3 us
    ppermute x3, waiting for transfers between devices, neighbour(): return lax.ppermute(x, axis, [(i, i ^ 1) for i in range(count)])  1.83 us
  transfers between devices with their start and end apart: 11, of which 6 were waited for; matrix products, arithmetic and copies ran while one was open for 1% of the time, Pallas kernels for 23%

profile of v6, /device:TPU:0, one launch (start us, length us, event | category | flops | bytes accessed | tf_op | source)
XLA Modules:
  0.0 32.6 jit_solution(17991831871240520696)
XLA Ops:
  0.6 1.0 %shard_map.76 = (bf16[128,256]{1,0:T(8,128)(2,1)S(1)}, bf16[272,256]{1,0:T(8,128)(2,1)S(1)}, bf16[64,1024]{1,0:T(8,128)(2,1)S(1)}, bf16[64,1024]{1,0:T(8,128)(2,1)S(1)}, bf16[16,1024]{1,0:T(8,128)(2,1)S(1)}) custom-call(s32[1]{0:T(128)} %bitcast.odd_ref, bf16[64,1024]{1,0:T(8,128)(2,1)} %bitcast.9, bf16[64,1024]{1,0:T(8,128)(2,1)} %bitcast.10, ...), custom_call_target="tpu_custom_call" | custom-call | tf_op jit(solution)/shard_map/pallas_call | solution.py:411
  1.7 3.0 %collective-permute-start = (bf16[272,256]{1,0:T(8,128)(2,1)S(1)}, bf16[272,256]{1,0:T(8,128)(2,1)S(1)}, u32[]{:S(2)}, u32[]{:S(2)}) collective-permute-start(bf16[272,256]{1,0:T(8,128)(2,1)S(1)} %get-tuple-element.31), channel_id=1, source_target_pairs={{1,2},{2,1},{3,4},{4,3},{5,6},{6,5},{7,8},{8,7},{9,10},{10,9},{11,... | collective-permute-start | bytes 417800 | tf_op jit(solution)/shard_map/ppermute | solution.py:495
  4.7 0.1 collective-permute-start.1
  4.9 2.7 %shard_map.77 = (bf16[576,1024]{1,0:T(8,128)(2,1)S(1)}, bf16[576,1024]{1,0:T(8,128)(2,1)S(1)}, bf16[192,576]{1,0:T(8,128)(2,1)S(1)}, bf16[192,576]{1,0:T(8,128)(...) custom-call(s32[1]{0:T(128)} %bitcast.odd_ref, bf16[64,1024]{1,0:T(8,128)(2,1)S(1)} %get-tuple-element.33.f_ref, ...), custom_call_target="tpu_custom_call" | custom-call | flops 452984832 | tf_op jit(solution)/shard_map/pallas_call | solution.py:411
  7.5 0.0 collective-permute-done.1.near_ref
  7.5 0.4 %shard_map.78 = (bf16[576,256]{1,0:T(8,128)(2,1)S(1)}, bf16[576,256]{1,0:T(8,128)(2,1)S(1)}, bf16[64,1024]{1,0:T(8,128)(2,1)S(1)}, bf16[64,1024]{1,0:T(8,128)(2,1)S(1)}) custom-call(s32[1]{0:T(128)} %bitcast.odd_ref, bf16[128,256]{1,0:T(8,128)(2,1)S(1)} %collective-permute-done.1.near_ref, bf16[16,1024]{1,0:T(8,128)(2,1)S(1)} %get-tuple-element.32.m_ref, ...), custom_call_target="tpu_custom_call" | custom-call | flops 56623104 | tf_op jit(solution)/shard_map/pallas_call | solution.py:411
  8.0 0.0 collective-permute-done.far_ref
  8.0 1.2 %shard_map.79 = (bf16[992,128]{1,0:T(8,128)(2,1)S(1)}, f32[128,256]{1,0:T(8,128)S(1)}, bf16[64,1024]{1,0:T(8,128)(2,1)S(1)}, bf16[64,1024]{1,0:T(8,128)(2,1)S(1)}, bf16[576,512]{1,0:T(8,128)(2,1)S(1)}) custom-call(s32[1]{0:T(128)} %bitcast.odd_ref, bf16[272,256]{1,0:T(8,128)(2,1)S(1)} %collective-permute-done.far_ref, ...), custom_call_target="tpu_custom_call" | custom-call | flops 452984832 | tf_op jit(solution)/shard_map/pallas_call | solution.py:411
  9.2 0.3 collective-permute-start.2
  9.5 0.9 %shard_map.80 = (f32[864,128]{1,0:T(8,128)S(1)}, bf16[64,256]{1,0:T(8,128)(2,1)S(1)}) custom-call(s32[1]{0:T(128)} %bitcast.odd_ref, bf16[576,1024]{1,0:T(8,128)(2,1)S(1)} %get-tuple-element.46.s_keep, bf16[576,512]{1,0:T(8,128)(2,1)S(1)} %get-tuple-element.47.rims, bf16[64,1024]{1,0:T(8,128)(2,1)S(1)} %get-tuple-element.48.kept_ref, ...), custom_call_target="tpu_custom_call" | custom-call | flops 226492416 | tf_op jit(solution)/shard_map/pallas_call | solution.py:411
  10.4 0.4 %collective-permute-done.2.near_ref = bf16[992,128]{1,0:T(8,128)(2,1)S(1)} collective-permute-done((bf16[992,128]{1,0:T(8,128)(2,1)S(1)}, bf16[992,128]{1,0:T(8,128)(2,1)S(1)}, u32[]{:S(2)}, u32[]{:S(2)}) %collective-permute-start.2) | collective-permute-done | bytes 253984 | tf_op jit(solution)/shard_map/ppermute | solution.py:434
  10.8 2.8 %collective-permute-start.6 = (bf16[384,128]{1,0:T(8,128)(2,1)S(1)}, bf16[384,128]{1,0:T(8,128)(2,1)S(1)}, u32[]{:S(2)}, u32[]{:S(2)}) collective-permute-start(bf16[384,128]{1,0:T(8,128)(2,1)S(1)} %slice.24), channel_id=1, source_target_pairs={{0,2},{1,9},{2,0},{3,11},{4,6},{5,13},{6,4},{7,15},{8,10},{9,1},{1... | collective-permute-start | bytes 294920 | tf_op jit(solution)/shard_map/ppermute | solution.py:431
  13.6 0.1 collective-permute-start.3
  13.7 2.5 %collective-permute-done.6 = bf16[384,128]{1,0:T(8,128)(2,1)S(1)} collective-permute-done((bf16[384,128]{1,0:T(8,128)(2,1)S(1)}, bf16[384,128]{1,0:T(8,128)(2,1)S(1)}, u32[]{:S(2)}, u32[]{:S(2)}) %collective-permute-start.6) | collective-permute-done | bytes 98336 | tf_op jit(solution)/shard_map/ppermute | solution.py:431
  16.3 1.7 %collective-permute-start.7 = (bf16[384,128]{1,0:T(8,128)(2,1)S(1)}, bf16[384,128]{1,0:T(8,128)(2,1)S(1)}, u32[]{:S(2)}, u32[]{:S(2)}) collective-permute-start(bf16[384,128]{1,0:T(8,128)(2,1)S(1)} %add_convert_fusion.6), channel_id=1, source_target_pairs={{0,4},{1,3},{2,6},{3,1},{4,0},{5,7},{6,2},{7,5},{8,12},{9,11},{10,... | collective-permute-start | bytes 294920 | tf_op jit(solution)/shard_map/ppermute | solution.py:431
  17.9 0.7 %collective-permute-done.3 = bf16[480,128]{1,0:T(8,128)(2,1)S(1)} collective-permute-done((bf16[480,128]{1,0:T(8,128)(2,1)S(1)}, bf16[480,128]{1,0:T(8,128)(2,1)S(1)}, u32[]{:S(2)}, u32[]{:S(2)}) %collective-permute-start.3) | collective-permute-done | bytes 122912 | tf_op jit(solution)/shard_map/ppermute | solution.py:431
  18.6 1.6 %collective-permute-start.4 = (bf16[480,128]{1,0:T(8,128)(2,1)S(1)}, bf16[480,128]{1,0:T(8,128)(2,1)S(1)}, u32[]{:S(2)}, u32[]{:S(2)}) collective-permute-start(bf16[480,128]{1,0:T(8,128)(2,1)S(1)} %add_convert_fusion.3), channel_id=1, source_target_pairs={{0,4},{1,3},{2,6},{3,1},{4,0},{5,7},{6,2},{7,5},{8,12},{9,11},{10,... | collective-permute-start | bytes 368648 | tf_op jit(solution)/shard_map/ppermute | solution.py:431
  20.3 0.9 %collective-permute-done.7 = bf16[384,128]{1,0:T(8,128)(2,1)S(1)} collective-permute-done((bf16[384,128]{1,0:T(8,128)(2,1)S(1)}, bf16[384,128]{1,0:T(8,128)(2,1)S(1)}, u32[]{:S(2)}, u32[]{:S(2)}) %collective-permute-start.7) | collective-permute-done | bytes 98336 | tf_op jit(solution)/shard_map/ppermute | solution.py:431
  21.2 2.5 %collective-permute-start.8 = (bf16[384,128]{1,0:T(8,128)(2,1)S(1)}, bf16[384,128]{1,0:T(8,128)(2,1)S(1)}, u32[]{:S(2)}, u32[]{:S(2)}) collective-permute-start(bf16[384,128]{1,0:T(8,128)(2,1)S(1)} %add_convert_fusion.5), channel_id=1, source_target_pairs={{0,8},{1,5},{2,10},{3,7},{4,12},{5,1},{6,14},{7,3},{8,0},{9,13},{1... | collective-permute-start | bytes 294920 | tf_op jit(solution)/shard_map/ppermute | solution.py:431
  23.6 0.0 collective-permute-done.4
  23.7 2.6 %collective-permute-start.5 = (bf16[480,128]{1,0:T(8,128)(2,1)S(1)}, bf16[480,128]{1,0:T(8,128)(2,1)S(1)}, u32[]{:S(2)}, u32[]{:S(2)}) collective-permute-start(bf16[480,128]{1,0:T(8,128)(2,1)S(1)} %add_convert_fusion.2._), channel_id=1, source_target_pairs={{0,8},{1,5},{2,10},{3,7},{4,12},{5,1},{6,14},{7,3},{8,0},{9,13},{1... | collective-permute-start | bytes 368648 | tf_op jit(solution)/shard_map/ppermute | solution.py:431
  26.3 2.4 %shard_map.81 = (bf16[64,1024]{1,0:T(8,128)(2,1)}, f32[8,128]{1,0:T(8,128)S(1)}) custom-call(s32[1]{0:T(128)} %bitcast.odd_ref, bf16[992,128]{1,0:T(8,128)(2,1)S(1)} %collective-permute-done.2.near_ref, bf16[64,256]{1,0:T(8,128)(2,1)S(1)} %get-tuple-element.50.far_ref, bf16[16,1024]{1,0:T(8,128)(2,1)S(1)} %get-tuple-element.32.m_ref, ...), custom_call_target="tpu_custom_call" | custom-call | flops 452984832 | tf_op jit(solution)/shard_map/pallas_call | solution.py:411
  28.6 0.0 collective-permute-done.8
  28.7 0.1 collective-permute-start.9
  28.8 1.3 %collective-permute-done.9._.rest = bf16[384,128]{1,0:T(8,128)(2,1)S(1)} collective-permute-done((bf16[384,128]{1,0:T(8,128)(2,1)S(1)}, bf16[384,128]{1,0:T(8,128)(2,1)S(1)}, u32[]{:S(2)}, u32[]{:S(2)}) %collective-permute-start.9) | collective-permute-done | bytes 98336 | tf_op jit(solution)/shard_map/ppermute | solution.py:434
  30.1 0.0 collective-permute-done.5
  30.1 0.1 add_convert_fusion.1.part
  30.1 0.2 collective-permute-start.10
  30.3 1.0 %shard_map.83 = (f32[27,64,64]{2,1,0:T(8,128)}, f32[27,64,64]{2,1,0:T(8,128)}) custom-call(s32[1]{0:T(128)} %bitcast.odd_ref, bf16[480,128]{1,0:T(8,128)(2,1)S(1)} %add_convert_fusion.1.part, bf16[384,128]{1,0:T(8,128)(2,1)S(1)} %add_convert_fusion.4.rest), custom_call_target="tpu_custom_call" | custom-call | flops 226492416 | tf_op jit(solution)/shard_map/pallas_call | solution.py:411
  31.3 0.2 collective-permute-done.10.part
  31.5 1.0 %shard_map.84 = (f32[27,64,64]{2,1,0:T(8,128)}, f32[27,64,64]{2,1,0:T(8,128)}) custom-call(s32[1]{0:T(128)} %bitcast.odd_ref, bf16[480,128]{1,0:T(8,128)(2,1)S(1)} %collective-permute-done.10.part, bf16[384,128]{1,0:T(8,128)(2,1)S(1)} %collective-permute-done.9._.rest, ...), custom_call_target="tpu_custom_call", output_to_operand_aliasing={{0}: (3, {}), {1}: (4, {})} | custom-call | tf_op jit(solution)/shard_map/pallas_call | solution.py:411
  (11 shorter events, 0.2 us)
Async XLA Ops:
  1.7 6.2 %collective-permute-start = (bf16[272,256]{1,0:T(8,128)(2,1)S(1)}, bf16[272,256]{1,0:T(8,128)(2,1)S(1)}, u32[]{:S(2)}, u32[]{:S(2)}) collective-permute-start(bf16[272,256]{1,0:T(8,128)(2,1)S(1)} %get-tuple-element.31), channel_id=1, source_target_pairs={{1,2},{2,1},{3,4},{4,3},{5,6},{6,5},{7,8},{8,7},{9,10},{10,9},{11,... | collective-permute-start | bytes 417800 | tf_op jit(solution)/shard_map/ppermute | solution.py:495
  4.7 2.8 %collective-permute-start.1 = (bf16[128,256]{1,0:T(8,128)(2,1)S(1)}, bf16[128,256]{1,0:T(8,128)(2,1)S(1)}, u32[]{:S(2)}, u32[]{:S(2)}) collective-permute-start(bf16[128,256]{1,0:T(8,128)(2,1)S(1)} %get-tuple-element.40), channel_id=1, source_target_pairs={{0,1},{1,0},{2,3},{3,2},{4,5},{5,4},{6,7},{7,6},{8,9},{9,8},{10,11... | collective-permute-start | bytes 196616 | tf_op jit(solution)/shard_map/ppermute | solution.py:494
  9.2 1.6 %collective-permute-start.2 = (bf16[992,128]{1,0:T(8,128)(2,1)S(1)}, bf16[992,128]{1,0:T(8,128)(2,1)S(1)}, u32[]{:S(2)}, u32[]{:S(2)}) collective-permute-start(bf16[992,128]{1,0:T(8,128)(2,1)S(1)} %get-tuple-element.45), channel_id=1, source_target_pairs={{0,1},{1,0},{2,3},{3,2},{4,5},{5,4},{6,7},{7,6},{8,9},{9,8},{10,11... | collective-permute-start | bytes 761864 | tf_op jit(solution)/shard_map/ppermute | solution.py:434
  10.8 5.4 %collective-permute-start.6 = (bf16[384,128]{1,0:T(8,128)(2,1)S(1)}, bf16[384,128]{1,0:T(8,128)(2,1)S(1)}, u32[]{:S(2)}, u32[]{:S(2)}) collective-permute-start(bf16[384,128]{1,0:T(8,128)(2,1)S(1)} %slice.24), channel_id=1, source_target_pairs={{0,2},{1,9},{2,0},{3,11},{4,6},{5,13},{6,4},{7,15},{8,10},{9,1},{1... | collective-permute-start | bytes 294920 | tf_op jit(solution)/shard_map/ppermute | solution.py:431
  13.6 4.9 %collective-permute-start.3 = (bf16[480,128]{1,0:T(8,128)(2,1)S(1)}, bf16[480,128]{1,0:T(8,128)(2,1)S(1)}, u32[]{:S(2)}, u32[]{:S(2)}) collective-permute-start(bf16[480,128]{1,0:T(8,128)(2,1)S(1)} %slice.23), channel_id=1, source_target_pairs={{0,2},{1,9},{2,0},{3,11},{4,6},{5,13},{6,4},{7,15},{8,10},{9,1},{1... | collective-permute-start | bytes 368648 | tf_op jit(solution)/shard_map/ppermute | solution.py:431
  16.3 4.9 %collective-permute-start.7 = (bf16[384,128]{1,0:T(8,128)(2,1)S(1)}, bf16[384,128]{1,0:T(8,128)(2,1)S(1)}, u32[]{:S(2)}, u32[]{:S(2)}) collective-permute-start(bf16[384,128]{1,0:T(8,128)(2,1)S(1)} %add_convert_fusion.6), channel_id=1, source_target_pairs={{0,4},{1,3},{2,6},{3,1},{4,0},{5,7},{6,2},{7,5},{8,12},{9,11},{10,... | collective-permute-start | bytes 294920 | tf_op jit(solution)/shard_map/ppermute | solution.py:431
  18.6 5.0 %collective-permute-start.4 = (bf16[480,128]{1,0:T(8,128)(2,1)S(1)}, bf16[480,128]{1,0:T(8,128)(2,1)S(1)}, u32[]{:S(2)}, u32[]{:S(2)}) collective-permute-start(bf16[480,128]{1,0:T(8,128)(2,1)S(1)} %add_convert_fusion.3), channel_id=1, source_target_pairs={{0,4},{1,3},{2,6},{3,1},{4,0},{5,7},{6,2},{7,5},{8,12},{9,11},{10,... | collective-permute-start | bytes 368648 | tf_op jit(solution)/shard_map/ppermute | solution.py:431
  21.2 7.5 %collective-permute-start.8 = (bf16[384,128]{1,0:T(8,128)(2,1)S(1)}, bf16[384,128]{1,0:T(8,128)(2,1)S(1)}, u32[]{:S(2)}, u32[]{:S(2)}) collective-permute-start(bf16[384,128]{1,0:T(8,128)(2,1)S(1)} %add_convert_fusion.5), channel_id=1, source_target_pairs={{0,8},{1,5},{2,10},{3,7},{4,12},{5,1},{6,14},{7,3},{8,0},{9,13},{1... | collective-permute-start | bytes 294920 | tf_op jit(solution)/shard_map/ppermute | solution.py:431
  23.7 6.4 %collective-permute-start.5 = (bf16[480,128]{1,0:T(8,128)(2,1)S(1)}, bf16[480,128]{1,0:T(8,128)(2,1)S(1)}, u32[]{:S(2)}, u32[]{:S(2)}) collective-permute-start(bf16[480,128]{1,0:T(8,128)(2,1)S(1)} %add_convert_fusion.2._), channel_id=1, source_target_pairs={{0,8},{1,5},{2,10},{3,7},{4,12},{5,1},{6,14},{7,3},{8,0},{9,13},{1... | collective-permute-start | bytes 368648 | tf_op jit(solution)/shard_map/ppermute | solution.py:431
  28.7 1.4 %collective-permute-start.9 = (bf16[384,128]{1,0:T(8,128)(2,1)S(1)}, bf16[384,128]{1,0:T(8,128)(2,1)S(1)}, u32[]{:S(2)}, u32[]{:S(2)}) collective-permute-start(bf16[384,128]{1,0:T(8,128)(2,1)S(1)} %add_convert_fusion.4.rest), channel_id=1, source_target_pairs={{0,1},{1,0},{2,3},{3,2},{4,5},{5,4},{6,7},{7,6},{8,9},{9,8},{10,11... | collective-permute-start | bytes 294920 | tf_op jit(solution)/shard_map/ppermute | solution.py:434
  30.1 1.4 %collective-permute-start.10 = (bf16[480,128]{1,0:T(8,128)(2,1)S(1)}, bf16[480,128]{1,0:T(8,128)(2,1)S(1)}, u32[]{:S(2)}, u32[]{:S(2)}) collective-permute-start(bf16[480,128]{1,0:T(8,128)(2,1)S(1)} %add_convert_fusion.1.part), channel_id=1, source_target_pairs={{0,1},{1,0},{2,3},{3,2},{4,5},{5,4},{6,7},{7,6},{8,9},{9,8},{10,11... | collective-permute-start | bytes 368648 | tf_op jit(solution)/shard_map/ppermute | solution.py:434

commit v7 on v6

--- a/solution.py
+++ b/solution.py
@@ -173,7 +173,7 @@
     pack_two(ref, two_ref)
 
 
-def near_kernel(odd_ref, near_ref, m_ref, wf, wb, pre_ref, hg_ref, r_keep, r_send, hid_ref, pg_ref):
+def near_kernel(odd_ref, near_ref, m_ref, wf, wb, pre_ref, hg_ref, s_send, r_keep, r_send, hid_ref, pg_ref, one_ref, two_ref):
     chans, n = pg_ref.shape
 
     def work(even, r_f, r_c):
@@ -197,6 +197,14 @@
         pg_ref[:, lanes] = pg
         hid_ref[:, far] = jnp.zeros((chans, RIM), BF)
         pg_ref[:, far] = jnp.zeros((chans, RIM), BF)
+        if even:
+            hidden = hid_ref[...]
+            two_ref[...] = dot(fan(hidden), s_send[...], 1, 1)
+            two_ref[2 * chans :, :] += dot(hidden[:, n - RIM :], r_c[...], 1, 1)
+        else:
+            pg = pg_ref[...]
+            one_ref[...] = dot(s_send[...], fan(pg), 1, 1)
+            one_ref[:, :chans] += dot(r_f[...], pg[:, :RIM], 1, 1)
 
     @pl.when(odd_ref[0] % 2 == 0)
     def _():
@@ -208,7 +216,7 @@
 
 
 def send_kernel(odd_ref, far_ref, m_ref, s_send, wf, wb, pre_ref, hg_ref, near_keep, near_send, hid_part, pg_part,
-                send_ref, side_ref, pg_ref, kept_ref, r_keep, r_send, one_ref, two_ref):
+                one_part, two_part, send_ref, side_ref, pg_ref, kept_ref, r_keep, r_send, one_ref, two_ref):
     chans, n = pg_ref.shape
     first = send_ref.shape[0] - RIM // 2
 
@@ -226,7 +234,8 @@
         pre = pre_ref[:, own] + dot(wf[edge, :], r_f[:, far_lanes], 1, 0)
         hg = hg_ref[:, own] + dot(wb[edge, :], r_c[:, far_lanes], 1, 0)
         hidden, pg = slope(hg, pre, m_ref[0:1, own.start - RIM : own.stop - RIM].astype(F32))
-        hidden = hidden.astype(BF)
+        far_hidden, far_pg = hidden.astype(BF), pg
+        hidden = far_hidden
         if even:
             hidden = jnp.concatenate([hidden, hid_part[:, RIM:]], 1)
             pg = jnp.concatenate([pg, pg_part[:, RIM:]], 1)
@@ -236,10 +245,18 @@
         pg_ref[...] = pg
         if even:
             kept_ref[...] = pg
-            grad_two(send_ref, s_send, r_c, hidden, two_ref)
+            beside = (r_c[:, far_lanes], s_send[:, :RIM], s_send[:, RIM : 2 * RIM])
+            for i, plane in enumerate(beside):
+                block = slice(i * chans, (i + 1) * chans)
+                two_ref[block, :] = two_part[block, :] + dot(far_hidden, plane, 1, 1)
+            pack_two(send_ref, two_ref)
         else:
             kept_ref[...] = hidden
-            grad_one(send_ref, s_send, r_f, pg, one_ref)
+            beside = (s_send[:, n - 2 * RIM : n - RIM], s_send[:, n - RIM :], r_f[:, far_lanes])
+            for i, plane in enumerate(beside):
+                block = slice(i * chans, (i + 1) * chans)
+                one_ref[:, block] = one_part[:, block] + dot(plane, far_pg, 1, 1)
+            pack_one(send_ref, one_ref)
         near_plane, beyond = (n - RIM, 0) if even else (0, n + RIM)
         side_ref[:chans, :] = pre_ref[:, beyond : beyond + RIM]
         side_ref[chans:, :] = hg_ref[:, beyond : beyond + RIM]
@@ -504,16 +521,17 @@
     )
     half = koff * chans // 2
     grad_scratch = [pltpu.VMEM((taps, 3 * chans), F32), pltpu.VMEM((3 * chans, taps), F32)]
-    near_keep, near_send, hid, pg = call(
+    near_keep, near_send, hid, pg, one, two = call(
         near_kernel,
-        (odd, near_in, m, wf, wb, pre, hg),
-        [array(taps, RIM), array(taps, RIM), array(chans, rows), array(chans, rows)],
+        (odd, near_in, m, wf, wb, pre, hg, s_send),
+        [array(taps, RIM), array(taps, RIM), array(chans, rows), array(chans, rows),
+         array(taps, 3 * chans, kind=F32), array(3 * chans, taps, kind=F32)],
         specs={0: SCALAR},
         flops=2 * RIM * koff * chans * chans,
     )
     send, side, pg, kept, rims = call(
         send_kernel,
-        (odd, far_in, m, s_send, wf, wb, pre, hg, near_keep, near_send, hid, pg),
+        (odd, far_in, m, s_send, wf, wb, pre, hg, near_keep, near_send, hid, pg, one, two),
         [array(half + RIM // 2, 2 * chans), array(2 * chans, RIM, kind=F32), array(chans, rows), array(chans, rows),
          array(taps, 2 * RIM)],
         [pltpu.VMEM((taps, 2 * RIM), BF), *grad_scratch],

time: 32.9 us -> 32.5 us (0.988)
  waiting for transfers between devices: 5.89 us -> 5.55 us
    ppermute x6, starting transfers between devices: 11.2 us -> 10.7 us  [swap(): return lax.ppermute(x, axis, [(i, i ^ bit[i & 1]) for i in range(count)])]
    ppermute x3, starting transfers between devices: 0.59 us -> 0.96 us  [neighbour(): return lax.ppermute(x, axis, [(i, i ^ 1) for i in range(count)])]
  transfers between devices with their start and end apart: 11 -> 11, of which waited for: 6 -> 6; matrix products, arithmetic and copies ran while one was open for 1% -> 1% of each run, Pallas kernels for 23% -> 24%
where the time goes in v7:
time: 32.5 us; the launch traced here: 32.1 us
  starting transfers between devices  14.8 us (46%)
  Pallas kernels  10.6 us (33%)
  waiting for transfers between devices  5.55 us (17%)
  between operations  0.78 us (2%)
    ppermute x6, starting transfers between devices, swap(): return lax.ppermute(x, axis, [(i, i ^ bit[i & 1]) for i in range(count)])  10.7 us
    pallas_call x9, Pallas kernels, call(): pl.pallas_call(kernel, grid=(1,), in_specs=[specs.get(i, whole(x.shape))...  10.6 us
    ppermute x6, waiting for transfers between devices, swap(): return lax.ppermute(x, axis, [(i, i ^ bit[i & 1]) for i in range(count)])  3.85 us
    ppermute x1, starting transfers between devices, on_device(): far_in = lax.ppermute(far, ('parts', 'slab'), far_pairs)  3 us
    ppermute x3, waiting for transfers between devices, neighbour(): return lax.ppermute(x, axis, [(i, i ^ 1) for i in range(count)])  1.7 us
    ppermute x3, starting transfers between devices, neighbour(): return lax.ppermute(x, axis, [(i, i ^ 1) for i in range(count)])  0.96 us
  transfers between devices with their start and end apart: 11, of which 6 were waited for; matrix products, arithmetic and copies ran while one was open for 1% of the time, Pallas kernels for 24%

profile of v7, /device:TPU:0, one launch (start us, length us, event | category | flops | bytes accessed | tf_op | source)
XLA Modules:
  0.0 32.1 jit_solution(10957844507860340888)
XLA Ops:
  0.6 1.0 %shard_map.76 = (bf16[128,256]{1,0:T(8,128)(2,1)S(1)}, bf16[272,256]{1,0:T(8,128)(2,1)S(1)}, bf16[64,1024]{1,0:T(8,128)(2,1)S(1)}, bf16[64,1024]{1,0:T(8,128)(2,1)S(1)}, bf16[16,1024]{1,0:T(8,128)(2,1)S(1)}) custom-call(s32[1]{0:T(128)} %bitcast.odd_ref, bf16[64,1024]{1,0:T(8,128)(2,1)} %bitcast.9, bf16[64,1024]{1,0:T(8,128)(2,1)} %bitcast.10, ...), custom_call_target="tpu_custom_call" | custom-call | tf_op jit(solution)/shard_map/pallas_call | solution.py:428
  1.7 3.0 %collective-permute-start = (bf16[272,256]{1,0:T(8,128)(2,1)S(1)}, bf16[272,256]{1,0:T(8,128)(2,1)S(1)}, u32[]{:S(2)}, u32[]{:S(2)}) collective-permute-start(bf16[272,256]{1,0:T(8,128)(2,1)S(1)} %get-tuple-element.33), channel_id=1, source_target_pairs={{1,2},{2,1},{3,4},{4,3},{5,6},{6,5},{7,8},{8,7},{9,10},{10,9},{11,... | collective-permute-start | bytes 417800 | tf_op jit(solution)/shard_map/ppermute | solution.py:512
  4.7 0.1 collective-permute-start.1
  4.9 2.7 %shard_map.77 = (bf16[576,1024]{1,0:T(8,128)(2,1)S(1)}, bf16[576,1024]{1,0:T(8,128)(2,1)S(1)}, bf16[192,576]{1,0:T(8,128)(2,1)S(1)}, bf16[192,576]{1,0:T(8,128)(...) custom-call(s32[1]{0:T(128)} %bitcast.odd_ref, bf16[64,1024]{1,0:T(8,128)(2,1)S(1)} %get-tuple-element.35.f_ref, ...), custom_call_target="tpu_custom_call" | custom-call | flops 452984832 | tf_op jit(solution)/shard_map/pallas_call | solution.py:428
  7.5 0.0 collective-permute-done.1.near_ref
  7.5 0.9 %shard_map.78 = (bf16[576,256]{1,0:T(8,128)(2,1)S(1)}, bf16[576,256]{1,0:T(8,128)(2,1)S(1)}, bf16[64,1024]{1,0:T(8,128)(2,1)S(1)}, bf16[64,1024]{1,0:T(8,128)(2,...) custom-call(s32[1]{0:T(128)} %bitcast.odd_ref, bf16[128,256]{1,0:T(8,128)(2,1)S(1)} %collective-permute-done.1.near_ref, ...), custom_call_target="tpu_custom_call" | custom-call | flops 56623104 | tf_op jit(solution)/shard_map/pallas_call | solution.py:428
  8.4 0.0 collective-permute-done.far_ref
  8.4 0.7 %shard_map.79 = (bf16[992,128]{1,0:T(8,128)(2,1)S(1)}, f32[128,256]{1,0:T(8,128)S(1)}, bf16[64,1024]{1,0:T(8,128)(2,1)S(1)}, bf16[64,1024]{1,0:T(8,128)(2,1)S(1)}, bf16[576,512]{1,0:T(8,128)(2,1)S(1)}) custom-call(s32[1]{0:T(128)} %bitcast.odd_ref, bf16[272,256]{1,0:T(8,128)(2,1)S(1)} %collective-permute-done.far_ref, ...), custom_call_target="tpu_custom_call" | custom-call | flops 452984832 | tf_op jit(solution)/shard_map/pallas_call | solution.py:428
  9.1 0.7 %collective-permute-start.2 = (bf16[992,128]{1,0:T(8,128)(2,1)S(1)}, bf16[992,128]{1,0:T(8,128)(2,1)S(1)}, u32[]{:S(2)}, u32[]{:S(2)}) collective-permute-start(bf16[992,128]{1,0:T(8,128)(2,1)S(1)} %get-tuple-element.49), channel_id=1, source_target_pairs={{0,1},{1,0},{2,3},{3,2},{4,5},{5,4},{6,7},{7,6},{8,9},{9,8},{10,11... | collective-permute-start | bytes 761864 | tf_op jit(solution)/shard_map/ppermute | solution.py:451
  9.8 0.9 %shard_map.80 = (f32[864,128]{1,0:T(8,128)S(1)}, bf16[64,256]{1,0:T(8,128)(2,1)S(1)}) custom-call(s32[1]{0:T(128)} %bitcast.odd_ref, bf16[576,1024]{1,0:T(8,128)(2,1)S(1)} %get-tuple-element.50.s_keep, bf16[576,512]{1,0:T(8,128)(2,1)S(1)} %get-tuple-element.51.rims, bf16[64,1024]{1,0:T(8,128)(2,1)S(1)} %get-tuple-element.52.kept_ref, ...), custom_call_target="tpu_custom_call" | custom-call | flops 226492416 | tf_op jit(solution)/shard_map/pallas_call | solution.py:428
  10.7 0.2 collective-permute-done.2.near_ref
  11.0 0.1 add_convert_fusion
  11.0 2.1 %collective-permute-start.6 = (bf16[384,128]{1,0:T(8,128)(2,1)S(1)}, bf16[384,128]{1,0:T(8,128)(2,1)S(1)}, u32[]{:S(2)}, u32[]{:S(2)}) collective-permute-start(bf16[384,128]{1,0:T(8,128)(2,1)S(1)} %slice.24), channel_id=1, source_target_pairs={{0,2},{1,9},{2,0},{3,11},{4,6},{5,13},{6,4},{7,15},{8,10},{9,1},{1... | collective-permute-start | bytes 294920 | tf_op jit(solution)/shard_map/ppermute | solution.py:448
  13.1 0.1 collective-permute-start.3
  13.2 2.5 %collective-permute-done.6 = bf16[384,128]{1,0:T(8,128)(2,1)S(1)} collective-permute-done((bf16[384,128]{1,0:T(8,128)(2,1)S(1)}, bf16[384,128]{1,0:T(8,128)(2,1)S(1)}, u32[]{:S(2)}, u32[]{:S(2)}) %collective-permute-start.6) | collective-permute-done | bytes 98336 | tf_op jit(solution)/shard_map/ppermute | solution.py:448
  15.8 1.9 %collective-permute-start.7 = (bf16[384,128]{1,0:T(8,128)(2,1)S(1)}, bf16[384,128]{1,0:T(8,128)(2,1)S(1)}, u32[]{:S(2)}, u32[]{:S(2)}) collective-permute-start(bf16[384,128]{1,0:T(8,128)(2,1)S(1)} %add_convert_fusion.6), channel_id=1, source_target_pairs={{0,4},{1,3},{2,6},{3,1},{4,0},{5,7},{6,2},{7,5},{8,12},{9,11},{10,... | collective-permute-start | bytes 294920 | tf_op jit(solution)/shard_map/ppermute | solution.py:448
  17.6 0.5 %collective-permute-done.3 = bf16[480,128]{1,0:T(8,128)(2,1)S(1)} collective-permute-done((bf16[480,128]{1,0:T(8,128)(2,1)S(1)}, bf16[480,128]{1,0:T(8,128)(2,1)S(1)}, u32[]{:S(2)}, u32[]{:S(2)}) %collective-permute-start.3) | collective-permute-done | bytes 122912 | tf_op jit(solution)/shard_map/ppermute | solution.py:448
  18.1 1.6 %collective-permute-start.4 = (bf16[480,128]{1,0:T(8,128)(2,1)S(1)}, bf16[480,128]{1,0:T(8,128)(2,1)S(1)}, u32[]{:S(2)}, u32[]{:S(2)}) collective-permute-start(bf16[480,128]{1,0:T(8,128)(2,1)S(1)} %add_convert_fusion.3), channel_id=1, source_target_pairs={{0,4},{1,3},{2,6},{3,1},{4,0},{5,7},{6,2},{7,5},{8,12},{9,11},{10,... | collective-permute-start | bytes 368648 | tf_op jit(solution)/shard_map/ppermute | solution.py:448
  19.8 0.9 %collective-permute-done.7 = bf16[384,128]{1,0:T(8,128)(2,1)S(1)} collective-permute-done((bf16[384,128]{1,0:T(8,128)(2,1)S(1)}, bf16[384,128]{1,0:T(8,128)(2,1)S(1)}, u32[]{:S(2)}, u32[]{:S(2)}) %collective-permute-start.7) | collective-permute-done | bytes 98336 | tf_op jit(solution)/shard_map/ppermute | solution.py:448
  20.7 2.7 %collective-permute-start.8 = (bf16[384,128]{1,0:T(8,128)(2,1)S(1)}, bf16[384,128]{1,0:T(8,128)(2,1)S(1)}, u32[]{:S(2)}, u32[]{:S(2)}) collective-permute-start(bf16[384,128]{1,0:T(8,128)(2,1)S(1)} %add_convert_fusion.5), channel_id=1, source_target_pairs={{0,8},{1,5},{2,10},{3,7},{4,12},{5,1},{6,14},{7,3},{8,0},{9,13},{1... | collective-permute-start | bytes 294920 | tf_op jit(solution)/shard_map/ppermute | solution.py:448
  23.4 0.0 collective-permute-done.4
  23.4 2.4 %collective-permute-start.5 = (bf16[480,128]{1,0:T(8,128)(2,1)S(1)}, bf16[480,128]{1,0:T(8,128)(2,1)S(1)}, u32[]{:S(2)}, u32[]{:S(2)}) collective-permute-start(bf16[480,128]{1,0:T(8,128)(2,1)S(1)} %add_convert_fusion.2._), channel_id=1, source_target_pairs={{0,8},{1,5},{2,10},{3,7},{4,12},{5,1},{6,14},{7,3},{8,0},{9,13},{1... | collective-permute-start | bytes 368648 | tf_op jit(solution)/shard_map/ppermute | solution.py:448
  25.8 2.4 %shard_map.81 = (bf16[64,1024]{1,0:T(8,128)(2,1)}, f32[8,128]{1,0:T(8,128)S(1)}) custom-call(s32[1]{0:T(128)} %bitcast.odd_ref, bf16[992,128]{1,0:T(8,128)(2,1)S(1)} %collective-permute-done.2.near_ref, bf16[64,256]{1,0:T(8,128)(2,1)S(1)} %get-tuple-element.54.far_ref, bf16[16,1024]{1,0:T(8,128)(2,1)S(1)} %get-tuple-element.34.m_ref, ...), custom_call_target="tpu_custom_call" | custom-call | flops 452984832 | tf_op jit(solution)/shard_map/pallas_call | solution.py:428
  28.1 0.0 collective-permute-done.8
  28.2 0.1 collective-permute-start.9
  28.3 1.3 %collective-permute-done.9._.rest = bf16[384,128]{1,0:T(8,128)(2,1)S(1)} collective-permute-done((bf16[384,128]{1,0:T(8,128)(2,1)S(1)}, bf16[384,128]{1,0:T(8,128)(2,1)S(1)}, u32[]{:S(2)}, u32[]{:S(2)}) %collective-permute-start.9) | collective-permute-done | bytes 98336 | tf_op jit(solution)/shard_map/ppermute | solution.py:451
  29.6 0.0 collective-permute-done.5
  29.6 0.1 add_convert_fusion.1.part
  29.6 0.2 collective-permute-start.10
  29.9 1.0 %shard_map.83 = (f32[27,64,64]{2,1,0:T(8,128)}, f32[27,64,64]{2,1,0:T(8,128)}) custom-call(s32[1]{0:T(128)} %bitcast.odd_ref, bf16[480,128]{1,0:T(8,128)(2,1)S(1)} %add_convert_fusion.1.part, bf16[384,128]{1,0:T(8,128)(2,1)S(1)} %add_convert_fusion.4.rest), custom_call_target="tpu_custom_call" | custom-call | flops 226492416 | tf_op jit(solution)/shard_map/pallas_call | solution.py:428
  30.8 0.2 collective-permute-done.10.part
  31.0 1.0 %shard_map.84 = (f32[27,64,64]{2,1,0:T(8,128)}, f32[27,64,64]{2,1,0:T(8,128)}) custom-call(s32[1]{0:T(128)} %bitcast.odd_ref, bf16[480,128]{1,0:T(8,128)(2,1)S(1)} %collective-permute-done.10.part, bf16[384,128]{1,0:T(8,128)(2,1)S(1)} %collective-permute-done.9._.rest, ...), custom_call_target="tpu_custom_call", output_to_operand_aliasing={{0}: (3, {}), {1}: (4, {})} | custom-call | tf_op jit(solution)/shard_map/pallas_call | solution.py:428
  (10 shorter events, 0.2 us)
Async XLA Ops:
  1.7 6.7 %collective-permute-start = (bf16[272,256]{1,0:T(8,128)(2,1)S(1)}, bf16[272,256]{1,0:T(8,128)(2,1)S(1)}, u32[]{:S(2)}, u32[]{:S(2)}) collective-permute-start(bf16[272,256]{1,0:T(8,128)(2,1)S(1)} %get-tuple-element.33), channel_id=1, source_target_pairs={{1,2},{2,1},{3,4},{4,3},{5,6},{6,5},{7,8},{8,7},{9,10},{10,9},{11,... | collective-permute-start | bytes 417800 | tf_op jit(solution)/shard_map/ppermute | solution.py:512
  4.7 2.8 %collective-permute-start.1 = (bf16[128,256]{1,0:T(8,128)(2,1)S(1)}, bf16[128,256]{1,0:T(8,128)(2,1)S(1)}, u32[]{:S(2)}, u32[]{:S(2)}) collective-permute-start(bf16[128,256]{1,0:T(8,128)(2,1)S(1)} %get-tuple-element.42), channel_id=1, source_target_pairs={{0,1},{1,0},{2,3},{3,2},{4,5},{5,4},{6,7},{7,6},{8,9},{9,8},{10,11... | collective-permute-start | bytes 196616 | tf_op jit(solution)/shard_map/ppermute | solution.py:511
  9.1 1.8 %collective-permute-start.2 = (bf16[992,128]{1,0:T(8,128)(2,1)S(1)}, bf16[992,128]{1,0:T(8,128)(2,1)S(1)}, u32[]{:S(2)}, u32[]{:S(2)}) collective-permute-start(bf16[992,128]{1,0:T(8,128)(2,1)S(1)} %get-tuple-element.49), channel_id=1, source_target_pairs={{0,1},{1,0},{2,3},{3,2},{4,5},{5,4},{6,7},{7,6},{8,9},{9,8},{10,11... | collective-permute-start | bytes 761864 | tf_op jit(solution)/shard_map/ppermute | solution.py:451
  11.0 4.7 %collective-permute-start.6 = (bf16[384,128]{1,0:T(8,128)(2,1)S(1)}, bf16[384,128]{1,0:T(8,128)(2,1)S(1)}, u32[]{:S(2)}, u32[]{:S(2)}) collective-permute-start(bf16[384,128]{1,0:T(8,128)(2,1)S(1)} %slice.24), channel_id=1, source_target_pairs={{0,2},{1,9},{2,0},{3,11},{4,6},{5,13},{6,4},{7,15},{8,10},{9,1},{1... | collective-permute-start | bytes 294920 | tf_op jit(solution)/shard_map/ppermute | solution.py:448
  13.1 4.9 %collective-permute-start.3 = (bf16[480,128]{1,0:T(8,128)(2,1)S(1)}, bf16[480,128]{1,0:T(8,128)(2,1)S(1)}, u32[]{:S(2)}, u32[]{:S(2)}) collective-permute-start(bf16[480,128]{1,0:T(8,128)(2,1)S(1)} %slice.23), channel_id=1, source_target_pairs={{0,2},{1,9},{2,0},{3,11},{4,6},{5,13},{6,4},{7,15},{8,10},{9,1},{1... | collective-permute-start | bytes 368648 | tf_op jit(solution)/shard_map/ppermute | solution.py:448
  15.8 4.9 %collective-permute-start.7 = (bf16[384,128]{1,0:T(8,128)(2,1)S(1)}, bf16[384,128]{1,0:T(8,128)(2,1)S(1)}, u32[]{:S(2)}, u32[]{:S(2)}) collective-permute-start(bf16[384,128]{1,0:T(8,128)(2,1)S(1)} %add_convert_fusion.6), channel_id=1, source_target_pairs={{0,4},{1,3},{2,6},{3,1},{4,0},{5,7},{6,2},{7,5},{8,12},{9,11},{10,... | collective-permute-start | bytes 294920 | tf_op jit(solution)/shard_map/ppermute | solution.py:448
  18.1 5.2 %collective-permute-start.4 = (bf16[480,128]{1,0:T(8,128)(2,1)S(1)}, bf16[480,128]{1,0:T(8,128)(2,1)S(1)}, u32[]{:S(2)}, u32[]{:S(2)}) collective-permute-start(bf16[480,128]{1,0:T(8,128)(2,1)S(1)} %add_convert_fusion.3), channel_id=1, source_target_pairs={{0,4},{1,3},{2,6},{3,1},{4,0},{5,7},{6,2},{7,5},{8,12},{9,11},{10,... | collective-permute-start | bytes 368648 | tf_op jit(solution)/shard_map/ppermute | solution.py:448
  20.7 7.5 %collective-permute-start.8 = (bf16[384,128]{1,0:T(8,128)(2,1)S(1)}, bf16[384,128]{1,0:T(8,128)(2,1)S(1)}, u32[]{:S(2)}, u32[]{:S(2)}) collective-permute-start(bf16[384,128]{1,0:T(8,128)(2,1)S(1)} %add_convert_fusion.5), channel_id=1, source_target_pairs={{0,8},{1,5},{2,10},{3,7},{4,12},{5,1},{6,14},{7,3},{8,0},{9,13},{1... | collective-permute-start | bytes 294920 | tf_op jit(solution)/shard_map/ppermute | solution.py:448
  23.4 6.2 %collective-permute-start.5 = (bf16[480,128]{1,0:T(8,128)(2,1)S(1)}, bf16[480,128]{1,0:T(8,128)(2,1)S(1)}, u32[]{:S(2)}, u32[]{:S(2)}) collective-permute-start(bf16[480,128]{1,0:T(8,128)(2,1)S(1)} %add_convert_fusion.2._), channel_id=1, source_target_pairs={{0,8},{1,5},{2,10},{3,7},{4,12},{5,1},{6,14},{7,3},{8,0},{9,13},{1... | collective-permute-start | bytes 368648 | tf_op jit(solution)/shard_map/ppermute | solution.py:448
  28.2 1.4 %collective-permute-start.9 = (bf16[384,128]{1,0:T(8,128)(2,1)S(1)}, bf16[384,128]{1,0:T(8,128)(2,1)S(1)}, u32[]{:S(2)}, u32[]{:S(2)}) collective-permute-start(bf16[384,128]{1,0:T(8,128)(2,1)S(1)} %add_convert_fusion.4.rest), channel_id=1, source_target_pairs={{0,1},{1,0},{2,3},{3,2},{4,5},{5,4},{6,7},{7,6},{8,9},{9,8},{10,11... | collective-permute-start | bytes 294920 | tf_op jit(solution)/shard_map/ppermute | solution.py:451
  29.6 1.4 %collective-permute-start.10 = (bf16[480,128]{1,0:T(8,128)(2,1)S(1)}, bf16[480,128]{1,0:T(8,128)(2,1)S(1)}, u32[]{:S(2)}, u32[]{:S(2)}) collective-permute-start(bf16[480,128]{1,0:T(8,128)(2,1)S(1)} %add_convert_fusion.1.part), channel_id=1, source_target_pairs={{0,1},{1,0},{2,3},{3,2},{4,5},{5,4},{6,7},{7,6},{8,9},{9,8},{10,11... | collective-permute-start | bytes 368648 | tf_op jit(solution)/shard_map/ppermute | solution.py:451
